TPU v7x, 256 devices: a whole 4x4x8 slice. The times are simulated.
256 devices in a mesh: outer: 8 (over x, y_hi), inner: 32 (over y_lo, z, core).
Axes of the slice: x: 4, y: 4 (y_hi: 2, y_lo: 2; y = y_hi * 2 + y_lo), z: 8, core: 2. Of those that a mesh axis runs over, the one named last changes fastest.
Arguments:
- query: bfloat16 [2, 16384, 640], P(None, ('outer', 'inner')), may hold values from -16 to 16
- key: bfloat16 [2, 16384, 128], P(None, ('outer', 'inner')), may hold values from -8 to 8
- value: bfloat16 [2, 16384, 128], P(None, ('outer', 'inner')), may hold values from -6 to 6
- d_attended: bfloat16 [2, 16384, 640], P(None, ('outer', 'inner')), may hold values from -6 to 6
- stretch_ids: int32 [256], replicated, may hold values from 0 to 255, each once
Outputs:
- attended: bfloat16 [2, 16384, 640], P(None, ('outer', 'inner'))
- grad_query: float32 [2, 16384, 640], P(None, ('outer', 'inner'))
- grad_key: float32 [2, 16384, 128], P(None, ('outer', 'inner'))
- grad_value: float32 [2, 16384, 128], P(None, ('outer', 'inner'))
Inputs may be any that keep to these rules, and one draw needn't show every extreme that they name: `stretch_ids`: each shard number appears once.
All inputs are finite; a program needn't handle non-finite values.
Results may differ from a plain program's by a relative error of at most 0.029.
Values may be sent and summed in bfloat16 or wider, within the bound.
No kernel may reach another device: no remote copies, remote signals or barrier semaphores. Data moves between devices by JAX's collectives and lax.ppermute only.
A program may use at most 128 MiB of HBM per device.

v0:
```python
import math

import jax
import jax.numpy as jnp
from jax import lax
from jax.sharding import PartitionSpec as P

masked_score = -1e30


def merged(part, axis, combine):
    gathered = jax.tree.map(lambda a: lax.all_gather(a, axis), part)

    def take(source):
        return jax.tree.map(lambda a: lax.dynamic_index_in_dim(a, source, 0, False), gathered)

    return lax.fori_loop(
        1, lax.axis_size(axis), lambda source, state: combine(state, take(source)), take(0)
    )


def shard_positions(stretch_list, stretch_rows, shard_count):
    offset = jnp.arange(stretch_rows, dtype=jnp.int32)
    leading = stretch_list[:, None] * stretch_rows + offset[None, :]
    trailing = (2 * shard_count - 1 - stretch_list[:, None]) * stretch_rows + offset[None, :]
    return jnp.stack([leading, trailing], axis=1)


def head_positions(places, head_count):
    return jnp.broadcast_to(places[:, :, None], places.shape + (head_count,)).reshape(-1)


def score_block(query_rows, key_rows, scaling):
    return (
        jnp.einsum("rd,kd->rk", query_rows, key_rows, preferred_element_type=jnp.float32) * scaling
    )


def absorb(carried, query_rows, key_rows, value_rows, visible, scaling):
    running_max, running_sum, running_out = carried
    scores = score_block(query_rows, key_rows, scaling)
    if visible is None:
        new_max = jnp.maximum(running_max, jnp.max(scores, axis=1))
        weights = jnp.exp(scores - new_max[:, None])
    else:
        new_max = jnp.maximum(
            running_max, jnp.max(jnp.where(visible, scores, masked_score), axis=1)
        )
        weights = jnp.where(visible, jnp.exp(scores - new_max[:, None]), 0.0)
    shrink = jnp.exp(running_max - new_max)
    running_sum = running_sum * shrink + jnp.sum(weights, axis=1)
    mixed = jnp.dot(
        weights,
        value_rows.astype(jnp.float32),
        precision=lax.Precision.HIGHEST,
        preferred_element_type=jnp.float32,
    )
    running_out = running_out * shrink[:, None] + mixed
    return (new_max, running_sum, running_out)


def combine_states(former, latter):
    joint_max = jnp.maximum(former[0], latter[0])
    former_weight = jnp.exp(former[0] - joint_max)
    latter_weight = jnp.exp(latter[0] - joint_max)
    joint_sum = former[1] * former_weight + latter[1] * latter_weight
    joint_out = former[2] * former_weight[..., None] + latter[2] * latter_weight[..., None]
    return (joint_max, joint_sum, joint_out)


def gradients(query_rows, grad_rows, log_rows, delta_rows, key_rows, value_rows, visible, scaling):
    scores = score_block(query_rows, key_rows, scaling)
    attention = jnp.exp(scores - log_rows[:, None])
    if visible is not None:
        attention = jnp.where(visible, attention, 0.0)
    grad_weights = jnp.einsum(
        "rd,kd->rk", grad_rows, value_rows, preferred_element_type=jnp.float32
    )
    grad_scores = (attention * (grad_weights - delta_rows[:, None])).astype(jnp.bfloat16)
    grad_query = jnp.dot(grad_scores, key_rows, preferred_element_type=jnp.float32)
    grad_key = jnp.einsum("rk,rd->kd", grad_scores, query_rows, preferred_element_type=jnp.float32)
    grad_value = jnp.einsum(
        "rk,rd->kd", attention.astype(jnp.bfloat16), grad_rows, preferred_element_type=jnp.float32
    )
    return (grad_query, grad_key, grad_value)


def key_groups(key_rows, value_rows, stretch_list, stretch_rows, shard_count, head_width):
    number = stretch_list.shape[0]
    bundle = math.gcd(number, 8)
    bundles = number // bundle
    keys_split = key_rows.reshape(bundles, bundle, 2, stretch_rows, head_width)
    values_split = value_rows.reshape(bundles, bundle, 2, stretch_rows, head_width)
    places = shard_positions(stretch_list, stretch_rows, shard_count).reshape(
        bundles, bundle, 2, stretch_rows
    )
    span = bundle * stretch_rows
    return (
        keys_split[:, :, 0].reshape(bundles, span, head_width),
        keys_split[:, :, 1].reshape(bundles, span, head_width),
        values_split[:, :, 0].reshape(bundles, span, head_width),
        values_split[:, :, 1].reshape(bundles, span, head_width),
        places[:, :, 0].reshape(bundles, span),
        places[:, :, 1].reshape(bundles, span),
    )


def on_device(query, key, value, d_attended, stretch_ids):
    outer_at = lax.axis_index("outer")
    inner_at = lax.axis_index("inner")
    outer_count = lax.axis_size("outer")
    inner_count = lax.axis_size("inner")
    shard_count = stretch_ids.shape[0]
    shard_rows = query.shape[1]
    stretch_rows = shard_rows // 2
    head_width = key.shape[2]
    head_count = query.shape[2] // head_width
    scaling = head_width ** (-0.5)
    grid_ids = stretch_ids.reshape(outer_count, inner_count)
    column_ids = lax.dynamic_slice_in_dim(grid_ids, inner_at, 1, 1)[:, 0]
    row_ids = lax.dynamic_slice_in_dim(stretch_ids, outer_at * inner_count, inner_count)
    column_places = shard_positions(column_ids, stretch_rows, shard_count)
    leading_places = head_positions(column_places[:, 0], head_count)
    trailing_places = head_positions(column_places[:, 1], head_count)
    column_rows = outer_count * stretch_rows * head_count
    band = stretch_rows * head_count
    results = ([], [], [], [])
    for sequence in range(query.shape[0]):
        query_column = lax.all_gather(query[sequence], "outer", axis=0, tiled=True)
        query_parts = query_column.reshape(outer_count, 2, band, head_width)
        leading_rows = query_parts[:, 0].reshape(column_rows, head_width)
        trailing_rows = query_parts[:, 1].reshape(column_rows, head_width)
        empty_state = (
            jnp.full((column_rows,), masked_score, jnp.float32),
            jnp.zeros((column_rows,), jnp.float32),
            jnp.zeros((column_rows, head_width), jnp.float32),
        )
        carried = (empty_state, empty_state)

        def fold_step(running, blocks):
            key_lead, key_trail, value_lead, value_trail, place_lead, place_trail = blocks
            lead_state, trail_state = running
            lead_state = absorb(
                lead_state,
                leading_rows,
                key_lead,
                value_lead,
                place_lead[None, :] <= leading_places[:, None],
                scaling,
            )
            trail_state = absorb(trail_state, trailing_rows, key_lead, value_lead, None, scaling)
            trail_state = absorb(
                trail_state,
                trailing_rows,
                key_trail,
                value_trail,
                place_trail[None, :] <= trailing_places[:, None],
                scaling,
            )
            return ((lead_state, trail_state), None)

        carried, unused = lax.scan(
            fold_step,
            carried,
            key_groups(
                lax.all_gather(key[sequence], "inner", axis=0, tiled=True),
                lax.all_gather(value[sequence], "inner", axis=0, tiled=True),
                row_ids,
                stretch_rows,
                shard_count,
                head_width,
            ),
        )
        lead_state, trail_state = carried
        key_row, value_row = (
            lax.all_gather(key[sequence], "inner", axis=0, tiled=True),
            lax.all_gather(value[sequence], "inner", axis=0, tiled=True),
        )
        running_max = jnp.stack(
            [lead_state[0].reshape(outer_count, band), trail_state[0].reshape(outer_count, band)],
            axis=1,
        )
        running_sum = jnp.stack(
            [lead_state[1].reshape(outer_count, band), trail_state[1].reshape(outer_count, band)],
            axis=1,
        )
        running_out = jnp.stack(
            [
                lead_state[2].reshape(outer_count, band, head_width),
                trail_state[2].reshape(outer_count, band, head_width),
            ],
            axis=1,
        )
        grad_column = lax.all_gather(d_attended[sequence], "outer", axis=0, tiled=True).reshape(
            outer_count, 2, band, head_width
        )
        running_max, running_sum, running_out = merged(
            (running_max, running_sum, running_out), "outer", combine_states
        )
        out_column = (running_out / running_sum[..., None]).astype(jnp.bfloat16)
        log_column = running_max + jnp.log(running_sum)
        delta_column = jnp.sum(
            grad_column.astype(jnp.float32) * out_column.astype(jnp.float32), axis=-1
        )
        out_own = lax.dynamic_index_in_dim(out_column, outer_at, 0, keepdims=False)
        grad_leading = grad_column[:, 0].reshape(column_rows, head_width)
        grad_trailing = grad_column[:, 1].reshape(column_rows, head_width)
        log_leading = log_column[:, 0].reshape(column_rows)
        log_trailing = log_column[:, 1].reshape(column_rows)
        delta_leading = delta_column[:, 0].reshape(column_rows)
        delta_trailing = delta_column[:, 1].reshape(column_rows)

        def grad_step(running, blocks):
            query_lead, query_trail = running
            key_lead, key_trail, value_lead, value_trail, place_lead, place_trail = blocks
            grads_one = gradients(
                leading_rows,
                grad_leading,
                log_leading,
                delta_leading,
                key_lead,
                value_lead,
                place_lead[None, :] <= leading_places[:, None],
                scaling,
            )
            grads_two = gradients(
                trailing_rows,
                grad_trailing,
                log_trailing,
                delta_trailing,
                key_lead,
                value_lead,
                None,
                scaling,
            )
            grads_three = gradients(
                trailing_rows,
                grad_trailing,
                log_trailing,
                delta_trailing,
                key_trail,
                value_trail,
                place_trail[None, :] <= trailing_places[:, None],
                scaling,
            )
            running = (query_lead + grads_one[0], query_trail + grads_two[0] + grads_three[0])
            return (
                running,
                (
                    grads_one[1] + grads_two[1],
                    grads_three[1],
                    grads_one[2] + grads_two[2],
                    grads_three[2],
                ),
            )

        zero_query = jnp.zeros((column_rows, head_width), jnp.float32)
        (query_lead, query_trail), (key_lead, key_trail, value_lead, value_trail) = lax.scan(
            grad_step,
            (zero_query, zero_query),
            key_groups(key_row, value_row, row_ids, stretch_rows, shard_count, head_width),
        )
        key_all = jnp.stack(
            [
                key_lead.reshape(inner_count, stretch_rows, head_width),
                key_trail.reshape(inner_count, stretch_rows, head_width),
            ],
            axis=1,
        ).reshape(inner_count, shard_rows * head_width)
        value_all = jnp.stack(
            [
                value_lead.reshape(inner_count, stretch_rows, head_width),
                value_trail.reshape(inner_count, stretch_rows, head_width),
            ],
            axis=1,
        ).reshape(inner_count, shard_rows * head_width)
        key_own, value_own = (
            lax.psum_scatter(key_all, "inner", scatter_dimension=0, tiled=True),
            lax.psum_scatter(value_all, "inner", scatter_dimension=0, tiled=True),
        )
        query_all = jnp.stack(
            [
                query_lead.reshape(outer_count, stretch_rows, head_count * head_width),
                query_trail.reshape(outer_count, stretch_rows, head_count * head_width),
            ],
            axis=1,
        ).reshape(outer_count, shard_rows * head_count * head_width)
        query_own = lax.psum_scatter(query_all, "outer", scatter_dimension=0, tiled=True)
        results[0].append(out_own.reshape(shard_rows, head_count * head_width))
        results[1].append((query_own * scaling).reshape(shard_rows, head_count * head_width))
        results[2].append((key_own * scaling).reshape(shard_rows, head_width))
        results[3].append(value_own.reshape(shard_rows, head_width))
    return (
        jnp.stack(results[0], axis=0),
        jnp.stack(results[1], axis=0),
        jnp.stack(results[2], axis=0),
        jnp.stack(results[3], axis=0),
    )


def solution(mesh):
    in_specs = (
        P(None, ("outer", "inner"), None),
        P(None, ("outer", "inner"), None),
        P(None, ("outer", "inner"), None),
        P(None, ("outer", "inner"), None),
        P(),
    )
    out_specs = (
        P(None, ("outer", "inner"), None),
        P(None, ("outer", "inner"), None),
        P(None, ("outer", "inner"), None),
        P(None, ("outer", "inner"), None),
    )
    return jax.shard_map(
        on_device, mesh=mesh, in_specs=in_specs, out_specs=out_specs, check_vma=False
    )
```

profile of v0, /device:TPU:1, one launch (start us, length us, event | category | flops | bytes accessed | tf_op | source)
XLA Modules:
  0.0 1150.8 jit_solution(2769677852596996435)
XLA Ops:
  10.7 39.9 %all-gather.6 = bf16[1,2048,128]{2,1,0:T(8,128)(2,1)S(1)} all-gather(bf16[1,64,128]{2,1,0:T(8,128)(2,1)S(1)} %get-tuple-element.1359), channel_id=8, replica_groups=mesh['outer'=8,'inner'=32] {'inner'}, dimensions={1}, use_global_device_ids=true | all-gather | bytes 540672 | tf_op jit(solution)/shard_map/all_gather | solution.py:166
  52.2 29.7 %all-gather.7 = bf16[1,512,640]{2,1,0:T(8,128)(2,1)S(1)} all-gather(bf16[1,64,640]{2,1,0:T(8,128)(2,1)S(1)} %get-tuple-element.1353), channel_id=9, replica_groups=mesh['outer'=8,'inner'=32] {'outer'}, dimensions={1}, use_global_device_ids=true | all-gather | bytes 737280 | tf_op jit(solution)/shard_map/all_gather | solution.py:129
  83.3 37.3 %all-gather.8 = bf16[1,2048,128]{2,1,0:T(8,128)(2,1)S(1)} all-gather(bf16[1,64,128]{2,1,0:T(8,128)(2,1)S(1)} %get-tuple-element.1357), channel_id=10, replica_groups=mesh['outer'=8,'inner'=32] {'inner'}, dimensions={1}, use_global_device_ids=true | all-gather | bytes 540672 | tf_op jit(solution)/shard_map/all_gather | solution.py:167
  121.7 45.0 %while.125 = (s32[]{:T(128)}, f32[1280]{0:T(1024)S(1)}, f32[1280]{0:T(1024)S(1)}, f32[1280,128]{1,0:T(8,128)}, f32[1280]{0:T(1024)S(1)}, /*index=5*/f32[1280]{0:...) while((s32[]{:T(128)}, f32[1280]{0:T(1024)S(1)}, ...), condition=%wide.region_17.18_spmd.clone, body=%wide.region_10.17_spmd.clone.sunk | while | flops 1771781120 | bytes 26325328 | solution.py:162
  129.9 3.0 convolution_add_fusion.29
  141.2 3.0 convolution_add_fusion.29
  152.4 3.0 convolution_add_fusion.29
  163.7 3.0 convolution_add_fusion.29
  170.2 30.4 %all-gather.1 = bf16[1,512,640]{2,1,0:T(8,128)(2,1)S(1)} all-gather(bf16[1,64,640]{2,1,0:T(8,128)(2,1)S(1)} %copy-done.58), channel_id=3, replica_groups=mesh['outer'=8,'inner'=32] {'outer'}, dimensions={1}, use_global_device_ids=true | all-gather | bytes 737280 | tf_op jit(solution)/shard_map/all_gather | solution.py:129
  201.1 40.0 %all-gather = bf16[1,2048,128]{2,1,0:T(8,128)(2,1)S(1)} all-gather(bf16[1,64,128]{2,1,0:T(8,128)(2,1)S(1)} %copy-done.88), channel_id=2, replica_groups=mesh['outer'=8,'inner'=32] {'inner'}, dimensions={1}, use_global_device_ids=true | all-gather | bytes 540672 | tf_op jit(solution)/shard_map/all_gather | solution.py:166
  241.9 33.3 %all-gather.2 = bf16[1,2048,128]{2,1,0:T(8,128)(2,1)S(1)} all-gather(bf16[1,64,128]{2,1,0:T(8,128)(2,1)S(1)} %copy-done.89), channel_id=4, replica_groups=mesh['outer'=8,'inner'=32] {'inner'}, dimensions={1}, use_global_device_ids=true | all-gather | bytes 540672 | tf_op jit(solution)/shard_map/all_gather | solution.py:167
  276.8 46.2 %while.124 = (s32[]{:T(128)}, f32[1280]{0:T(1024)S(1)}, f32[1280]{0:T(1024)S(1)}, f32[1280,128]{1,0:T(8,128)}, f32[1280]{0:T(1024)S(1)}, /*index=5*/f32[1280]{0:...) while((s32[]{:T(128)}, f32[1280]{0:T(1024)S(1)}, ...), condition=%wide.region_7.8_spmd.clone, body=%wide.region_0.7_spmd.clone.sunk | while | flops 1771781120 | bytes 26440240 | solution.py:162
  326.3 31.0 %all-gather.13 = bf16[1,512,640]{2,1,0:T(8,128)(2,1)S(1)} all-gather(bf16[1,64,640]{2,1,0:T(8,128)(2,1)S(1)} %get-tuple-element.1355), channel_id=15, replica_groups=mesh['outer'=8,'inner'=32] {'outer'}, dimensions={1}, use_global_device_ids=true | all-gather | bytes 737280 | tf_op jit(solution)/shard_map/all_gather | solution.py:194
  358.1 28.5 %all-gather.9 = f32[64,2,160]{2,1,0:T(2,128)S(1)} all-gather(f32[8,2,160]{2,1,0:T(2,128)S(1)} %pad_maximum_fusion.14), channel_id=11, replica_groups=mesh['outer'=8,'inner'=32] {'outer'}, dimensions={0}, use_global_device_ids=true | all-gather | bytes 92160 | tf_op jit(solution)/shard_map/all_gather | solution.py:12
  386.8 28.4 %all-gather.10 = f32[64,2,160]{2,1,0:T(2,128)S(1)} all-gather(f32[8,2,160]{2,1,0:T(2,128)S(1)} %pad_maximum_fusion.15), channel_id=12, replica_groups=mesh['outer'=8,'inner'=32] {'outer'}, dimensions={0}, use_global_device_ids=true | all-gather | bytes 92160 | tf_op jit(solution)/shard_map/all_gather | solution.py:12
  415.3 29.7 %all-gather.12 = bf16[1,512,640]{2,1,0:T(8,128)(2,1)S(1)} all-gather(bf16[1,64,640]{2,1,0:T(8,128)(2,1)S(1)} %get-tuple-element.1354), channel_id=14, replica_groups=mesh['outer'=8,'inner'=32] {'outer'}, dimensions={1}, use_global_device_ids=true | all-gather | bytes 737280 | tf_op jit(solution)/shard_map/all_gather | solution.py:194
  445.6 29.3 %all-gather.3 = f32[64,2,160]{2,1,0:T(2,128)S(1)} all-gather(f32[8,2,160]{2,1,0:T(2,128)S(1)} %pad_maximum_fusion.12), channel_id=5, replica_groups=mesh['outer'=8,'inner'=32] {'outer'}, dimensions={0}, use_global_device_ids=true | all-gather | bytes 92160 | tf_op jit(solution)/shard_map/all_gather | solution.py:12
  475.1 28.0 %all-gather.4 = f32[64,2,160]{2,1,0:T(2,128)S(1)} all-gather(f32[8,2,160]{2,1,0:T(2,128)S(1)} %pad_maximum_fusion.13), channel_id=6, replica_groups=mesh['outer'=8,'inner'=32] {'outer'}, dimensions={0}, use_global_device_ids=true | all-gather | bytes 92160 | tf_op jit(solution)/shard_map/all_gather | solution.py:12
  506.4 14.8 %while.123 = (s32[]{:T(128)}, f32[8,2,160]{2,1,0:T(2,128)S(1)}, f32[8,2,160]{2,1,0:T(2,128)S(1)}, f32[8,2,160,128]{3,2,1,0:T(8,128)S(1)}, f32[8,8,2,160]{3,2,1,0...) while((s32[]{:T(128)}, f32[8,2,160]{2,1,0:T(2,128)S(1)}, ...), condition=%wide.region_19.20_spmd, body=%wide.region_18.19_spmd.sunk | while | flops 998405 | bytes 4034711 | solution.py:17
  522.7 20.0 %while.122 = (s32[]{:T(128)}, f32[8,2,160]{2,1,0:T(2,128)S(1)}, f32[8,2,160]{2,1,0:T(2,128)S(1)}, f32[8,2,160,128]{3,2,1,0:T(8,128)S(1)}, f32[8,8,2,160]{3,2,1,0...) while((s32[]{:T(128)}, f32[8,2,160]{2,1,0:T(2,128)S(1)}, ...), condition=%wide.region_9.10_spmd, body=%wide.region_8.9_spmd.sunk | while | flops 998405 | bytes 4034711 | solution.py:17
  550.1 82.4 %while.127 = (s32[]{:T(128)}, f32[1280,128]{1,0:T(8,128)}, f32[1280,128]{1,0:T(8,128)}, f32[4,256,128]{2,1,0:T(8,128)}, f32[4,256,128]{2,1,0:T(8,128)}, /*index=...) while((s32[]{:T(128)}, f32[1280,128]{1,0:T(8,128)}, ...), condition=%wide.region_26.27_spmd.clone, body=%wide.region_25.26_spmd.clone.sunk | while | flops 1266384896 | bytes 45644568 | solution.py:258
  643.5 82.1 %while.126 = (s32[]{:T(128)}, f32[1280,128]{1,0:T(8,128)}, f32[1280,128]{1,0:T(8,128)}, f32[4,256,128]{2,1,0:T(8,128)}, f32[4,256,128]{2,1,0:T(8,128)}, /*index=...) while((s32[]{:T(128)}, f32[1280,128]{1,0:T(8,128)}, ...), condition=%wide.region_22.23_spmd.clone, body=%wide.region_21.22_spmd.clone.sunk | while | flops 1266384896 | bytes 44333820 | solution.py:258
  743.5 152.3 %all-reduce.13.cloned.1.call-done = (f32[8,40960]{1,0:T(8,128)}, f32[8,40960]{1,0:T(8,128)}) async-done(((f32[8,40960]{1,0:T(8,128)}, f32[8,40960]{1,0:T(8,128)}), (f32[8,40960]{1,0:T(8,128)}, f32[8,40960]{1,0:T(8,128)})) %all-reduce.13.cloned.1.call-update) | async-done | bytes 2621456
  901.6 234.7 %all-reduce.11.cloned.1.call-done = (f32[32,8192]{1,0:T(8,128)}, f32[32,8192]{1,0:T(8,128)}, f32[32,8192]{1,0:T(8,128)}, f32[32,8192]{1,0:T(8,128)}) async-done(((f32[32,8192]{1,0:T(8,128)}, f32[32,8192]{1,0:T(8,128)}, f32[32,8192]{1,0:T(8,128)}, f32[32,8192]{1,0:T(8,128)}), (f32[32,8192]{1,0:T(8,128)}, f32[32,8192]{1,0:T(8,128)}, f32[32,8192]{1,0:T(8,128)}, ...) | async-done | bytes 4194320
  (1003 shorter events, 347.0 us)
Async XLA Ops:
  7.2 44.4 %copy-start.80 = (bf16[2,64,640]{2,1,0:T(8,128)(2,1)S(1)}, bf16[2,64,640]{2,1,0:T(8,128)(2,1)}, u32[]{:S(2)}) copy-start(bf16[2,64,640]{2,1,0:T(8,128)(2,1)} %param.17) | copy-start | bytes 491524
  7.2 497.8 %all-gather.19.cloned.1.call-start = ((), (), s32[]{:S(2)}) async-start(), calls=%async_computation.1 | async-start | bytes 11796480 | tf_op jit(solution)/shard_map/all_gather | solution.py:12
  169.3 31.8 %copy-start.88 = (bf16[1,64,128]{2,1,0:T(8,128)(2,1)S(1)}, bf16[1,64,128]{2,1,0:T(8,128)(2,1)}, u32[]{:S(2)}) copy-start(bf16[1,64,128]{2,1,0:T(8,128)(2,1)} %get-tuple-element.1358) | copy-start | bytes 49156
  169.3 351.9 %all-gather.17.cloned.1.call-start = ((), (), s32[]{:S(2)}) async-start(), calls=%async_computation | async-start | bytes 11796480 | tf_op jit(solution)/shard_map/all_gather | solution.py:12
  200.6 41.3 %copy-start.89 = (bf16[1,64,128]{2,1,0:T(8,128)(2,1)S(1)}, bf16[1,64,128]{2,1,0:T(8,128)(2,1)}, u32[]{:S(2)}) copy-start(bf16[1,64,128]{2,1,0:T(8,128)(2,1)} %get-tuple-element.1356) | copy-start | bytes 49156
  325.4 570.4 %all-reduce.13.cloned.1.call-start = ((), (), s32[]{:S(2)}) async-start(), calls=%async_computation.3 | async-start | bytes 5242880
  357.9 145.2 %copy-start.35 = (bf16[8,2,160,128]{3,2,1,0:T(8,128)(2,1)}, bf16[8,2,160,128]{3,2,1,0:T(8,128)(2,1)S(1)}, u32[]{:S(2)}) copy-start(bf16[8,2,160,128]{3,2,1,0:T(8,128)(2,1)S(1)} %reshape.189) | copy-start | bytes 1966084
  386.6 88.3 %copy-start.77 = (f32[1280]{0:T(1024)S(1)}, f32[1280]{0:T(1024)}, u32[]{:S(2)}) copy-start(f32[1280]{0:T(1024)} %get-tuple-element.791) | copy-start | bytes 15364
  445.4 59.5 %copy-start.33 = (bf16[8,2,160,128]{3,2,1,0:T(8,128)(2,1)}, bf16[8,2,160,128]{3,2,1,0:T(8,128)(2,1)S(1)}, u32[]{:S(2)}) copy-start(bf16[8,2,160,128]{3,2,1,0:T(8,128)(2,1)S(1)} %reshape.187) | copy-start | bytes 1966084
  474.9 30.0 %copy-start.56 = (f32[64,2,160]{2,1,0:T(2,128)}, f32[64,2,160]{2,1,0:T(2,128)S(1)}, u32[]{:S(2)}) copy-start(f32[64,2,160]{2,1,0:T(2,128)S(1)} %all-gather.3) | copy-start | bytes 245764
  521.2 21.5 %copy-start.49 = (f32[8,2,160]{2,1,0:T(2,128)}, f32[8,2,160]{2,1,0:T(2,128)S(1)}, u32[]{:S(2)}) copy-start(f32[8,2,160]{2,1,0:T(2,128)S(1)} %get-tuple-element.803) | copy-start | bytes 30724
  569.1 5.8 copy-start.67
  569.1 6.3 copy-start.71
  590.2 5.8 copy-start.67
  590.2 6.3 copy-start.71
  611.3 5.8 copy-start.67
  611.4 6.3 copy-start.71
  662.6 5.9 copy-start.59
  662.6 6.4 copy-start.63
  683.6 5.9 copy-start.59
  683.6 6.4 copy-start.63
  704.6 5.9 copy-start.59
  704.7 6.4 copy-start.63
  731.0 405.3 %all-reduce.11.cloned.1.call-start = ((), (), s32[]{:S(2)}) async-start(), calls=%async_computation.2 | async-start | bytes 8388608
  (214 other events, 389.6 us)
Sparse Core Ops, SparseCore 0:
  169.4 139.5 all-gather.18
  325.6 148.1 all-gather.16
  731.1 164.7 all-reduce.12
  898.6 237.6 all-reduce.10
where the time goes:
time: 1160 us; the launch traced here: 1150 us
  waiting for transfers between devices  387 us (33%)
  blocking collectives  386 us (33%)
  matrix products  219 us (19%)
  local copies, waits for them, and re-layouts  73.7 us (6%)
  other arithmetic  66.4 us (6%)
  between operations  14.7 us (1%)
    unnamed x6, waiting for transfers between devices  387 us
    all_gather x4, blocking collectives, merged(): gathered = jax.tree.map(lambda a: lax.all_gather(a, axis), part)  114 us
    all_gather x2, blocking collectives, on_device(): lax.all_gather(key[sequence], 'inner', axis=0, tiled=True)  79.9 us
    all_gather x2, blocking collectives, on_device(): lax.all_gather(value[sequence], 'inner', axis=0, tiled=True)  70.5 us
    all_gather x2, blocking collectives, on_device(): lax.all_gather(d_attended[sequence], 'outer', axis=0, tiled=True)  60.7 us
    all_gather x2, blocking collectives, on_device(): query_column = lax.all_gather(query[sequence], 'outer', axis=0, tiled=True)  60.2 us
    dot_general x24, matrix products, gradients(): jnp.dot(grad_scores, key_rows, preferred_element_type=jnp.float32)  49.9 us
    dot_general x24, matrix products, absorb(): jnp.dot(weights, value_rows.astype(jnp.float32), precision=lax.Precision....  47.5 us
  transfers between devices with their start and end apart: 4, of which 2 were waited for; matrix products, arithmetic and copies ran while one was open for 7% of the time, Pallas kernels for 0%

commit v1 on v0

v1 whole, which is shorter than its diff:
```python
import functools, math
import jax
import jax.numpy as jnp
from jax import lax
from jax.experimental import pallas as pl
from jax.experimental.pallas import tpu as pltpu
from jax.sharding import PartitionSpec as P

bf16, f32, i32 = jnp.bfloat16, jnp.float32, jnp.int32
HIDE = -float(2**18)
NONE = -1e30
NT = (((1,), (1,)), ((), ()))
NN = (((1,), (0,)), ((), ()))
SMEM = pl.BlockSpec(memory_space=pltpu.SMEM)
VMEM = pl.BlockSpec(memory_space=pltpu.VMEM)
LIMIT = 48 * 2**20
AXES = ("outer", "inner")
NX, NY, NZ = 4, 4, 8


def dot(a, b, dims=NN):
    return lax.dot_general(a, b, dims, preferred_element_type=f32)


class Cfg:
    def __init__(s, heads, half, width, C=512, R=256):
        s.heads, s.half, s.width, s.C, s.R = heads, half, width, C, R
        s.tokens = 4 * half
        s.row_blocks, s.key_blocks = 4 * NX, 4 * NY * NZ
        s.span = half * heads
        s.rows, s.keys = s.row_blocks * s.span, s.key_blocks * half
        s.nr, s.nc = s.rows // R, s.keys // C
        s.slab = s.keys // NY


def place(x, y, z, core):
    return (x * 2 + (y >> 1)) * 32 + ((y & 1) * NZ + z) * 2 + core


def shift(a, dx=0, dy=0, dz=0, core=0):
    pairs = [(place(x, y, z, c), place((x + dx) % NX, (y + dy) % NY, (z + dz) % NZ, c ^ core))
             for x in range(NX) for y in range(NY) for z in range(NZ) for c in range(2)]
    return lax.ppermute(a, AXES, pairs)


def tables_body(cfg, shard_count, ids, tab_ref, qpos_ref):
    hf, span = cfg.half, cfg.span
    outer_at, inner_at = lax.axis_index("outer"), lax.axis_index("inner")
    x, core = outer_at >> 1, inner_at & 1
    y, z = (outer_at & 1) * 2 + (inner_at >> 4), (inner_at >> 1) & 7
    top = 2 * shard_count - 1
    line = lax.broadcasted_iota(i32, (1, 128), 1)

    def ranked(count, source):
        held = jnp.full((1, 128), 0, i32)
        for j in range(count):
            held = jnp.where(line >> 1 == j, ids[source(j)], held)
        held = jnp.where(line & 1 == 1, top - held, held)
        held = jnp.where(line < 2 * count, held, top + 1 + line).astype(f32)
        across = jnp.broadcast_to(held, (128, 128))
        down = across.T
        lane = lax.broadcasted_iota(i32, (128, 128), 1)
        rank = jnp.sum((down < across).astype(f32), axis=0, keepdims=True)
        rank_down = jnp.sum((across < down).astype(f32), axis=1, keepdims=True).astype(i32)
        rising = jnp.sum(jnp.where(rank_down == lane, down, 0.0), axis=0, keepdims=True)
        return rank, rising

    row_rank, rows = ranked(2 * NX, lambda j: place((x + (j >> 1)) & (NX - 1), y, z, core ^ (j & 1)))
    key_rank, keys = ranked(2 * NY * NZ, lambda j: place(x, (y + (j >> 4)) & (NY - 1), (z + ((j >> 1) & 7)) & (NZ - 1), core ^ (j & 1)))
    row_down = jnp.broadcast_to(rows, (128, 128)).T
    counts = jnp.zeros((1, 128), f32)
    for r in range(cfg.nr):
        first, last = r * cfg.R // span, ((r + 1) * cfg.R - 1) // span
        seen = jnp.sum((keys <= row_down[last:last + 1]).astype(f32), axis=1, keepdims=True)
        whole = jnp.sum((keys < row_down[first:first + 1]).astype(f32), axis=1, keepdims=True)
        counts = jnp.where(line == r, jnp.floor((seen * hf + (cfg.C - 1)) * (1.0 / cfg.C)), counts)
        counts = jnp.where(line == 64 + r, jnp.floor(whole * hf * (1.0 / cfg.C)), counts)
    tab_ref[0:1] = row_rank.astype(i32)
    tab_ref[1:2] = key_rank.astype(i32)
    tab_ref[2:3] = keys.astype(i32)
    tab_ref[3:4] = counts.astype(i32)
    spot = lax.broadcasted_iota(i32, (1, cfg.rows), 1)
    pos = jnp.zeros((1, cfg.rows), f32)
    for i in range(cfg.row_blocks):
        pos = jnp.where(spot >= i * span, row_down[i:i + 1, :1], pos)
    qpos_ref[...] = pos.astype(i32) * hf + (spot & (hf - 1))


def tables(cfg, ids):
    return pl.pallas_call(
        functools.partial(tables_body, cfg, ids.shape[0]),
        out_shape=(jax.ShapeDtypeStruct((4, 128), i32), jax.ShapeDtypeStruct((1, cfg.rows), i32)),
        in_specs=[SMEM], out_specs=(VMEM,) * 2, name="tables",
    )(ids)


def aligned(at, by):
    return at * by if isinstance(at, int) else pl.multiple_of(at * by, by)


def load_rows(cfg, tab, sources, dst):
    w, hf, hd = cfg.width, cfg.half, cfg.heads
    for i in range(cfg.row_blocks):
        at = aligned(tab[0, i], cfg.span)
        for h in range(hd):
            dst[pl.ds(pl.multiple_of(at + h * hf, hf), hf), :] = sources[i // 4][(i % 4) * hf:(i % 4 + 1) * hf, h * w:(h + 1) * w]


def load_keys(cfg, tab, sources, ks, vs):
    w, hf = cfg.width, cfg.half
    per = cfg.key_blocks // len(sources)
    for n, source in enumerate(sources):
        def step(j, _):
            to = pl.ds(aligned(tab[1, n * per + j], hf), hf)
            block = source[pl.ds(aligned(j, hf), hf), :]
            ks[to, :] = block[:, :w]
            vs[to, :] = block[:, w:]
            return 0

        lax.fori_loop(0, per, step, 0, unroll=4)


def unload_rows(cfg, tab, src, outs):
    w, hf, hd = cfg.width, cfg.half, cfg.heads
    for i in range(cfg.row_blocks):
        at = aligned(tab[0, i], cfg.span)
        for h in range(hd):
            outs[i // 4][(i % 4) * hf:(i % 4 + 1) * hf, h * w:(h + 1) * w] = src[pl.ds(pl.multiple_of(at + h * hf, hf), hf), :].astype(bf16)


def visible(cfg, tab, qpos_ref, c, r):
    hf, C, R = cfg.half, cfg.C, cfg.R
    per = C // hf
    step = lax.broadcasted_iota(i32, (hf, 128), 0)
    held = jnp.concatenate([step + tab[2, c * per + b] * hf for b in range(per)], axis=0)
    wide = jnp.concatenate([held] * (R // 128), axis=1)
    return wide <= qpos_ref[:, pl.ds(aligned(r, R), R)]


def forward_body(cfg, *refs):
    tab, qpos = refs[:2]
    q, kv, do = refs[2:6], refs[6:10], refs[10:14]
    outs, stat_ref = refs[14:18], refs[18]
    qs, ks, vs, vt, dos, os, ls = refs[19:]
    w, C, R = cfg.width, cfg.C, cfg.R
    load_rows(cfg, tab, q, qs)
    load_rows(cfg, tab, do, dos)
    load_keys(cfg, tab, kv, ks, vs)
    for c in range(cfg.keys // 256):
        vt[:, c * 256:(c + 1) * 256] = vs[c * 256:(c + 1) * 256, :].T
    scale = math.log2(math.e) / math.sqrt(w)

    def tile(r, _):
        here = pl.ds(aligned(r, R), R)

        def step(masked, c, state):
            m, l, acc = state
            keys = pl.ds(aligned(c, C), C)
            s = dot(ks[keys, :], qs[here, :], NT)
            if masked:
                s = jnp.where(visible(cfg, tab, qpos, c, r), s, HIDE)
            top = jnp.maximum(m, jnp.max(s, axis=0, keepdims=True) * scale)
            p = jnp.exp2(s * scale - top)
            shrink = jnp.exp2(m - top)
            l = l * shrink + jnp.sum(p, axis=0, keepdims=True)
            acc = acc * shrink + dot(vt[:, keys], p.astype(bf16))
            return top, l, acc

        state = (jnp.full((1, R), NONE, f32), jnp.zeros((1, R), f32), jnp.zeros((w, R), f32))
        state = lax.fori_loop(0, tab[3, 64 + r], functools.partial(step, False), state)
        m, l, acc = lax.fori_loop(tab[3, 64 + r], tab[3, r], functools.partial(step, True), state)
        safe = jnp.maximum(l, 1e-30)
        acc = acc * (1.0 / safe)
        lse = m + jnp.log2(safe)
        stat_ref[0:1, here] = lse
        stat_ref[1:2, here] = jnp.sum(acc * dos[here, :].astype(f32).T, axis=0, keepdims=True)
        os[here, :] = acc.T
        ls[here, :] = jnp.broadcast_to(lse, (w, R)).T
        return 0

    lax.fori_loop(0, cfg.nr, tile, 0)
    unload_rows(cfg, tab, os, outs)
    hf, hd = cfg.half, cfg.heads
    lane = lax.broadcasted_iota(i32, (hf, w), 1)
    for i in range(cfg.row_blocks):
        at = aligned(tab[0, i], cfg.span)
        extra = jnp.zeros((hf, w), f32)
        for h in range(hd):
            rest = ls[pl.ds(pl.multiple_of(at + h * hf, hf), hf), :]
            for n in range(3):
                piece = rest.astype(bf16).astype(f32)
                extra = jnp.where(lane == 3 * h + n, piece, extra)
                rest = rest - piece
        outs[i // 4][(i % 4) * hf:(i % 4 + 1) * hf, hd * w:] = extra.astype(bf16)


def forward(cfg, tab, qpos, q, kv, do):
    wide = cfg.heads * cfg.width
    row, key = (cfg.rows, cfg.width), (cfg.keys, cfg.width)
    found = pl.pallas_call(
        functools.partial(forward_body, cfg),
        out_shape=(jax.ShapeDtypeStruct((cfg.tokens, wide + cfg.width), bf16),) * 4 + (jax.ShapeDtypeStruct((2, cfg.rows), f32),),
        in_specs=[SMEM] + [VMEM] * 13, out_specs=(VMEM,) * 5,
        scratch_shapes=[pltpu.VMEM(row, bf16), pltpu.VMEM(key, bf16), pltpu.VMEM(key, bf16), pltpu.VMEM(key[::-1], bf16),
                        pltpu.VMEM(row, bf16), pltpu.VMEM(row, f32), pltpu.VMEM(row, f32)],
        compiler_params=pltpu.CompilerParams(vmem_limit_bytes=LIMIT),
        name="attend",
    )(tab, qpos, *q, *kv, *do)
    return found[:4], found[4]


def backward_body(cfg, *refs):
    tab, qpos = refs[:2]
    q, kv, do, stat = refs[2:6], refs[6:10], refs[10:14], refs[14:18]
    gq, gkv = refs[18:22], refs[22:26]
    qs, ks, vs, kt, dos, gqs, gks, gvs = refs[26:]
    w, C, R, hf = cfg.width, cfg.C, cfg.R, cfg.half
    load_rows(cfg, tab, q, qs)
    load_rows(cfg, tab, do, dos)
    load_keys(cfg, tab, kv, ks, vs)
    for c in range(cfg.keys // 256):
        kt[:, c * 256:(c + 1) * 256] = ks[c * 256:(c + 1) * 256, :].T
    gks[...] = jnp.zeros_like(gks)
    gvs[...] = jnp.zeros_like(gvs)
    scale = math.log2(math.e) / math.sqrt(w)

    def tile(r, _):
        here = pl.ds(aligned(r, R), R)
        part = [s[0:1, here] for s in stat]
        top = functools.reduce(jnp.maximum, part)
        share = [jnp.exp2(v - top) for v in part]
        total = sum(share)
        lse = top + jnp.log2(total)
        delta = sum(v * s[1:2, here] for v, s in zip(share, stat)) / total

        def step(masked, c, acc):
            keys = pl.ds(aligned(c, C), C)
            s = dot(ks[keys, :], qs[here, :], NT)
            if masked:
                s = jnp.where(visible(cfg, tab, qpos, c, r), s, HIDE)
            p = jnp.exp2(s * scale - lse)
            gw = dot(vs[keys, :], dos[here, :], NT)
            ds = (p * (gw - delta)).astype(bf16)
            gvs[keys, :] += dot(p.astype(bf16), dos[here, :])
            gks[keys, :] += dot(ds, qs[here, :])
            return acc + dot(kt[:, keys], ds)

        acc = lax.fori_loop(0, tab[3, 64 + r], functools.partial(step, False), jnp.zeros((w, R), f32))
        acc = lax.fori_loop(tab[3, 64 + r], tab[3, r], functools.partial(step, True), acc)
        gqs[here, :] = acc.T
        return 0

    lax.fori_loop(0, cfg.nr, tile, 0)
    unload_rows(cfg, tab, gqs, gq)
    per = cfg.key_blocks // len(gkv)
    for n, out in enumerate(gkv):
        def put(j, _):
            own = pl.ds(aligned(tab[1, n * per + j], hf), hf)
            to = pl.ds(aligned(j, hf), hf)
            out[to, :w] = gks[own, :].astype(bf16)
            out[to, w:] = gvs[own, :].astype(bf16)
            return 0

        lax.fori_loop(0, per, put, 0, unroll=4)


def backward(cfg, tab, qpos, q, kv, do, stat):
    row, key = (cfg.rows, cfg.width), (cfg.keys, cfg.width)
    found = pl.pallas_call(
        functools.partial(backward_body, cfg),
        out_shape=(jax.ShapeDtypeStruct((cfg.tokens, cfg.heads * cfg.width), bf16),) * 4
        + (jax.ShapeDtypeStruct((cfg.slab, 2 * cfg.width), bf16),) * 4,
        in_specs=[SMEM] + [VMEM] * 17, out_specs=(VMEM,) * 8,
        scratch_shapes=[pltpu.VMEM(row, bf16), pltpu.VMEM(key, bf16), pltpu.VMEM(key, bf16), pltpu.VMEM(key[::-1], bf16),
                        pltpu.VMEM(row, bf16), pltpu.VMEM(row, f32), pltpu.VMEM(key, f32), pltpu.VMEM(key, f32)],
        compiler_params=pltpu.CompilerParams(vmem_limit_bytes=LIMIT),
        name="grads",
    )(tab, qpos, *q, *kv, *do, *stat)
    return found[:4], found[4:]


def merge_body(cfg, *refs):
    parts, outs = refs[:4], refs[4:]
    w, hd, n = cfg.width, cfg.heads, cfg.tokens // 2
    extra = [p[:, hd * w:].astype(f32) for p in parts]
    level = [e + pltpu.roll(e, w - 1, 1) + pltpu.roll(e, w - 2, 1) for e in extra]
    top = functools.reduce(jnp.maximum, level)
    share = [jnp.exp2(v - top) for v in level]
    total = 1.0 / sum(share)
    share = [v * total for v in share]
    for h in range(hd):
        at = slice(h * w, (h + 1) * w)
        mixed = sum(p[:, at].astype(f32) * v[:, 3 * h:3 * h + 1] for p, v in zip(parts, share)).astype(bf16)
        outs[0][:, at] = mixed[:n]
        outs[1][:, at] = mixed[n:]


def merge(cfg, parts):
    out = jax.ShapeDtypeStruct((cfg.tokens // 2, cfg.heads * cfg.width), bf16)
    return pl.pallas_call(functools.partial(merge_body, cfg), out_shape=(out, out), in_specs=[VMEM] * 4,
                          out_specs=(VMEM,) * 2, name="merge")(*parts)


def add(parts):
    return functools.reduce(jnp.add, [p.astype(f32) for p in parts])


def on_device(query, key, value, d_attended, stretch_ids):
    width = key.shape[2]
    cfg = Cfg(query.shape[2] // width, key.shape[1] // 2, width)
    core = lax.axis_index("inner") & 1
    tab, qpos = tables(cfg, stretch_ids)

    def paired(a):
        mine = lax.dynamic_index_in_dim(a, core, 0, False)
        given = lax.dynamic_index_in_dim(a, 1 - core, 0, False)
        return jnp.concatenate([mine, shift(given, core=1)], axis=0)

    pairs = paired(jnp.concatenate([key, value], axis=2))
    q0 = paired(query)
    do0 = paired(d_attended)
    slab = jnp.concatenate([pairs] + [shift(pairs, dz=-d) for d in range(1, NZ)], axis=0)
    q = [q0] + [shift(q0, dx=-d) for d in range(1, NX)]
    kv = [slab] + [shift(slab, dy=-d) for d in range(1, NY)]
    do = [do0] + [shift(do0, dx=-d) for d in range(1, NX)]
    parts, stat = forward(cfg, tab, qpos, q, kv, do)
    stats = [stat] + [shift(stat, dx=-d) for d in range(1, NX)]
    sent = [parts[0]] + [shift(parts[d], dx=d) for d in range(1, NX)]
    gq, gkv = backward(cfg, tab, qpos, q, kv, do, stats)
    slab = add([gkv[0]] + [shift(gkv[d], dy=d) for d in range(1, NY)]).astype(bf16)
    n = cfg.tokens
    gkv = add([slab[:n]] + [shift(slab[d * n:(d + 1) * n], dz=d) for d in range(1, NZ)])
    gq = add([gq[0]] + [shift(gq[d], dx=d) for d in range(1, NX)])
    att, att_given = merge(cfg, sent)

    def settled(mine, given):
        got = shift(given, core=1)
        return jnp.where(core == 0, jnp.stack([mine, got]), jnp.stack([got, mine]))

    half = n // 2
    scaling = width ** -0.5
    att = settled(att, att_given)
    gq = settled(gq[:half], gq[half:]) * scaling
    gkv = settled(gkv[:half], gkv[half:])
    return att, gq, gkv[..., :width] * scaling, gkv[..., width:]


def solution(mesh):
    split = P(None, AXES, None)
    return jax.shard_map(on_device, mesh=mesh, in_specs=(split,) * 4 + (P(),), out_specs=(split,) * 4, check_vma=False)
```

time: 1160 us -> 184 us (0.16)
  blocking collectives: 386 us -> 0 us
  waiting for transfers between devices: 387 us -> 42.2 us
  matrix products: 219 us -> 0 us
  local copies, waits for them, and re-layouts: 73.7 us -> 3.19 us
  Pallas kernels: 0 us -> 66.3 us
  starting transfers between devices: 0.16 us -> 66 us
  other arithmetic: 66.4 us -> 3.47 us
  between operations: 14.7 us -> 0.85 us
    unnamed x6 -> x0, waiting for transfers between devices: 387 us -> none
    all_gather x12 -> x0, blocking collectives: 386 us -> none  [the longest x4 114 us: merged(): gathered = jax.tree.map(lambda a: lax.all_gather(a, axis), part)]
    dot_general x168 -> x0, matrix products: 219 us -> none  [the longest x24 49.9 us: gradients(): jnp.dot(grad_scores, key_rows, preferred_element_type=jnp.float32)]
    pallas_call x0 -> x4, Pallas kernels: none -> 66.3 us  [the longest x1 31.7 us: forward(): pl.pallas_call(functools.partial(forward_body, cfg), out_shape=(jax.Shape...]
    ppermute x0 -> x41, starting transfers between devices: none -> 66 us  [shift(): return lax.ppermute(a, AXES, pairs)]
    ppermute x0 -> x41, waiting for transfers between devices: none -> 42.2 us  [shift(): return lax.ppermute(a, AXES, pairs)]
    add x40 -> x2, other arithmetic: 35.4 us -> 1.06 us  [add(): return functools.reduce(jnp.add, [p.astype(f32) for p in parts])]
    another operation x28 -> x2, local copies, waits for them, and re-layouts: 15.7 us -> 0.03 us  [settled(): return jnp.where(core == 0, jnp.stack([mine, got]), jnp.stack([got, mine]))]
  transfers between devices with their start and end apart: 4 -> 41, of which waited for: 2 -> 18; matrix products, arithmetic and copies ran while one was open for 7% -> 2% of each run, Pallas kernels for 0% -> 2%
where the time goes in v1:
time: 184 us; the launch traced here: 182 us
  Pallas kernels  66.3 us (36%)
  starting transfers between devices  66 us (36%)
  waiting for transfers between devices  42.2 us (23%)
  other arithmetic  3.47 us (2%)
  local copies, waits for them, and re-layouts  3.19 us (2%)
    ppermute x41, starting transfers between devices, shift(): return lax.ppermute(a, AXES, pairs)  66 us
    ppermute x41, waiting for transfers between devices, shift(): return lax.ppermute(a, AXES, pairs)  42.2 us
    pallas_call x1, Pallas kernels, forward(): pl.pallas_call(functools.partial(forward_body, cfg), out_shape=(jax.Shape...  31.7 us
    pallas_call x1, Pallas kernels, backward(): pl.pallas_call(functools.partial(backward_body, cfg), out_shape=(jax.Shap...  30.4 us
  transfers between devices with their start and end apart: 41, of which 18 were waited for; matrix products, arithmetic and copies ran while one was open for 2% of the time, Pallas kernels for 2%

profile of v1, /device:TPU:1, one launch (start us, length us, event | category | flops | bytes accessed | tf_op | source)
XLA Modules:
  0.0 182.0 jit_solution(45752944634919372)
XLA Ops:
  1.6 3.3 %collective-permute-start = (bf16[64,640]{1,0:T(8,128)(2,1)S(1)}, bf16[64,640]{1,0:T(8,128)(2,1)S(1)}, u32[]{:S(2)}, u32[]{:S(2)}) collective-permute-start(bf16[64,640]{1,0:T(8,128)(2,1)S(1)} %get-tuple-element.52), channel_id=1, source_target_pairs={{0,1},{1,0},{2,3},{3,2},{4,5},{5,4},{6,7},{7,6},{8,9},{9,8},{10,11... | collective-permute-start | bytes 245768 | tf_op jit(solution)/shard_map/ppermute | solution.py:43
  6.3 3.8 %collective-permute-start.5 = (bf16[128,256]{1,0:T(8,128)(2,1)S(1)}, bf16[128,256]{1,0:T(8,128)(2,1)S(1)}, u32[]{:S(2)}, u32[]{:S(2)}) collective-permute-start(bf16[128,256]{1,0:T(8,128)(2,1)S(1)} %pad_maximum_fusion.2), channel_id=1, source_target_pairs={{0,14},{1,15},{2,0},{3,1},{4,2},{5,3},{6,4},{7,5},{8,6},{9,7},{10,... | collective-permute-start | bytes 196616 | tf_op jit(solution)/shard_map/ppermute | solution.py:43
  11.8 4.5 %collective-permute-start.8 = (bf16[128,256]{1,0:T(8,128)(2,1)S(1)}, bf16[128,256]{1,0:T(8,128)(2,1)S(1)}, u32[]{:S(2)}, u32[]{:S(2)}) collective-permute-start(bf16[128,256]{1,0:T(8,128)(2,1)S(1)} %pad_maximum_fusion.2), channel_id=1, source_target_pairs={{0,8},{1,9},{2,10},{3,11},{4,12},{5,13},{6,14},{7,15},{8,0},{9,1},... | collective-permute-start | bytes 196616 | tf_op jit(solution)/shard_map/ppermute | solution.py:43
  18.0 3.8 %collective-permute-start.10 = (bf16[128,256]{1,0:T(8,128)(2,1)S(1)}, bf16[128,256]{1,0:T(8,128)(2,1)S(1)}, u32[]{:S(2)}, u32[]{:S(2)}) collective-permute-start(bf16[128,256]{1,0:T(8,128)(2,1)S(1)} %pad_maximum_fusion.2), channel_id=1, source_target_pairs={{0,4},{1,5},{2,6},{3,7},{4,8},{5,9},{6,10},{7,11},{8,12},{9,13},{1... | collective-permute-start | bytes 196616 | tf_op jit(solution)/shard_map/ppermute | solution.py:43
  21.8 3.6 %collective-permute-start.11 = (bf16[128,256]{1,0:T(8,128)(2,1)S(1)}, bf16[128,256]{1,0:T(8,128)(2,1)S(1)}, u32[]{:S(2)}, u32[]{:S(2)}) collective-permute-start(bf16[128,256]{1,0:T(8,128)(2,1)S(1)} %pad_maximum_fusion.2), channel_id=1, source_target_pairs={{0,2},{1,3},{2,4},{3,5},{4,6},{5,7},{6,8},{7,9},{8,10},{9,11},{10,... | collective-permute-start | bytes 196616 | tf_op jit(solution)/shard_map/ppermute | solution.py:43
  25.4 2.6 %collective-permute-done.10 = bf16[128,256]{1,0:T(8,128)(2,1)S(1)} collective-permute-done((bf16[128,256]{1,0:T(8,128)(2,1)S(1)}, bf16[128,256]{1,0:T(8,128)(2,1)S(1)}, u32[]{:S(2)}, u32[]{:S(2)}) %collective-permute-start.10) | collective-permute-done | bytes 65568 | tf_op jit(solution)/shard_map/ppermute | solution.py:43
  28.0 2.8 %collective-permute-start.12 = (bf16[1024,256]{1,0:T(8,128)(2,1)S(1)}, bf16[1024,256]{1,0:T(8,128)(2,1)S(1)}, u32[]{:S(2)}, u32[]{:S(2)}) collective-permute-start(bf16[1024,256]{1,0:T(8,128)(2,1)S(1)} %constant_dynamic-update-slice_fusion.2.refs_6_), channel_id=1, source_target_pairs={{0,48},{1,49},{2,50},{3,51},{4,52},{5,53},{6,54},{7,55},{8,56},{9,... | collective-permute-start | bytes 1572872 | tf_op jit(solution)/shard_map/ppermute | solution.py:43
  31.9 2.6 %collective-permute-start.1 = (bf16[128,640]{1,0:T(8,128)(2,1)S(1)}, bf16[128,640]{1,0:T(8,128)(2,1)S(1)}, u32[]{:S(2)}, u32[]{:S(2)}) collective-permute-start(bf16[128,640]{1,0:T(8,128)(2,1)S(1)} %pad_maximum_fusion.refs_2_), channel_id=1, source_target_pairs={{0,192},{1,193},{2,194},{3,195},{4,196},{5,197},{6,198},{7,199},{8... | collective-permute-start | bytes 491528 | tf_op jit(solution)/shard_map/ppermute | solution.py:43
  35.0 3.5 %collective-permute-done.1.refs_3_ = bf16[128,640]{1,0:T(8,128)(2,1)S(1)} collective-permute-done((bf16[128,640]{1,0:T(8,128)(2,1)S(1)}, bf16[128,640]{1,0:T(8,128)(2,1)S(1)}, u32[]{:S(2)}, u32[]{:S(2)}) %collective-permute-start.1) | collective-permute-done | bytes 163872 | tf_op jit(solution)/shard_map/ppermute | solution.py:43
  41.8 4.4 %collective-permute-done.3.refs_5_ = bf16[128,640]{1,0:T(8,128)(2,1)S(1)} collective-permute-done((bf16[128,640]{1,0:T(8,128)(2,1)S(1)}, bf16[128,640]{1,0:T(8,128)(2,1)S(1)}, u32[]{:S(2)}, u32[]{:S(2)}) %collective-permute-start.3) | collective-permute-done | bytes 163872 | tf_op jit(solution)/shard_map/ppermute | solution.py:43
  48.9 3.4 %collective-permute-done.17.refs_12_ = bf16[128,640]{1,0:T(8,128)(2,1)S(1)} collective-permute-done((bf16[128,640]{1,0:T(8,128)(2,1)S(1)}, bf16[128,640]{1,0:T(8,128)(2,1)S(1)}, u32[]{:S(2)}, u32[]{:S(2)}) %collective-permute-start.17) | collective-permute-done | bytes 163872 | tf_op jit(solution)/shard_map/ppermute | solution.py:43
  53.7 3.7 %collective-permute-done.14.refs_9_ = bf16[1024,256]{1,0:T(8,128)(2,1)S(1)} collective-permute-done((bf16[1024,256]{1,0:T(8,128)(2,1)S(1)}, bf16[1024,256]{1,0:T(8,128)(2,1)S(1)}, u32[]{:S(2)}, u32[]{:S(2)}) %collective-permute-start.14) | collective-permute-done | bytes 524320 | tf_op jit(solution)/shard_map/ppermute | solution.py:43
  58.1 31.7 %attend.1 = (bf16[128,768]{1,0:T(8,128)(2,1)S(1)}, bf16[128,768]{1,0:T(8,128)(2,1)}, bf16[128,768]{1,0:T(8,128)(2,1)S(1)}, bf16[128,768]{1,0:T(8,128)(2,1)S(1)}, f32[2,2560]{1,0:T(2,128)S(1)}) custom-call(s32[4,128]{1,0:T(4,128)S(1)} %copy-done.4, s32[1,2560]{1,0:T(1,128)S(1)} %copy-done.3, bf16[128,640]{1,0:T(8,128)(2,1)S(1)} %pad_maximum_fusion.refs_2_, ...), custom_call_target="tpu_custom_call" | custom-call | tf_op jit(solution)/shard_map/attend/pallas_call | solution.py:200
  93.0 3.0 %collective-permute-done.24.refs_16_ = f32[2,2560]{1,0:T(2,128)S(1)} collective-permute-done((f32[2,2560]{1,0:T(2,128)S(1)}, f32[2,2560]{1,0:T(2,128)S(1)}, u32[]{:S(2)}, u32[]{:S(2)}) %collective-permute-start.24) | collective-permute-done | bytes 20512 | tf_op jit(solution)/shard_map/ppermute | solution.py:43
  96.7 30.4 %grads.1 = (bf16[128,640]{1,0:T(8,128)(2,1)S(1)}, bf16[128,640]{1,0:T(8,128)(2,1)}, bf16[128,640]{1,0:T(8,128)(2,1)S(1)}, bf16[128,640]{1,0:T(8,128)(2,1)S(1)}, ...) custom-call(s32[4,128]{1,0:T(4,128)S(1)} %copy-done.4, ...), custom_call_target="tpu_custom_call" | custom-call | tf_op jit(solution)/shard_map/grads/pallas_call | solution.py:269
  133.4 2.5 %collective-permute-start.26 = (bf16[128,640]{1,0:T(8,128)(2,1)}, bf16[128,640]{1,0:T(8,128)(2,1)S(1)}, u32[]{:S(2)}, u32[]{:S(2)}) collective-permute-start(bf16[128,640]{1,0:T(8,128)(2,1)} %get-tuple-element.31), channel_id=1, source_target_pairs={{0,64},{1,65},{2,66},{3,67},{4,68},{5,69},{6,70},{7,71},{8,72},{9,... | collective-permute-start | bytes 491528 | tf_op jit(solution)/shard_map/ppermute | solution.py:43
  135.9 4.5 %collective-permute-done.26 = bf16[128,640]{1,0:T(8,128)(2,1)S(1)} collective-permute-done((bf16[128,640]{1,0:T(8,128)(2,1)}, bf16[128,640]{1,0:T(8,128)(2,1)S(1)}, u32[]{:S(2)}, u32[]{:S(2)}) %collective-permute-start.26) | collective-permute-done | bytes 163872 | tf_op jit(solution)/shard_map/ppermute | solution.py:43
  141.0 3.3 %collective-permute-start.21 = (bf16[128,768]{1,0:T(8,128)(2,1)}, bf16[128,768]{1,0:T(8,128)(2,1)S(1)}, u32[]{:S(2)}, u32[]{:S(2)}) collective-permute-start(bf16[128,768]{1,0:T(8,128)(2,1)} %copy-done.5), channel_id=1, source_target_pairs={{0,192},{1,193},{2,194},{3,195},{4,196},{5,197},{6,198},{7,199},{8... | collective-permute-start | bytes 589832 | tf_op jit(solution)/shard_map/ppermute | solution.py:43
  148.7 2.5 %merge.1 = (bf16[64,640]{1,0:T(8,128)(2,1)}, bf16[64,640]{1,0:T(8,128)(2,1)}) custom-call(bf16[128,768]{1,0:T(8,128)(2,1)} %copy-done.1, bf16[128,768]{1,0:T(8,128)(2,1)} %copy-done.7, bf16[128,768]{1,0:T(8,128)(2,1)} %copy-done.8, bf16[128,768]{1,0:T(8,128)(2,1)} %copy-done.9), custom_call_target="tpu_custom_call" | custom-call | tf_op jit(solution)/shard_map/merge/pallas_call | solution.py:300
  151.1 5.3 %collective-permute-start.22 = (bf16[64,640]{1,0:T(8,128)(2,1)}, bf16[64,640]{1,0:T(8,128)(2,1)S(1)}, u32[]{:S(2)}, u32[]{:S(2)}) collective-permute-start(bf16[64,640]{1,0:T(8,128)(2,1)} %get-tuple-element.28), channel_id=1, source_target_pairs={{0,1},{1,0},{2,3},{3,2},{4,5},{5,4},{6,7},{7,6},{8,9},{9,8},{10,11... | collective-permute-start | bytes 245768 | tf_op jit(solution)/shard_map/ppermute | solution.py:43
  156.7 2.5 %collective-permute-start.39 = (bf16[128,256]{1,0:T(8,128)(2,1)S(1)}, bf16[128,256]{1,0:T(8,128)(2,1)S(1)}, u32[]{:S(2)}, u32[]{:S(2)}) collective-permute-start(bf16[128,256]{1,0:T(8,128)(2,1)S(1)} %get-tuple-element.41), channel_id=1, source_target_pairs={{0,14},{1,15},{2,0},{3,1},{4,2},{5,3},{6,4},{7,5},{8,6},{9,7},{10,... | collective-permute-start | bytes 196616 | tf_op jit(solution)/shard_map/ppermute | solution.py:43
  161.4 2.9 %collective-permute-start.37 = (bf16[128,256]{1,0:T(8,128)(2,1)S(1)}, bf16[128,256]{1,0:T(8,128)(2,1)S(1)}, u32[]{:S(2)}, u32[]{:S(2)}) collective-permute-start(bf16[128,256]{1,0:T(8,128)(2,1)S(1)} %get-tuple-element.43), channel_id=1, source_target_pairs={{0,10},{1,11},{2,12},{3,13},{4,14},{5,15},{6,0},{7,1},{8,2},{9,3},... | collective-permute-start | bytes 196616 | tf_op jit(solution)/shard_map/ppermute | solution.py:43
  165.0 2.4 %collective-permute-start.35 = (bf16[128,256]{1,0:T(8,128)(2,1)S(1)}, bf16[128,256]{1,0:T(8,128)(2,1)S(1)}, u32[]{:S(2)}, u32[]{:S(2)}) collective-permute-start(bf16[128,256]{1,0:T(8,128)(2,1)S(1)} %get-tuple-element.45), channel_id=1, source_target_pairs={{0,6},{1,7},{2,8},{3,9},{4,10},{5,11},{6,12},{7,13},{8,14},{9,15},... | collective-permute-start | bytes 196616 | tf_op jit(solution)/shard_map/ppermute | solution.py:43
  172.5 4.6 %collective-permute-done.35 = bf16[128,256]{1,0:T(8,128)(2,1)S(1)} collective-permute-done((bf16[128,256]{1,0:T(8,128)(2,1)S(1)}, bf16[128,256]{1,0:T(8,128)(2,1)S(1)}, u32[]{:S(2)}, u32[]{:S(2)}) %collective-permute-start.35) | collective-permute-done | bytes 65568 | tf_op jit(solution)/shard_map/ppermute | solution.py:43
  (117 shorter events, 43.8 us)
Async XLA Ops:
  1.6 30.2 %collective-permute-start = (bf16[64,640]{1,0:T(8,128)(2,1)S(1)}, bf16[64,640]{1,0:T(8,128)(2,1)S(1)}, u32[]{:S(2)}, u32[]{:S(2)}) collective-permute-start(bf16[64,640]{1,0:T(8,128)(2,1)S(1)} %get-tuple-element.52), channel_id=1, source_target_pairs={{0,1},{1,0},{2,3},{3,2},{4,5},{5,4},{6,7},{7,6},{8,9},{9,8},{10,11... | collective-permute-start | bytes 245768 | tf_op jit(solution)/shard_map/ppermute | solution.py:43
  5.2 29.3 %collective-permute-start.15 = (bf16[64,640]{1,0:T(8,128)(2,1)S(1)}, bf16[64,640]{1,0:T(8,128)(2,1)S(1)}, u32[]{:S(2)}, u32[]{:S(2)}) collective-permute-start(bf16[64,640]{1,0:T(8,128)(2,1)S(1)} %get-tuple-element.50), channel_id=1, source_target_pairs={{0,1},{1,0},{2,3},{3,2},{4,5},{5,4},{6,7},{7,6},{8,9},{9,8},{10,11... | collective-permute-start | bytes 245768 | tf_op jit(solution)/shard_map/ppermute | solution.py:43
  11.8 10.0 %collective-permute-start.8 = (bf16[128,256]{1,0:T(8,128)(2,1)S(1)}, bf16[128,256]{1,0:T(8,128)(2,1)S(1)}, u32[]{:S(2)}, u32[]{:S(2)}) collective-permute-start(bf16[128,256]{1,0:T(8,128)(2,1)S(1)} %pad_maximum_fusion.2), channel_id=1, source_target_pairs={{0,8},{1,9},{2,10},{3,11},{4,12},{5,13},{6,14},{7,15},{8,0},{9,1},... | collective-permute-start | bytes 196616 | tf_op jit(solution)/shard_map/ppermute | solution.py:43
  16.3 9.1 %collective-permute-start.9 = (bf16[128,256]{1,0:T(8,128)(2,1)S(1)}, bf16[128,256]{1,0:T(8,128)(2,1)S(1)}, u32[]{:S(2)}, u32[]{:S(2)}) collective-permute-start(bf16[128,256]{1,0:T(8,128)(2,1)S(1)} %pad_maximum_fusion.2), channel_id=1, source_target_pairs={{0,6},{1,7},{2,8},{3,9},{4,10},{5,11},{6,12},{7,13},{8,14},{9,15},... | collective-permute-start | bytes 196616 | tf_op jit(solution)/shard_map/ppermute | solution.py:43
  18.0 10.0 %collective-permute-start.10 = (bf16[128,256]{1,0:T(8,128)(2,1)S(1)}, bf16[128,256]{1,0:T(8,128)(2,1)S(1)}, u32[]{:S(2)}, u32[]{:S(2)}) collective-permute-start(bf16[128,256]{1,0:T(8,128)(2,1)S(1)} %pad_maximum_fusion.2), channel_id=1, source_target_pairs={{0,4},{1,5},{2,6},{3,7},{4,8},{5,9},{6,10},{7,11},{8,12},{9,13},{1... | collective-permute-start | bytes 196616 | tf_op jit(solution)/shard_map/ppermute | solution.py:43
  28.0 25.7 %collective-permute-start.12 = (bf16[1024,256]{1,0:T(8,128)(2,1)S(1)}, bf16[1024,256]{1,0:T(8,128)(2,1)S(1)}, u32[]{:S(2)}, u32[]{:S(2)}) collective-permute-start(bf16[1024,256]{1,0:T(8,128)(2,1)S(1)} %constant_dynamic-update-slice_fusion.2.refs_6_), channel_id=1, source_target_pairs={{0,48},{1,49},{2,50},{3,51},{4,52},{5,53},{6,54},{7,55},{8,56},{9,... | collective-permute-start | bytes 1572872 | tf_op jit(solution)/shard_map/ppermute | solution.py:43
  30.8 22.9 %collective-permute-start.13 = (bf16[1024,256]{1,0:T(8,128)(2,1)S(1)}, bf16[1024,256]{1,0:T(8,128)(2,1)S(1)}, u32[]{:S(2)}, u32[]{:S(2)}) collective-permute-start(bf16[1024,256]{1,0:T(8,128)(2,1)S(1)} %constant_dynamic-update-slice_fusion.2.refs_6_), channel_id=1, source_target_pairs={{0,32},{1,33},{2,34},{3,35},{4,36},{5,37},{6,38},{7,39},{8,40},{9,... | collective-permute-start | bytes 1572872 | tf_op jit(solution)/shard_map/ppermute | solution.py:43
  31.1 26.2 %collective-permute-start.14 = (bf16[1024,256]{1,0:T(8,128)(2,1)S(1)}, bf16[1024,256]{1,0:T(8,128)(2,1)S(1)}, u32[]{:S(2)}, u32[]{:S(2)}) collective-permute-start(bf16[1024,256]{1,0:T(8,128)(2,1)S(1)} %constant_dynamic-update-slice_fusion.2.refs_6_), channel_id=1, source_target_pairs={{0,16},{1,17},{2,18},{3,19},{4,20},{5,21},{6,22},{7,23},{8,24},{9,... | collective-permute-start | bytes 1572872 | tf_op jit(solution)/shard_map/ppermute | solution.py:43
  38.4 7.8 %collective-permute-start.3 = (bf16[128,640]{1,0:T(8,128)(2,1)S(1)}, bf16[128,640]{1,0:T(8,128)(2,1)S(1)}, u32[]{:S(2)}, u32[]{:S(2)}) collective-permute-start(bf16[128,640]{1,0:T(8,128)(2,1)S(1)} %pad_maximum_fusion.refs_2_), channel_id=1, source_target_pairs={{0,64},{1,65},{2,66},{3,67},{4,68},{5,69},{6,70},{7,71},{8,72},{9,... | collective-permute-start | bytes 491528 | tf_op jit(solution)/shard_map/ppermute | solution.py:43
  46.2 7.4 %collective-permute-start.18 = (bf16[128,640]{1,0:T(8,128)(2,1)S(1)}, bf16[128,640]{1,0:T(8,128)(2,1)S(1)}, u32[]{:S(2)}, u32[]{:S(2)}) collective-permute-start(bf16[128,640]{1,0:T(8,128)(2,1)S(1)} %pad_maximum_fusion.1.refs_10_), channel_id=1, source_target_pairs={{0,64},{1,65},{2,66},{3,67},{4,68},{5,69},{6,70},{7,71},{8,72},{9,... | collective-permute-start | bytes 491528 | tf_op jit(solution)/shard_map/ppermute | solution.py:43
  128.6 27.8 %collective-permute-start.32 = (bf16[1024,256]{1,0:T(8,128)(2,1)}, bf16[1024,256]{1,0:T(8,128)(2,1)S(1)}, u32[]{:S(2)}, u32[]{:S(2)}) collective-permute-start(bf16[1024,256]{1,0:T(8,128)(2,1)} %get-tuple-element.37), channel_id=1, source_target_pairs={{0,48},{1,49},{2,50},{3,51},{4,52},{5,53},{6,54},{7,55},{8,56},{9,... | collective-permute-start | bytes 1572872 | tf_op jit(solution)/shard_map/ppermute | solution.py:43
  128.6 27.8 %collective-permute-start.31 = (bf16[1024,256]{1,0:T(8,128)(2,1)}, bf16[1024,256]{1,0:T(8,128)(2,1)S(1)}, u32[]{:S(2)}, u32[]{:S(2)}) collective-permute-start(bf16[1024,256]{1,0:T(8,128)(2,1)} %get-tuple-element.36), channel_id=1, source_target_pairs={{0,32},{1,33},{2,34},{3,35},{4,36},{5,37},{6,38},{7,39},{8,40},{9,... | collective-permute-start | bytes 1572872 | tf_op jit(solution)/shard_map/ppermute | solution.py:43
  129.6 26.8 %collective-permute-start.30 = (bf16[1024,256]{1,0:T(8,128)(2,1)}, bf16[1024,256]{1,0:T(8,128)(2,1)S(1)}, u32[]{:S(2)}, u32[]{:S(2)}) collective-permute-start(bf16[1024,256]{1,0:T(8,128)(2,1)} %get-tuple-element.35), channel_id=1, source_target_pairs={{0,16},{1,17},{2,18},{3,19},{4,20},{5,21},{6,22},{7,23},{8,24},{9,... | collective-permute-start | bytes 1572872 | tf_op jit(solution)/shard_map/ppermute | solution.py:43
  131.9 9.1 %collective-permute-start.19 = (bf16[128,768]{1,0:T(8,128)(2,1)}, bf16[128,768]{1,0:T(8,128)(2,1)S(1)}, u32[]{:S(2)}, u32[]{:S(2)}) collective-permute-start(bf16[128,768]{1,0:T(8,128)(2,1)} %get-tuple-element.24), channel_id=1, source_target_pairs={{0,64},{1,65},{2,66},{3,67},{4,68},{5,69},{6,70},{7,71},{8,72},{9,... | collective-permute-start | bytes 589832 | tf_op jit(solution)/shard_map/ppermute | solution.py:43
  141.0 7.0 %collective-permute-start.21 = (bf16[128,768]{1,0:T(8,128)(2,1)}, bf16[128,768]{1,0:T(8,128)(2,1)S(1)}, u32[]{:S(2)}, u32[]{:S(2)}) collective-permute-start(bf16[128,768]{1,0:T(8,128)(2,1)} %copy-done.5), channel_id=1, source_target_pairs={{0,192},{1,193},{2,194},{3,195},{4,196},{5,197},{6,198},{7,199},{8... | collective-permute-start | bytes 589832 | tf_op jit(solution)/shard_map/ppermute | solution.py:43
  151.1 13.8 %collective-permute-start.22 = (bf16[64,640]{1,0:T(8,128)(2,1)}, bf16[64,640]{1,0:T(8,128)(2,1)S(1)}, u32[]{:S(2)}, u32[]{:S(2)}) collective-permute-start(bf16[64,640]{1,0:T(8,128)(2,1)} %get-tuple-element.28), channel_id=1, source_target_pairs={{0,1},{1,0},{2,3},{3,2},{4,5},{5,4},{6,7},{7,6},{8,9},{9,8},{10,11... | collective-permute-start | bytes 245768 | tf_op jit(solution)/shard_map/ppermute | solution.py:43
  156.7 10.7 %collective-permute-start.39 = (bf16[128,256]{1,0:T(8,128)(2,1)S(1)}, bf16[128,256]{1,0:T(8,128)(2,1)S(1)}, u32[]{:S(2)}, u32[]{:S(2)}) collective-permute-start(bf16[128,256]{1,0:T(8,128)(2,1)S(1)} %get-tuple-element.41), channel_id=1, source_target_pairs={{0,14},{1,15},{2,0},{3,1},{4,2},{5,3},{6,4},{7,5},{8,6},{9,7},{10,... | collective-permute-start | bytes 196616 | tf_op jit(solution)/shard_map/ppermute | solution.py:43
  159.3 9.8 %collective-permute-start.38 = (bf16[128,256]{1,0:T(8,128)(2,1)S(1)}, bf16[128,256]{1,0:T(8,128)(2,1)S(1)}, u32[]{:S(2)}, u32[]{:S(2)}) collective-permute-start(bf16[128,256]{1,0:T(8,128)(2,1)S(1)} %get-tuple-element.42), channel_id=1, source_target_pairs={{0,12},{1,13},{2,14},{3,15},{4,0},{5,1},{6,2},{7,3},{8,4},{9,5},{1... | collective-permute-start | bytes 196616 | tf_op jit(solution)/shard_map/ppermute | solution.py:43
  161.4 9.3 %collective-permute-start.37 = (bf16[128,256]{1,0:T(8,128)(2,1)S(1)}, bf16[128,256]{1,0:T(8,128)(2,1)S(1)}, u32[]{:S(2)}, u32[]{:S(2)}) collective-permute-start(bf16[128,256]{1,0:T(8,128)(2,1)S(1)} %get-tuple-element.43), channel_id=1, source_target_pairs={{0,10},{1,11},{2,12},{3,13},{4,14},{5,15},{6,0},{7,1},{8,2},{9,3},... | collective-permute-start | bytes 196616 | tf_op jit(solution)/shard_map/ppermute | solution.py:43
  164.3 8.1 %collective-permute-start.36 = (bf16[128,256]{1,0:T(8,128)(2,1)S(1)}, bf16[128,256]{1,0:T(8,128)(2,1)S(1)}, u32[]{:S(2)}, u32[]{:S(2)}) collective-permute-start(bf16[128,256]{1,0:T(8,128)(2,1)S(1)} %get-tuple-element.44), channel_id=1, source_target_pairs={{0,8},{1,9},{2,10},{3,11},{4,12},{5,13},{6,14},{7,15},{8,0},{9,1},... | collective-permute-start | bytes 196616 | tf_op jit(solution)/shard_map/ppermute | solution.py:43
  165.0 12.1 %collective-permute-start.35 = (bf16[128,256]{1,0:T(8,128)(2,1)S(1)}, bf16[128,256]{1,0:T(8,128)(2,1)S(1)}, u32[]{:S(2)}, u32[]{:S(2)}) collective-permute-start(bf16[128,256]{1,0:T(8,128)(2,1)S(1)} %get-tuple-element.45), channel_id=1, source_target_pairs={{0,6},{1,7},{2,8},{3,9},{4,10},{5,11},{6,12},{7,13},{8,14},{9,15},... | collective-permute-start | bytes 196616 | tf_op jit(solution)/shard_map/ppermute | solution.py:43
  167.4 9.7 %collective-permute-start.34 = (bf16[128,256]{1,0:T(8,128)(2,1)S(1)}, bf16[128,256]{1,0:T(8,128)(2,1)S(1)}, u32[]{:S(2)}, u32[]{:S(2)}) collective-permute-start(bf16[128,256]{1,0:T(8,128)(2,1)S(1)} %get-tuple-element.46), channel_id=1, source_target_pairs={{0,4},{1,5},{2,6},{3,7},{4,8},{5,9},{6,10},{7,11},{8,12},{9,13},{1... | collective-permute-start | bytes 196616 | tf_op jit(solution)/shard_map/ppermute | solution.py:43
  169.1 10.2 %collective-permute-start.33 = (bf16[128,256]{1,0:T(8,128)(2,1)S(1)}, bf16[128,256]{1,0:T(8,128)(2,1)S(1)}, u32[]{:S(2)}, u32[]{:S(2)}) collective-permute-start(bf16[128,256]{1,0:T(8,128)(2,1)S(1)} %get-tuple-element.40), channel_id=1, source_target_pairs={{0,2},{1,3},{2,4},{3,5},{4,6},{5,7},{6,8},{7,9},{8,10},{9,11},{10,... | collective-permute-start | bytes 196616 | tf_op jit(solution)/shard_map/ppermute | solution.py:43
  170.8 9.7 %collective-permute-start.29 = (f32[64,640]{1,0:T(8,128)S(1)}, f32[64,640]{1,0:T(8,128)S(1)}, u32[]{:S(2)}, u32[]{:S(2)}) collective-permute-start(f32[64,640]{1,0:T(8,128)S(1)} %get-tuple-element.48), channel_id=1, source_target_pairs={{0,1},{1,0},{2,3},{3,2},{4,5},{5,4},{6,7},{7,6},{8,9},{9,8},{10,11... | collective-permute-start | bytes 491528 | tf_op jit(solution)/shard_map/ppermute | solution.py:43
  (31 other events, 269.8 us)

commit v2 on v1

v2 whole, which is shorter than its diff:
```python
import functools, math
import jax
import jax.numpy as jnp
from jax import lax
from jax.experimental import pallas as pl
from jax.experimental.pallas import tpu as pltpu
from jax.sharding import PartitionSpec as P

bf16, f32, i32 = jnp.bfloat16, jnp.float32, jnp.int32
HIDE = -float(2**18)
NONE = -1e30
NT = (((1,), (1,)), ((), ()))
NN = (((1,), (0,)), ((), ()))
SMEM = pl.BlockSpec(memory_space=pltpu.SMEM)
VMEM = pl.BlockSpec(memory_space=pltpu.VMEM)
LIMIT = 20 * 2**20
AXES = ("outer", "inner")
NX, NY, NZ = 4, 4, 8


def dot(a, b, dims=NN):
    return lax.dot_general(a, b, dims, preferred_element_type=f32)


class Cfg:
    def __init__(s, heads, half, width, C=256, R=256, G=4):
        s.heads, s.half, s.width, s.C, s.R, s.G = heads, half, width, C, R, G
        s.tokens = 4 * half
        s.span = half * heads
        s.row_blocks, s.slab_blocks = 4 * NX, 4 * NZ
        s.rows, s.slab = s.row_blocks * s.span, s.slab_blocks * half
        s.nr = s.rows // R


def place(x, y, z, core):
    return (x * 2 + (y >> 1)) * 32 + ((y & 1) * NZ + z) * 2 + core


def shift(a, dx=0, dy=0, dz=0, core=0):
    pairs = [(place(x, y, z, c), place((x + dx) % NX, (y + dy) % NY, (z + dz) % NZ, c ^ core))
             for x in range(NX) for y in range(NY) for z in range(NZ) for c in range(2)]
    return lax.ppermute(a, AXES, pairs)


def tables_body(cfg, sets, shard_count, ids, *refs):
    tabs, qpos_ref = refs[:-1], refs[-1]
    hf, span = cfg.half, cfg.span
    outer_at, inner_at = lax.axis_index("outer"), lax.axis_index("inner")
    x, core = outer_at >> 1, inner_at & 1
    y, z = (outer_at & 1) * 2 + (inner_at >> 4), (inner_at >> 1) & 7
    top = 2 * shard_count - 1
    line = lax.broadcasted_iota(i32, (1, 128), 1)

    def ranked(count, source):
        held = jnp.full((1, 128), 0, i32)
        for j in range(count):
            held = jnp.where(line >> 1 == j, ids[source(j)], held)
        held = jnp.where(line & 1 == 1, top - held, held)
        held = jnp.where(line < 2 * count, held, top + 1 + line).astype(f32)
        across = jnp.broadcast_to(held, (128, 128))
        down = across.T
        lane = lax.broadcasted_iota(i32, (128, 128), 1)
        rank = jnp.sum((down < across).astype(f32), axis=0, keepdims=True)
        rank_down = jnp.sum((across < down).astype(f32), axis=1, keepdims=True).astype(i32)
        rising = jnp.sum(jnp.where(rank_down == lane, down, 0.0), axis=0, keepdims=True)
        return rank, rising

    row_rank, rows = ranked(2 * NX, lambda j: place((x + (j >> 1)) & (NX - 1), y, z, core ^ (j & 1)))
    row_down = jnp.broadcast_to(rows, (128, 128)).T
    for slabs, tab_ref in zip(sets, tabs):
        key_rank, keys = ranked(
            2 * NZ * len(slabs), lambda j: place(x, (y + slabs[j >> 4]) & (NY - 1), (z + ((j >> 1) & 7)) & (NZ - 1), core ^ (j & 1)))
        counts = jnp.zeros((1, 128), f32)
        for r in range(cfg.nr):
            last = ((r + 1) * cfg.R - 1) // span
            seen = jnp.sum((keys <= row_down[last:last + 1]).astype(f32), axis=1, keepdims=True)
            chunks = jnp.maximum(jnp.floor((seen * hf + (cfg.C - 1)) * (1.0 / cfg.C)), 1.0)
            counts = jnp.where(line == r, chunks, counts) + jnp.where(line == 127, chunks, 0.0)
        tab_ref[0:1] = row_rank.astype(i32)
        tab_ref[1:2] = key_rank.astype(i32)
        tab_ref[2:3] = keys.astype(i32)
        tab_ref[3:4] = counts.astype(i32)
    spot = lax.broadcasted_iota(i32, (1, cfg.rows), 1)
    pos = jnp.zeros((1, cfg.rows), f32)
    for i in range(cfg.row_blocks):
        pos = jnp.where(spot >= i * span, row_down[i:i + 1, :1], pos)
    qpos_ref[...] = pos.astype(i32) * hf + (spot & (hf - 1))


def tables(cfg, sets, ids):
    found = pl.pallas_call(
        functools.partial(tables_body, cfg, sets, ids.shape[0]),
        out_shape=(jax.ShapeDtypeStruct((4, 128), i32),) * len(sets) + (jax.ShapeDtypeStruct((1, cfg.rows), i32),),
        in_specs=[SMEM], out_specs=(VMEM,) * (len(sets) + 1), name="tables",
    )(ids)
    return found[:-1], found[-1]


def aligned(at, by):
    return at * by if isinstance(at, int) else pl.multiple_of(at * by, by)


def load_rows(cfg, tab, sources, dst, base=0):
    w, hf, hd = cfg.width, cfg.half, cfg.heads
    for i in range(cfg.row_blocks):
        at = aligned(tab[0, i], cfg.span)
        for h in range(hd):
            dst[pl.ds(pl.multiple_of(at + h * hf, hf), hf), :] = sources[i // 4][(i % 4) * hf:(i % 4 + 1) * hf, (base + h) * w:(base + h + 1) * w]


def load_keys(cfg, tab, sources, ks, vs):
    w, hf = cfg.width, cfg.half
    per = cfg.slab_blocks
    for n, source in enumerate(sources):
        def step(j, _):
            to = pl.ds(aligned(tab[1, n * per + j], hf), hf)
            block = source[pl.ds(aligned(j, hf), hf), :]
            ks[to, :] = block[:, :w]
            vs[to, :] = block[:, w:]
            return 0

        lax.fori_loop(0, per, step, 0, unroll=4)


def unload_rows(cfg, tab, src, outs):
    w, hf, hd = cfg.width, cfg.half, cfg.heads
    for i in range(cfg.row_blocks):
        at = aligned(tab[0, i], cfg.span)
        for h in range(hd):
            outs[i // 4][(i % 4) * hf:(i % 4 + 1) * hf, h * w:(h + 1) * w] = src[pl.ds(pl.multiple_of(at + h * hf, hf), hf), :].astype(bf16)


def visible(cfg, tab, qpos_ref, c, r):
    hf, C, R = cfg.half, cfg.C, cfg.R
    per = C // hf
    step = lax.broadcasted_iota(i32, (hf, 128), 0)
    held = jnp.concatenate([step + tab[2, c * per + b] * hf for b in range(per)], axis=0)
    wide = jnp.concatenate([held] * (R // 128), axis=1)
    return wide <= qpos_ref[:, pl.ds(aligned(r, R), R)]


def each_tile(cfg, tab, nc, stages):
    def step(_, at):
        group = []
        for _ in range(cfg.G):
            r, c = at
            past = r >= cfg.nr
            group.append((jnp.where(past, 0, r), jnp.where(past, nc - 1, c)))
            end = c + 1 >= tab[3, jnp.where(past, 0, r)]
            at = (jnp.where(end, r + 1, r), jnp.where(end, 0, c + 1))
        held = [()] * cfg.G
        for stage in stages:
            held = [stage(*spot, *value) for spot, value in zip(group, held)]
        return at

    lax.fori_loop(0, lax.div(tab[3, 127] + (cfg.G - 1), cfg.G), step, (jnp.int32(0), jnp.int32(0)))


def work(cfg, n, products):
    pairs = cfg.rows * n * cfg.slab * 5 // 8
    return pl.CostEstimate(flops=4 * products * cfg.width * pairs, bytes_accessed=4 << 20, transcendentals=pairs)


def forward_body(cfg, n, first, last, *refs):
    refs = list(refs)
    take = lambda k: [refs.pop(0) for _ in range(k)]
    (tab, qpos), q, kv = take(2), take(4 if first else 2), take(n)
    before = [] if first else take(2)
    qs, dos = take(2) if first else q
    (stat_ref,) = take(1) if last else [None]
    ml, acc = take(2)
    ks, vs, vt = take(3)
    w, C, R = cfg.width, cfg.C, cfg.R
    keys = n * cfg.slab
    if first:
        load_rows(cfg, tab, q, qs)
        load_rows(cfg, tab, q, dos, cfg.heads)
    load_keys(cfg, tab, kv, ks, vs)
    for c in range(keys // 256):
        vt[:, c * 256:(c + 1) * 256] = vs[c * 256:(c + 1) * 256, :].T
    if first:
        ml[0:1, :] = jnp.full((1, cfg.rows), NONE, f32)
        ml[1:2, :] = jnp.zeros((1, cfg.rows), f32)
        acc[...] = jnp.zeros_like(acc)
    else:
        ml[...] = before[0][...]
        acc[...] = before[1][...]
    scale = math.log2(math.e) / math.sqrt(w)

    def scores(r, c):
        s = dot(ks[pl.ds(aligned(c, C), C), :], qs[pl.ds(aligned(r, R), R), :], NT)
        return (jnp.where(visible(cfg, tab, qpos, c, r), s, HIDE),)

    def weights(r, c, s):
        top = jnp.max(s, axis=0, keepdims=True) * scale
        p = jnp.exp2(s * scale - top)
        return top, jnp.sum(p, axis=0, keepdims=True), dot(vt[:, pl.ds(aligned(c, C), C)], p.astype(bf16))

    def absorb(r, c, top, total, mixed):
        here = pl.ds(aligned(r, R), R)
        old = ml[0:1, here]
        new = jnp.maximum(old, top)
        kept, added = jnp.exp2(old - new), jnp.exp2(top - new)
        ml[0:1, here] = new
        ml[1:2, here] = ml[1:2, here] * kept + total * added
        acc[:, here] = acc[:, here] * kept + mixed * added
        return ()

    each_tile(cfg, tab, keys // C, (scores, weights, absorb))
    if not last:
        return

    def settle(r, _):
        here = pl.ds(aligned(r, 256), 256)
        safe = jnp.maximum(ml[1:2, here], 1e-30)
        mixed = acc[:, here] * (1.0 / safe)
        acc[:, here] = mixed
        stat_ref[0:1, here] = ml[0:1, here] + jnp.log2(safe)
        stat_ref[1:2, here] = jnp.sum(mixed * dos[here, :].astype(f32).T, axis=0, keepdims=True)
        return 0

    lax.fori_loop(0, cfg.rows // 256, settle, 0, unroll=2)


def parts_body(cfg, tab, stat_ref, acc, *refs):
    outs, (os, ls) = refs[:4], refs[4:]
    w, hf, hd = cfg.width, cfg.half, cfg.heads

    def turn(r, _):
        here = pl.ds(aligned(r, 256), 256)
        os[here, :] = acc[:, here].T
        ls[here, :] = jnp.broadcast_to(stat_ref[0:1, here], (w, 256)).T
        return 0

    lax.fori_loop(0, cfg.rows // 256, turn, 0, unroll=2)
    unload_rows(cfg, tab, os, outs)
    lane = lax.broadcasted_iota(i32, (hf, w), 1)
    for i in range(cfg.row_blocks):
        at = aligned(tab[0, i], cfg.span)
        extra = jnp.zeros((hf, w), f32)
        for h in range(hd):
            rest = ls[pl.ds(pl.multiple_of(at + h * hf, hf), hf), :]
            for k in range(3):
                piece = rest.astype(bf16).astype(f32)
                extra = jnp.where(lane == 3 * h + k, piece, extra)
                rest = rest - piece
        outs[i // 4][(i % 4) * hf:(i % 4 + 1) * hf, hd * w:] = extra.astype(bf16)


def parts(cfg, tab, stat, acc):
    row = (cfg.rows, cfg.width)
    return pl.pallas_call(
        functools.partial(parts_body, cfg), out_shape=(jax.ShapeDtypeStruct((cfg.tokens, (cfg.heads + 1) * cfg.width), bf16),) * 4,
        in_specs=[SMEM, VMEM, VMEM], out_specs=(VMEM,) * 4, scratch_shapes=[pltpu.VMEM(row, f32)] * 2, name="parts",
        cost_estimate=pl.CostEstimate(flops=1 << 20, bytes_accessed=12 << 20, transcendentals=0),
    )(tab, stat, acc)


def forward(cfg, tab, qpos, q, kv, last, before=None):
    first, n, w = before is None, len(kv), cfg.width
    row, key = (cfg.rows, w), (n * cfg.slab, w)
    state = [jax.ShapeDtypeStruct((2, cfg.rows), f32), jax.ShapeDtypeStruct((w, cfg.rows), f32)]
    out = ([jax.ShapeDtypeStruct(row, bf16)] * 2 if first else []) + ([state[0]] if last else []) + state
    scratch = [pltpu.VMEM(key, bf16), pltpu.VMEM(key, bf16), pltpu.VMEM(key[::-1], bf16)]
    given = [tab, qpos, *q, *kv, *(before or ())]
    found = pl.pallas_call(
        functools.partial(forward_body, cfg, n, first, last), out_shape=tuple(out),
        in_specs=[SMEM] + [VMEM] * (len(given) - 1), out_specs=(VMEM,) * len(out), scratch_shapes=scratch,
        compiler_params=pltpu.CompilerParams(vmem_limit_bytes=LIMIT), name="attend", cost_estimate=work(cfg, n, 2),
    )(*given)
    return (found[0], found[2]) if last else found


def backward_body(cfg, n, first, last, *refs):
    refs = list(refs)
    take = lambda k: [refs.pop(0) for _ in range(k)]
    (tab, qpos, qs, dos), kv, stat = take(4), take(n), take(4 if first else 1)
    before = [] if first else take(1)
    parts_in = take(4) if last else []
    gq = take(4) if last else []
    (ld,) = take(1) if first else stat
    gqt = [] if last else take(1)
    gkv = take(n)
    ks, vs, kt, gks, gvs = take(5)
    gqt, gqs = (take(2) if last else (gqt[0], None))
    w, C, R, hf = cfg.width, cfg.C, cfg.R, cfg.half
    keys = n * cfg.slab
    load_keys(cfg, tab, kv, ks, vs)
    for c in range(keys // 256):
        kt[:, c * 256:(c + 1) * 256] = ks[c * 256:(c + 1) * 256, :].T
    gks[...] = jnp.zeros_like(gks)
    gvs[...] = jnp.zeros_like(gvs)
    gqt[...] = jnp.zeros_like(gqt) if first else before[0][...]
    if first:
        part = [s[0:1, :] for s in stat]
        top = functools.reduce(jnp.maximum, part)
        share = [jnp.exp2(v - top) for v in part]
        total = sum(share)
        ld[0:1, :] = top + jnp.log2(total)
        ld[1:2, :] = sum(v * s[1:2, :] for v, s in zip(share, stat)) / total
    scale = math.log2(math.e) / math.sqrt(w)

    def scores(r, c):
        at, here = pl.ds(aligned(c, C), C), pl.ds(aligned(r, R), R)
        s = dot(ks[at, :], qs[here, :], NT)
        gw = dot(vs[at, :], dos[here, :], NT)
        return jnp.where(visible(cfg, tab, qpos, c, r), s, HIDE), gw

    def weights(r, c, s, gw):
        here = pl.ds(aligned(r, R), R)
        p = jnp.exp2(s * scale - ld[0:1, here])
        return p.astype(bf16), (p * (gw - ld[1:2, here])).astype(bf16)

    def products(r, c, p, ds):
        at, here = pl.ds(aligned(c, C), C), pl.ds(aligned(r, R), R)
        return dot(p, dos[here, :]), dot(ds, qs[here, :]), dot(kt[:, at], ds)

    def absorb(r, c, gv, gk, gq):
        at, here = pl.ds(aligned(c, C), C), pl.ds(aligned(r, R), R)
        gvs[at, :] += gv
        gks[at, :] += gk
        gqt[:, here] += gq
        return ()

    each_tile(cfg, tab, keys // C, (scores, weights, products, absorb))
    if last:
        def turn(r, _):
            here = pl.ds(aligned(r, 256), 256)
            gqs[here, :] = gqt[:, here].T
            return 0

        lax.fori_loop(0, cfg.rows // 256, turn, 0, unroll=2)
        unload_rows(cfg, tab, gqs, gq)
        for part, out in zip(parts_in, gq):
            out[:, cfg.heads * w:] = part[...]
    for k, out in enumerate(gkv):
        def put(j, _):
            own = pl.ds(aligned(tab[1, k * cfg.slab_blocks + j], hf), hf)
            to = pl.ds(aligned(j, hf), hf)
            out[to, :w] = gks[own, :].astype(bf16)
            out[to, w:] = gvs[own, :].astype(bf16)
            return 0

        lax.fori_loop(0, cfg.slab_blocks, put, 0, unroll=4)


def backward(cfg, tab, qpos, q, kv, stat, before=None, parts=None):
    first, last, n, w = before is None, parts is not None, len(kv), cfg.width
    row, key = (cfg.rows, w), (n * cfg.slab, w)
    if last:
        out = [jax.ShapeDtypeStruct((cfg.tokens, (2 * cfg.heads + 1) * w), bf16)] * 4
    else:
        out = ([jax.ShapeDtypeStruct((2, cfg.rows), f32)] if first else []) + [jax.ShapeDtypeStruct(row[::-1], f32)]
    out += [jax.ShapeDtypeStruct((cfg.slab, 2 * w), bf16)] * n
    scratch = [pltpu.VMEM(key, bf16), pltpu.VMEM(key, bf16), pltpu.VMEM(key[::-1], bf16), pltpu.VMEM(key, f32), pltpu.VMEM(key, f32)]
    if last:
        scratch += [pltpu.VMEM(row[::-1], f32), pltpu.VMEM(row, f32)]
    given = [tab, qpos, *q, *kv, *stat] + ([] if first else [before]) + list(parts or ())
    found = pl.pallas_call(
        functools.partial(backward_body, cfg, n, first, last), out_shape=tuple(out),
        in_specs=[SMEM] + [VMEM] * (len(given) - 1), out_specs=(VMEM,) * len(out), scratch_shapes=scratch,
        compiler_params=pltpu.CompilerParams(vmem_limit_bytes=LIMIT), name="grads", cost_estimate=work(cfg, n, 5),
    )(*given)
    return (found[:4], found[4]) if last else found


def merge_body(cfg, *refs):
    parts, outs = refs[:4], refs[4:]
    w, hd, n = cfg.width, cfg.heads, cfg.tokens // 2
    scaling = w ** -0.5
    extra = [p[:, 2 * hd * w:].astype(f32) for p in parts]
    level = [e + pltpu.roll(e, w - 1, 1) + pltpu.roll(e, w - 2, 1) for e in extra]
    top = functools.reduce(jnp.maximum, level)
    share = [jnp.exp2(v - top) for v in level]
    total = 1.0 / sum(share)
    share = [v * total for v in share]
    for h in range(hd):
        at, behind = slice(h * w, (h + 1) * w), slice((hd + h) * w, (hd + h + 1) * w)
        mixed = sum(p[:, behind].astype(f32) * v[:, 3 * h:3 * h + 1] for p, v in zip(parts, share)).astype(bf16)
        outs[0][:, at] = mixed[:n]
        outs[1][:, at] = mixed[n:]
        summed = sum(p[:, at].astype(f32) for p in parts) * scaling
        outs[2][:, at] = summed[:n]
        outs[3][:, at] = summed[n:]


def merge(cfg, parts):
    out = [jax.ShapeDtypeStruct((cfg.tokens // 2, cfg.heads * cfg.width), t) for t in (bf16, bf16, f32, f32)]
    return pl.pallas_call(functools.partial(merge_body, cfg), out_shape=tuple(out), in_specs=[VMEM] * 4, out_specs=(VMEM,) * 4, name="merge",
                          cost_estimate=pl.CostEstimate(flops=1 << 20, bytes_accessed=8 << 20, transcendentals=0))(*parts)


def split_body(cfg, query, key, value, d_attended, *outs):
    w, wide = cfg.width, cfg.heads * cfg.width
    core = lax.axis_index("inner") & 1
    for k, (pair, rows) in enumerate((outs[:2], outs[2:])):
        at = core ^ k
        pair[:, :w] = key[at]
        pair[:, w:] = value[at]
        rows[:, :wide] = query[at]
        rows[:, wide:] = d_attended[at]


def split(cfg, query, key, value, d_attended):
    n = cfg.tokens // 2
    out = [jax.ShapeDtypeStruct((n, 2 * cfg.width), bf16), jax.ShapeDtypeStruct((n, 2 * cfg.heads * cfg.width), bf16)] * 2
    return pl.pallas_call(functools.partial(split_body, cfg), out_shape=tuple(out), in_specs=[VMEM] * 4, out_specs=(VMEM,) * 4,
                          name="split")(query, key, value, d_attended)


def add(parts):
    return functools.reduce(jnp.add, [p.astype(f32) for p in parts])


def along_x(parts):
    return [parts[0]] + [shift(parts[d], dx=d) for d in range(1, NX)]


def gather(b, rows, made):
    n = b.shape[0]
    plus, minus = shift(b, dz=-2), shift(b, dz=2)
    right, left = shift(rows, dx=-1), shift(rows, dx=1)
    plus, minus, right, left, made = lax.optimization_barrier((plus, minus, right, left, made))
    up = shift(jnp.concatenate([b, plus], axis=0), dz=-1)
    down = shift(jnp.concatenate([b, minus], axis=0), dz=1)
    far = shift(plus, dz=-2)
    facing = shift(rows, dx=2)
    slab = jnp.concatenate([b, up[:n], plus, up[n:], far, down[n:], minus, down[:n]], axis=0)
    slab, facing = lax.optimization_barrier((slab, facing))
    return slab, [rows, right, facing, left], made


def scatter(slab, gq, n):
    at = [slab[d * n:(d + 1) * n] for d in range(NZ)]
    low = [v.astype(bf16) for v in at]
    up = shift(jnp.concatenate([low[1], low[3]], axis=0), dz=1)
    down = shift(jnp.concatenate([low[7], low[5]], axis=0), dz=-1)
    gq = along_x(gq)
    up, down, gq = lax.optimization_barrier((up, down, gq))
    far = shift(low[4], dz=4)
    plus = shift((at[2] + up[n:]).astype(bf16), dz=2)
    minus = shift((at[6] + down[n:]).astype(bf16), dz=-2)
    return add([at[0], up[:n], down[:n], far, plus, minus]), gq


def on_device(query, key, value, d_attended, stretch_ids):
    width = key.shape[2]
    cfg = Cfg(query.shape[2] // width, key.shape[1] // 2, width)
    core = lax.axis_index("inner") & 1
    sets = ((0,), (1,), (2,), (3,), (1, 3))
    pair, rows, pair_given, rows_given = split(cfg, query, key, value, d_attended)
    pair = jnp.concatenate([pair, shift(pair_given, core=1)], axis=0)
    rows = jnp.concatenate([rows, shift(rows_given, core=1)], axis=0)
    pair, rows = lax.optimization_barrier((pair, rows))
    slab, q, (tabs, qpos) = gather(pair, rows, tables(cfg, sets, stretch_ids))
    tab_near, tab_after, tab_across, tab_before, tab_beside = tabs
    after, before = shift(slab, dy=-1), shift(slab, dy=1)
    half = slab.shape[0] // 2
    qs, dos, *state = forward(cfg, tab_near, qpos, q, [slab], False)
    q = (qs, dos)
    opposite = jnp.concatenate([shift(before[:half], dy=1), shift(after[half:], dy=-1)], axis=0)
    state = forward(cfg, tab_beside, qpos, q, [after, before], False, state)
    stat, acc = forward(cfg, tab_across, qpos, q, [opposite], True, state)
    sent = parts(cfg, tab_near, stat, acc)
    stats = [stat] + [shift(stat, dx=-d) for d in range(1, NX)]
    stats, sent = lax.optimization_barrier((stats, sent))
    stat, gqt, gkv_across = backward(cfg, tab_across, qpos, q, [opposite], stats)
    first, second = shift(gkv_across[:half], dy=1), shift(gkv_across[half:], dy=-1)
    gqt, gkv_after = backward(cfg, tab_after, qpos, q, [after], [stat], gqt)
    gqt, first, second = lax.optimization_barrier((gqt, first, second))
    gqt, gkv_before = backward(cfg, tab_before, qpos, q, [before], [stat], gqt)
    gkv_after = jnp.concatenate([add([gkv_after[:half], first]).astype(bf16), gkv_after[half:]], axis=0)
    gkv_before = jnp.concatenate([gkv_before[:half], add([gkv_before[half:], second]).astype(bf16)], axis=0)
    got = [shift(gkv_after, dy=1), shift(gkv_before, dy=-1)]
    gq, gkv_near = backward(cfg, tab_near, qpos, q, [slab], [stat], gqt, sent)
    n = cfg.tokens
    gkv = add([gkv_near] + got)
    gkv, gq = lax.optimization_barrier((gkv, gq))
    gkv, gq = scatter(gkv, gq, n)
    att, att_given, gq, gq_given = merge(cfg, gq)

    def settled(mine, given):
        other = shift(given, core=1)
        return jnp.where(core == 0, jnp.stack([mine, other]), jnp.stack([other, mine]))

    att = settled(att, att_given)
    gq = settled(gq, gq_given)
    gkv = settled(gkv[:n // 2], gkv[n // 2:])
    return att, gq, gkv[..., :width] * width ** -0.5, gkv[..., width:]


def solution(mesh):
    split = P(None, AXES, None)
    return jax.shard_map(on_device, mesh=mesh, in_specs=(split,) * 4 + (P(),), out_specs=(split,) * 4, check_vma=False)
```

time: 184 us -> 143 us (0.78)
  waiting for transfers between devices: 42.2 us -> 19.3 us
  starting transfers between devices: 66 us -> 50.8 us
  Pallas kernels: 66.3 us -> 62 us
  other arithmetic: 3.47 us -> 5.39 us
    ppermute x41 -> x32, waiting for transfers between devices: 42.2 us -> 19.3 us  [shift(): return lax.ppermute(a, AXES, pairs)]
    ppermute x41 -> x32, starting transfers between devices: 66 us -> 50.8 us  [shift(): return lax.ppermute(a, AXES, pairs)]
    pallas_call x4 -> x11, Pallas kernels: 66.3 us -> 62 us  [the longest x4 29.2 us: backward(): pl.pallas_call(functools.partial(backward_body, cfg, n, first, last), out...]
  transfers between devices with their start and end apart: 41 -> 32, of which waited for: 18 -> 10; matrix products, arithmetic and copies ran while one was open for 2% -> 2% of each run, Pallas kernels for 2% -> 27%
where the time goes in v2:
time: 143 us; the launch traced here: 142 us
  Pallas kernels  62 us (43%)
  starting transfers between devices  50.8 us (36%)
  waiting for transfers between devices  19.3 us (13%)
  other arithmetic  5.39 us (4%)
  local copies, waits for them, and re-layouts  3.67 us (3%)
    ppermute x32, starting transfers between devices, shift(): return lax.ppermute(a, AXES, pairs)  50.8 us
    pallas_call x4, Pallas kernels, backward(): pl.pallas_call(functools.partial(backward_body, cfg, n, first, last), out...  29.2 us
    pallas_call x3, Pallas kernels, forward(): pl.pallas_call(functools.partial(forward_body, cfg, n, first, last), out_...  22.9 us
    ppermute x32, waiting for transfers between devices, shift(): return lax.ppermute(a, AXES, pairs)  19.3 us
    unnamed x50, local copies, waits for them, and re-layouts  3.5 us
    pallas_call x1, Pallas kernels, parts(): pl.pallas_call(functools.partial(parts_body, cfg), out_shape=(jax.ShapeDt...  3.48 us
  transfers between devices with their start and end apart: 32, of which 10 were waited for; matrix products, arithmetic and copies ran while one was open for 2% of the time, Pallas kernels for 27%

profile of v2, /device:TPU:1, one launch (start us, length us, event | category | flops | bytes accessed | tf_op | source)
XLA Modules:
  0.0 142.2 jit_solution(9078264598311161556)
XLA Ops:
  2.4 3.2 %collective-permute-start.1 = (bf16[64,1280]{1,0:T(8,128)(2,1)}, bf16[64,1280]{1,0:T(8,128)(2,1)S(1)}, u32[]{:S(2)}, u32[]{:S(2)}) collective-permute-start(bf16[64,1280]{1,0:T(8,128)(2,1)} %get-tuple-element.81), channel_id=1, source_target_pairs={{0,1},{1,0},{2,3},{3,2},{4,5},{5,4},{6,7},{7,6},{8,9},{9,8},{10,11... | collective-permute-start | bytes 491528 | tf_op jit(solution)/shard_map/ppermute | solution.py:42
  10.4 5.3 %collective-permute-start.2 = (bf16[128,256]{1,0:T(8,128)(2,1)S(1)}, bf16[128,256]{1,0:T(8,128)(2,1)S(1)}, u32[]{:S(2)}, u32[]{:S(2)}) collective-permute-start(bf16[128,256]{1,0:T(8,128)(2,1)S(1)} %pad_maximum_fusion.7), channel_id=1, source_target_pairs={{0,12},{1,13},{2,14},{3,15},{4,0},{5,1},{6,2},{7,3},{8,4},{9,5},{1... | collective-permute-start | bytes 196616 | tf_op jit(solution)/shard_map/ppermute | solution.py:42
  15.7 1.9 %tables.1 = (s32[4,128]{1,0:T(4,128)}, s32[4,128]{1,0:T(4,128)}, s32[4,128]{1,0:T(4,128)}, s32[4,128]{1,0:T(4,128)}, s32[4,128]{1,0:T(4,128)}, /*index=5*/s32[1,2560]{1,0:T(1,128)}) custom-call(s32[256]{0:T(256)} %ids.1), custom_call_target="tpu_custom_call" | custom-call | tf_op jit(solution)/shard_map/tables/pallas_call | solution.py:91
  17.6 3.8 %collective-permute-done.3 = bf16[128,256]{1,0:T(8,128)(2,1)S(1)} collective-permute-done((bf16[128,256]{1,0:T(8,128)(2,1)S(1)}, bf16[128,256]{1,0:T(8,128)(2,1)S(1)}, u32[]{:S(2)}, u32[]{:S(2)}) %collective-permute-start.3) | collective-permute-done | bytes 65568 | tf_op jit(solution)/shard_map/ppermute | solution.py:42
  21.5 3.8 %collective-permute-start.6 = (bf16[256,256]{1,0:T(8,128)(2,1)S(1)}, bf16[256,256]{1,0:T(8,128)(2,1)S(1)}, u32[]{:S(2)}, u32[]{:S(2)}) collective-permute-start(bf16[256,256]{1,0:T(8,128)(2,1)S(1)} %get-tuple-element.166), channel_id=1, source_target_pairs={{0,14},{1,15},{2,0},{3,1},{4,2},{5,3},{6,4},{7,5},{8,6},{9,7},{10,... | collective-permute-start | bytes 393224 | tf_op jit(solution)/shard_map/ppermute | solution.py:42
  27.3 2.6 %collective-permute-done.7 = bf16[128,256]{1,0:T(8,128)(2,1)S(1)} collective-permute-done((bf16[128,256]{1,0:T(8,128)(2,1)S(1)}, bf16[128,256]{1,0:T(8,128)(2,1)S(1)}, u32[]{:S(2)}, u32[]{:S(2)}) %collective-permute-start.7) | collective-permute-done | bytes 65568 | tf_op jit(solution)/shard_map/ppermute | solution.py:42
  31.9 2.4 %collective-permute-done.9.refs_4_ = bf16[128,1280]{1,0:T(8,128)(2,1)S(1)} collective-permute-done((bf16[128,1280]{1,0:T(8,128)(2,1)S(1)}, bf16[128,1280]{1,0:T(8,128)(2,1)S(1)}, u32[]{:S(2)}, u32[]{:S(2)}) %collective-permute-start.9) | collective-permute-done | bytes 327712 | tf_op jit(solution)/shard_map/ppermute | solution.py:42
  37.1 6.1 %attend.3 = (bf16[2560,128]{1,0:T(8,128)(2,1)S(1)}, bf16[2560,128]{1,0:T(8,128)(2,1)S(1)}, f32[2,2560]{1,0:T(2,128)S(1)}, f32[128,2560]{1,0:T(8,128)S(1)}) custom-call(s32[4,128]{1,0:T(4,128)S(1)} %copy-done.4, s32[1,2560]{1,0:T(1,128)S(1)} %copy-done.10, bf16[128,1280]{1,0:T(8,128)(2,1)S(1)} %pad_maximum_fusion.2.refs_2_, ...), custom_call_target="tpu_custom_call" | custom-call | flops 1677721600 | bytes 4194304 | tf_op jit(solution)/shard_map/attend/pallas_call | solution.py:266
  43.2 3.3 %collective-permute-done.10.refs_5_.refs_4_ = bf16[1024,256]{1,0:T(8,128)(2,1)S(1)} collective-permute-done((bf16[1024,256]{1,0:T(8,128)(2,1)S(1)}, bf16[1024,256]{1,0:T(8,128)(2,1)S(1)}, u32[]{:S(2)}, u32[]{:S(2)}) %collective-permute-start.10) | collective-permute-done | bytes 524320 | tf_op jit(solution)/shard_map/ppermute | solution.py:42
  46.7 2.9 %collective-permute-start.13 = (bf16[512,256]{1,0:T(8,128)(2,1)S(1)}, bf16[512,256]{1,0:T(8,128)(2,1)S(1)}, u32[]{:S(2)}, u32[]{:S(2)}) collective-permute-start(bf16[512,256]{1,0:T(8,128)(2,1)S(1)} %slice.122), channel_id=1, source_target_pairs={{0,48},{1,49},{2,50},{3,51},{4,52},{5,53},{6,54},{7,55},{8,56},{9,... | collective-permute-start | bytes 786440 | tf_op jit(solution)/shard_map/ppermute | solution.py:42
  49.6 9.8 %attend.4 = (f32[2,2560]{1,0:T(2,128)S(1)}, f32[128,2560]{1,0:T(8,128)S(1)}) custom-call(s32[4,128]{1,0:T(4,128)S(1)} %copy-done.14, s32[1,2560]{1,0:T(1,128)S(1)} %copy-done.10, bf16[2560,128]{1,0:T(8,128)(2,1)S(1)} %get-tuple-element.98.refs_2_, bf16[2560,128]{1,0:T(8,128)(2,1)S(1)} %get-tuple-element.99.refs_3_, ...), custom_call_target="tpu_custom_call" | custom-call | flops 3355443200 | bytes 4194304 | tf_op jit(solution)/shard_map/attend/pallas_call | solution.py:266
  59.5 7.0 %attend.5 = (f32[2,2560]{1,0:T(2,128)S(1)}, f32[2,2560]{1,0:T(2,128)}, f32[128,2560]{1,0:T(8,128)S(1)}) custom-call(s32[4,128]{1,0:T(4,128)S(1)} %copy-done.13, s32[1,2560]{1,0:T(1,128)S(1)} %copy-done.10, bf16[2560,128]{1,0:T(8,128)(2,1)S(1)} %get-tuple-element.98.refs_2_, bf16[2560,128]{1,0:T(8,128)(2,1)S(1)} %get-tuple-element.99.refs_3_, ...), custom_call_target="tpu_custom_call" | custom-call | flops 1677721600 | bytes 4194304 | tf_op jit(solution)/shard_map/attend/pallas_call | solution.py:266
  69.1 3.5 %parts.1 = (bf16[128,768]{1,0:T(8,128)(2,1)}, bf16[128,768]{1,0:T(8,128)(2,1)}, bf16[128,768]{1,0:T(8,128)(2,1)}, bf16[128,768]{1,0:T(8,128)(2,1)}) custom-call(s32[4,128]{1,0:T(4,128)} %get-tuple-element.90.refs_0_.tab, f32[2,2560]{1,0:T(2,128)} %copy-done.2, f32[128,2560]{1,0:T(8,128)} %copy-done), custom_call_target="tpu_custom_call" | custom-call | flops 1048576 | bytes 12582912 | tf_op jit(solution)/shard_map/parts/pallas_call | solution.py:252
  74.7 7.1 %grads.4 = (f32[2,2560]{1,0:T(2,128)S(1)}, f32[128,2560]{1,0:T(8,128)S(1)}, bf16[1024,256]{1,0:T(8,128)(2,1)S(1)}) custom-call(s32[4,128]{1,0:T(4,128)S(1)} %copy-done.13, s32[1,2560]{1,0:T(1,128)S(1)} %copy-done.10, bf16[2560,128]{1,0:T(8,128)(2,1)S(1)} %get-tuple-element.98.refs_2_, bf16[2560,128]{1,0:T(8,128)(2,1)S(1)} %copy-done.16, ...), custom_call_target="tpu_custom_call" | custom-call | flops 4194304000 | bytes 4194304 | tf_op jit(solution)/shard_map/grads/pallas_call | solution.py:359
  82.0 2.7 %collective-permute-start.18 = (bf16[512,256]{1,0:T(8,128)(2,1)S(1)}, bf16[512,256]{1,0:T(8,128)(2,1)S(1)}, u32[]{:S(2)}, u32[]{:S(2)}) collective-permute-start(bf16[512,256]{1,0:T(8,128)(2,1)S(1)} %get-tuple-element.159), channel_id=1, source_target_pairs={{0,48},{1,49},{2,50},{3,51},{4,52},{5,53},{6,54},{7,55},{8,56},{9,... | collective-permute-start | bytes 786440 | tf_op jit(solution)/shard_map/ppermute | solution.py:42
  84.6 7.0 %grads.5 = (f32[128,2560]{1,0:T(8,128)S(1)}, bf16[1024,256]{1,0:T(8,128)(2,1)S(1)}) custom-call(s32[4,128]{1,0:T(4,128)S(1)} %copy-done.12, s32[1,2560]{1,0:T(1,128)S(1)} %copy-done.10, bf16[2560,128]{1,0:T(8,128)(2,1)S(1)} %get-tuple-element.98.refs_2_, bf16[2560,128]{1,0:T(8,128)(2,1)S(1)} %copy-done.16, ...), custom_call_target="tpu_custom_call" | custom-call | flops 4194304000 | bytes 4194304 | tf_op jit(solution)/shard_map/grads/pallas_call | solution.py:359
  91.7 7.0 %grads.6 = (f32[128,2560]{1,0:T(8,128)S(1)}, bf16[1024,256]{1,0:T(8,128)(2,1)S(1)}) custom-call(s32[4,128]{1,0:T(4,128)S(1)} %copy-done.11, s32[1,2560]{1,0:T(1,128)S(1)} %copy-done.10, bf16[2560,128]{1,0:T(8,128)(2,1)S(1)} %get-tuple-element.98.refs_2_, bf16[2560,128]{1,0:T(8,128)(2,1)S(1)} %copy-done.16, ...), custom_call_target="tpu_custom_call" | custom-call | flops 4194304000 | bytes 4194304 | tf_op jit(solution)/shard_map/grads/pallas_call | solution.py:359
  100.7 8.1 %grads.7 = (bf16[128,1408]{1,0:T(8,128)(2,1)S(1)}, bf16[128,1408]{1,0:T(8,128)(2,1)S(1)}, bf16[128,1408]{1,0:T(8,128)(2,1)S(1)}, bf16[128,1408]{1,0:T(8,128)(2,1)S(1)}, bf16[1024,256]{1,0:T(8,128)(2,1)S(1)}) custom-call(s32[4,128]{1,0:T(4,128)S(1)} %copy-done.5, s32[1,2560]{1,0:T(1,128)S(1)} %copy-done.10, bf16[2560,128]{1,0:T(8,128)(2,1)S(1)} %get-tuple-element.98.refs_2_, ...), custom_call_target="tpu_custom_call" | custom-call | flops 4194304000 | bytes 4194304 | tf_op jit(solution)/shard_map/grads/pallas_call | solution.py:359
  115.0 2.7 %collective-permute-start.22 = (bf16[256,256]{1,0:T(8,128)(2,1)S(1)}, bf16[256,256]{1,0:T(8,128)(2,1)S(1)}, u32[]{:S(2)}, u32[]{:S(2)}) collective-permute-start(bf16[256,256]{1,0:T(8,128)(2,1)S(1)} %pad_maximum_fusion.6), channel_id=1, source_target_pairs={{0,14},{1,15},{2,0},{3,1},{4,2},{5,3},{6,4},{7,5},{8,6},{9,7},{10,... | collective-permute-start | bytes 393224 | tf_op jit(solution)/shard_map/ppermute | solution.py:42
  117.8 2.3 %collective-permute-done.21 = bf16[256,256]{1,0:T(8,128)(2,1)S(1)} collective-permute-done((bf16[256,256]{1,0:T(8,128)(2,1)S(1)}, bf16[256,256]{1,0:T(8,128)(2,1)S(1)}, u32[]{:S(2)}, u32[]{:S(2)}) %collective-permute-start.21) | collective-permute-done | bytes 131104 | tf_op jit(solution)/shard_map/ppermute | solution.py:42
  120.0 2.0 %collective-permute-start.28 = (bf16[128,256]{1,0:T(8,128)(2,1)S(1)}, bf16[128,256]{1,0:T(8,128)(2,1)S(1)}, u32[]{:S(2)}, u32[]{:S(2)}) collective-permute-start(bf16[128,256]{1,0:T(8,128)(2,1)S(1)} %get-tuple-element.154), channel_id=1, source_target_pairs={{0,8},{1,9},{2,10},{3,11},{4,12},{5,13},{6,14},{7,15},{8,0},{9,1},... | collective-permute-start | bytes 196616 | tf_op jit(solution)/shard_map/ppermute | solution.py:42
  125.6 2.7 %merge.1 = (bf16[64,640]{1,0:T(8,128)(2,1)}, bf16[64,640]{1,0:T(8,128)(2,1)}, f32[64,640]{1,0:T(8,128)}, f32[64,640]{1,0:T(8,128)}) custom-call(bf16[128,1408]{1,0:T(8,128)(2,1)} %copy-done.1, bf16[128,1408]{1,0:T(8,128)(2,1)} %copy-done.17, bf16[128,1408]{1,0:T(8,128)(2,1)} %copy-done.18, bf16[128,1408]{1,0:T(8,128)(2,1)} %copy-done.19), custom_call_target="tpu_custom_call" | custom-call | flops 1048576 | bytes 8388608 | tf_op jit(solution)/shard_map/merge/pallas_call | solution.py:389
  128.3 8.5 %collective-permute-start.26 = (bf16[64,640]{1,0:T(8,128)(2,1)}, bf16[64,640]{1,0:T(8,128)(2,1)S(1)}, u32[]{:S(2)}, u32[]{:S(2)}) collective-permute-start(bf16[64,640]{1,0:T(8,128)(2,1)} %get-tuple-element.147), channel_id=1, source_target_pairs={{0,1},{1,0},{2,3},{3,2},{4,5},{5,4},{6,7},{7,6},{8,9},{9,8},{10,11... | collective-permute-start | bytes 245768 | tf_op jit(solution)/shard_map/ppermute | solution.py:42
  137.0 2.2 %collective-permute-start.31 = (f32[64,256]{1,0:T(8,128)S(1)}, f32[64,256]{1,0:T(8,128)S(1)}, u32[]{:S(2)}, u32[]{:S(2)}) collective-permute-start(f32[64,256]{1,0:T(8,128)S(1)} %get-tuple-element.164), channel_id=1, source_target_pairs={{0,1},{1,0},{2,3},{3,2},{4,5},{5,4},{6,7},{7,6},{8,9},{9,8},{10,11... | collective-permute-start | bytes 196616 | tf_op jit(solution)/shard_map/ppermute | solution.py:42
  (127 shorter events, 33.2 us)
Async XLA Ops:
  2.4 5.4 %collective-permute-start.1 = (bf16[64,1280]{1,0:T(8,128)(2,1)}, bf16[64,1280]{1,0:T(8,128)(2,1)S(1)}, u32[]{:S(2)}, u32[]{:S(2)}) collective-permute-start(bf16[64,1280]{1,0:T(8,128)(2,1)} %get-tuple-element.81), channel_id=1, source_target_pairs={{0,1},{1,0},{2,3},{3,2},{4,5},{5,4},{6,7},{7,6},{8,9},{9,8},{10,11... | collective-permute-start | bytes 491528 | tf_op jit(solution)/shard_map/ppermute | solution.py:42
  8.8 12.6 %collective-permute-start.4 = (bf16[128,1280]{1,0:T(8,128)(2,1)S(1)}, bf16[128,1280]{1,0:T(8,128)(2,1)S(1)}, u32[]{:S(2)}, u32[]{:S(2)}) collective-permute-start(bf16[128,1280]{1,0:T(8,128)(2,1)S(1)} %pad_maximum_fusion.2.refs_2_), channel_id=1, source_target_pairs={{0,192},{1,193},{2,194},{3,195},{4,196},{5,197},{6,198},{7,199},{8... | collective-permute-start | bytes 983048 | tf_op jit(solution)/shard_map/ppermute | solution.py:42
  9.6 11.8 %collective-permute-start.5 = (bf16[128,1280]{1,0:T(8,128)(2,1)S(1)}, bf16[128,1280]{1,0:T(8,128)(2,1)S(1)}, u32[]{:S(2)}, u32[]{:S(2)}) collective-permute-start(bf16[128,1280]{1,0:T(8,128)(2,1)S(1)} %pad_maximum_fusion.2.refs_2_), channel_id=1, source_target_pairs={{0,64},{1,65},{2,66},{3,67},{4,68},{5,69},{6,70},{7,71},{8,72},{9,... | collective-permute-start | bytes 983048 | tf_op jit(solution)/shard_map/ppermute | solution.py:42
  10.4 7.2 %collective-permute-start.2 = (bf16[128,256]{1,0:T(8,128)(2,1)S(1)}, bf16[128,256]{1,0:T(8,128)(2,1)S(1)}, u32[]{:S(2)}, u32[]{:S(2)}) collective-permute-start(bf16[128,256]{1,0:T(8,128)(2,1)S(1)} %pad_maximum_fusion.7), channel_id=1, source_target_pairs={{0,12},{1,13},{2,14},{3,15},{4,0},{5,1},{6,2},{7,3},{8,4},{9,5},{1... | collective-permute-start | bytes 196616 | tf_op jit(solution)/shard_map/ppermute | solution.py:42
  15.7 5.8 %collective-permute-start.3 = (bf16[128,256]{1,0:T(8,128)(2,1)S(1)}, bf16[128,256]{1,0:T(8,128)(2,1)S(1)}, u32[]{:S(2)}, u32[]{:S(2)}) collective-permute-start(bf16[128,256]{1,0:T(8,128)(2,1)S(1)} %pad_maximum_fusion.7), channel_id=1, source_target_pairs={{0,4},{1,5},{2,6},{3,7},{4,8},{5,9},{6,10},{7,11},{8,12},{9,13},{1... | collective-permute-start | bytes 196616 | tf_op jit(solution)/shard_map/ppermute | solution.py:42
  21.5 5.8 %collective-permute-start.6 = (bf16[256,256]{1,0:T(8,128)(2,1)S(1)}, bf16[256,256]{1,0:T(8,128)(2,1)S(1)}, u32[]{:S(2)}, u32[]{:S(2)}) collective-permute-start(bf16[256,256]{1,0:T(8,128)(2,1)S(1)} %get-tuple-element.166), channel_id=1, source_target_pairs={{0,14},{1,15},{2,0},{3,1},{4,2},{5,3},{6,4},{7,5},{8,6},{9,7},{10,... | collective-permute-start | bytes 393224 | tf_op jit(solution)/shard_map/ppermute | solution.py:42
  25.3 9.1 %collective-permute-start.9 = (bf16[128,1280]{1,0:T(8,128)(2,1)S(1)}, bf16[128,1280]{1,0:T(8,128)(2,1)S(1)}, u32[]{:S(2)}, u32[]{:S(2)}) collective-permute-start(bf16[128,1280]{1,0:T(8,128)(2,1)S(1)} %pad_maximum_fusion.2.refs_2_), channel_id=1, source_target_pairs={{0,128},{1,129},{2,130},{3,131},{4,132},{5,133},{6,134},{7,135},{8... | collective-permute-start | bytes 983048 | tf_op jit(solution)/shard_map/ppermute | solution.py:42
  26.5 5.3 %collective-permute-start.8 = (bf16[256,256]{1,0:T(8,128)(2,1)S(1)}, bf16[256,256]{1,0:T(8,128)(2,1)S(1)}, u32[]{:S(2)}, u32[]{:S(2)}) collective-permute-start(bf16[256,256]{1,0:T(8,128)(2,1)S(1)} %get-tuple-element.165), channel_id=1, source_target_pairs={{0,2},{1,3},{2,4},{3,5},{4,6},{5,7},{6,8},{7,9},{8,10},{9,11},{10,... | collective-permute-start | bytes 393224 | tf_op jit(solution)/shard_map/ppermute | solution.py:42
  34.3 12.2 %collective-permute-start.10 = (bf16[1024,256]{1,0:T(8,128)(2,1)S(1)}, bf16[1024,256]{1,0:T(8,128)(2,1)S(1)}, u32[]{:S(2)}, u32[]{:S(2)}) collective-permute-start(bf16[1024,256]{1,0:T(8,128)(2,1)S(1)} %slice_dynamic-update-slice_fusion.refs_6_.refs_4_), channel_id=1, source_target_pairs={{0,16},{1,17},{2,18},{3,19},{4,20},{5,21},{6,22},{7,23},{8,24},{9,... | collective-permute-start | bytes 1572872 | tf_op jit(solution)/shard_map/ppermute | solution.py:42
  35.6 11.0 %collective-permute-start.12 = (bf16[1024,256]{1,0:T(8,128)(2,1)S(1)}, bf16[1024,256]{1,0:T(8,128)(2,1)S(1)}, u32[]{:S(2)}, u32[]{:S(2)}) collective-permute-start(bf16[1024,256]{1,0:T(8,128)(2,1)S(1)} %slice_dynamic-update-slice_fusion.refs_6_.refs_4_), channel_id=1, source_target_pairs={{0,48},{1,49},{2,50},{3,51},{4,52},{5,53},{6,54},{7,55},{8,56},{9,... | collective-permute-start | bytes 1572872 | tf_op jit(solution)/shard_map/ppermute | solution.py:42
  46.5 12.8 %collective-permute-start.11 = (bf16[512,256]{1,0:T(8,128)(2,1)S(1)}, bf16[512,256]{1,0:T(8,128)(2,1)S(1)}, u32[]{:S(2)}, u32[]{:S(2)}) collective-permute-start(bf16[512,256]{1,0:T(8,128)(2,1)S(1)} %slice.121), channel_id=1, source_target_pairs={{0,16},{1,17},{2,18},{3,19},{4,20},{5,21},{6,22},{7,23},{8,24},{9,... | collective-permute-start | bytes 786440 | tf_op jit(solution)/shard_map/ppermute | solution.py:42
  46.7 12.7 %collective-permute-start.13 = (bf16[512,256]{1,0:T(8,128)(2,1)S(1)}, bf16[512,256]{1,0:T(8,128)(2,1)S(1)}, u32[]{:S(2)}, u32[]{:S(2)}) collective-permute-start(bf16[512,256]{1,0:T(8,128)(2,1)S(1)} %slice.122), channel_id=1, source_target_pairs={{0,48},{1,49},{2,50},{3,51},{4,52},{5,53},{6,54},{7,55},{8,56},{9,... | collective-permute-start | bytes 786440 | tf_op jit(solution)/shard_map/ppermute | solution.py:42
  81.9 9.8 %collective-permute-start.17 = (bf16[512,256]{1,0:T(8,128)(2,1)S(1)}, bf16[512,256]{1,0:T(8,128)(2,1)S(1)}, u32[]{:S(2)}, u32[]{:S(2)}) collective-permute-start(bf16[512,256]{1,0:T(8,128)(2,1)S(1)} %get-tuple-element.160), channel_id=1, source_target_pairs={{0,16},{1,17},{2,18},{3,19},{4,20},{5,21},{6,22},{7,23},{8,24},{9,... | collective-permute-start | bytes 786440 | tf_op jit(solution)/shard_map/ppermute | solution.py:42
  82.0 9.7 %collective-permute-start.18 = (bf16[512,256]{1,0:T(8,128)(2,1)S(1)}, bf16[512,256]{1,0:T(8,128)(2,1)S(1)}, u32[]{:S(2)}, u32[]{:S(2)}) collective-permute-start(bf16[512,256]{1,0:T(8,128)(2,1)S(1)} %get-tuple-element.159), channel_id=1, source_target_pairs={{0,48},{1,49},{2,50},{3,51},{4,52},{5,53},{6,54},{7,55},{8,56},{9,... | collective-permute-start | bytes 786440 | tf_op jit(solution)/shard_map/ppermute | solution.py:42
  99.0 9.8 %collective-permute-start.20 = (bf16[1024,256]{1,0:T(8,128)(2,1)S(1)}, bf16[1024,256]{1,0:T(8,128)(2,1)S(1)}, u32[]{:S(2)}, u32[]{:S(2)}) collective-permute-start(bf16[1024,256]{1,0:T(8,128)(2,1)S(1)} %pad_maximum_fusion.1), channel_id=1, source_target_pairs={{0,48},{1,49},{2,50},{3,51},{4,52},{5,53},{6,54},{7,55},{8,56},{9,... | collective-permute-start | bytes 1572872 | tf_op jit(solution)/shard_map/ppermute | solution.py:42
  99.2 9.6 %collective-permute-start.19 = (bf16[1024,256]{1,0:T(8,128)(2,1)S(1)}, bf16[1024,256]{1,0:T(8,128)(2,1)S(1)}, u32[]{:S(2)}, u32[]{:S(2)}) collective-permute-start(bf16[1024,256]{1,0:T(8,128)(2,1)S(1)} %pad_maximum_fusion), channel_id=1, source_target_pairs={{0,16},{1,17},{2,18},{3,19},{4,20},{5,21},{6,22},{7,23},{8,24},{9,... | collective-permute-start | bytes 1572872 | tf_op jit(solution)/shard_map/ppermute | solution.py:42
  109.6 12.4 %collective-permute-start.23 = (bf16[128,1408]{1,0:T(8,128)(2,1)S(1)}, bf16[128,1408]{1,0:T(8,128)(2,1)S(1)}, u32[]{:S(2)}, u32[]{:S(2)}) collective-permute-start(bf16[128,1408]{1,0:T(8,128)(2,1)S(1)} %get-tuple-element.139), channel_id=1, source_target_pairs={{0,64},{1,65},{2,66},{3,67},{4,68},{5,69},{6,70},{7,71},{8,72},{9,... | collective-permute-start | bytes 1081352 | tf_op jit(solution)/shard_map/ppermute | solution.py:42
  111.5 11.7 %collective-permute-start.24 = (bf16[128,1408]{1,0:T(8,128)(2,1)S(1)}, bf16[128,1408]{1,0:T(8,128)(2,1)S(1)}, u32[]{:S(2)}, u32[]{:S(2)}) collective-permute-start(bf16[128,1408]{1,0:T(8,128)(2,1)S(1)} %get-tuple-element.140), channel_id=1, source_target_pairs={{0,128},{1,129},{2,130},{3,131},{4,132},{5,133},{6,134},{7,135},{8... | collective-permute-start | bytes 1081352 | tf_op jit(solution)/shard_map/ppermute | solution.py:42
  113.2 9.9 %collective-permute-start.25 = (bf16[128,1408]{1,0:T(8,128)(2,1)S(1)}, bf16[128,1408]{1,0:T(8,128)(2,1)S(1)}, u32[]{:S(2)}, u32[]{:S(2)}) collective-permute-start(bf16[128,1408]{1,0:T(8,128)(2,1)S(1)} %get-tuple-element.141), channel_id=1, source_target_pairs={{0,192},{1,193},{2,194},{3,195},{4,196},{5,197},{6,198},{7,199},{8... | collective-permute-start | bytes 1081352 | tf_op jit(solution)/shard_map/ppermute | solution.py:42
  115.0 7.0 %collective-permute-start.22 = (bf16[256,256]{1,0:T(8,128)(2,1)S(1)}, bf16[256,256]{1,0:T(8,128)(2,1)S(1)}, u32[]{:S(2)}, u32[]{:S(2)}) collective-permute-start(bf16[256,256]{1,0:T(8,128)(2,1)S(1)} %pad_maximum_fusion.6), channel_id=1, source_target_pairs={{0,14},{1,15},{2,0},{3,1},{4,2},{5,3},{6,4},{7,5},{8,6},{9,7},{10,... | collective-permute-start | bytes 393224 | tf_op jit(solution)/shard_map/ppermute | solution.py:42
  120.0 16.8 %collective-permute-start.28 = (bf16[128,256]{1,0:T(8,128)(2,1)S(1)}, bf16[128,256]{1,0:T(8,128)(2,1)S(1)}, u32[]{:S(2)}, u32[]{:S(2)}) collective-permute-start(bf16[128,256]{1,0:T(8,128)(2,1)S(1)} %get-tuple-element.154), channel_id=1, source_target_pairs={{0,8},{1,9},{2,10},{3,11},{4,12},{5,13},{6,14},{7,15},{8,0},{9,1},... | collective-permute-start | bytes 196616 | tf_op jit(solution)/shard_map/ppermute | solution.py:42
  123.2 13.7 %collective-permute-start.30 = (bf16[128,256]{1,0:T(8,128)(2,1)S(1)}, bf16[128,256]{1,0:T(8,128)(2,1)S(1)}, u32[]{:S(2)}, u32[]{:S(2)}) collective-permute-start(bf16[128,256]{1,0:T(8,128)(2,1)S(1)} %get-tuple-element.153), channel_id=1, source_target_pairs={{0,12},{1,13},{2,14},{3,15},{4,0},{5,1},{6,2},{7,3},{8,4},{9,5},{1... | collective-permute-start | bytes 196616 | tf_op jit(solution)/shard_map/ppermute | solution.py:42
  124.5 12.4 %collective-permute-start.29 = (bf16[128,256]{1,0:T(8,128)(2,1)S(1)}, bf16[128,256]{1,0:T(8,128)(2,1)S(1)}, u32[]{:S(2)}, u32[]{:S(2)}) collective-permute-start(bf16[128,256]{1,0:T(8,128)(2,1)S(1)} %get-tuple-element.152), channel_id=1, source_target_pairs={{0,4},{1,5},{2,6},{3,7},{4,8},{5,9},{6,10},{7,11},{8,12},{9,13},{1... | collective-permute-start | bytes 196616 | tf_op jit(solution)/shard_map/ppermute | solution.py:42
  128.3 10.8 %collective-permute-start.26 = (bf16[64,640]{1,0:T(8,128)(2,1)}, bf16[64,640]{1,0:T(8,128)(2,1)S(1)}, u32[]{:S(2)}, u32[]{:S(2)}) collective-permute-start(bf16[64,640]{1,0:T(8,128)(2,1)} %get-tuple-element.147), channel_id=1, source_target_pairs={{0,1},{1,0},{2,3},{3,2},{4,5},{5,4},{6,7},{7,6},{8,9},{9,8},{10,11... | collective-permute-start | bytes 245768 | tf_op jit(solution)/shard_map/ppermute | solution.py:42
  (29 other events, 168.5 us)

commit v3 on v2

--- a/solution.py
+++ b/solution.py
@@ -23,8 +23,8 @@
 
 
 class Cfg:
-    def __init__(s, heads, half, width, C=256, R=256, G=4):
-        s.heads, s.half, s.width, s.C, s.R, s.G = heads, half, width, C, R, G
+    def __init__(s, heads, half, width, C=256, R=256):
+        s.heads, s.half, s.width, s.C, s.R = heads, half, width, C, R
         s.tokens = 4 * half
         s.span = half * heads
         s.row_blocks, s.slab_blocks = 4 * NX, 4 * NZ
@@ -92,6 +92,7 @@
         functools.partial(tables_body, cfg, sets, ids.shape[0]),
         out_shape=(jax.ShapeDtypeStruct((4, 128), i32),) * len(sets) + (jax.ShapeDtypeStruct((1, cfg.rows), i32),),
         in_specs=[SMEM], out_specs=(VMEM,) * (len(sets) + 1), name="tables",
+        compiler_params=pltpu.CompilerParams(vmem_limit_bytes=4 * 2**20),
     )(ids)
     return found[:-1], found[-1]
 
@@ -108,8 +109,11 @@
             dst[pl.ds(pl.multiple_of(at + h * hf, hf), hf), :] = sources[i // 4][(i % 4) * hf:(i % 4 + 1) * hf, (base + h) * w:(base + h + 1) * w]
 
 
-def load_keys(cfg, tab, sources, ks, vs):
+def load_keys(cfg, tab, sources, ks, vs, kpos):
     w, hf = cfg.width, cfg.half
+    offset = lax.broadcasted_iota(i32, (hf, 128), 0)
+    for j in range(ks.shape[0] // hf):
+        kpos[j * hf:(j + 1) * hf, :] = offset + tab[2, j] * hf
     per = cfg.slab_blocks
     for n, source in enumerate(sources):
         def step(j, _):
@@ -130,30 +134,27 @@
             outs[i // 4][(i % 4) * hf:(i % 4 + 1) * hf, h * w:(h + 1) * w] = src[pl.ds(pl.multiple_of(at + h * hf, hf), hf), :].astype(bf16)
 
 
-def visible(cfg, tab, qpos_ref, c, r):
-    hf, C, R = cfg.half, cfg.C, cfg.R
-    per = C // hf
-    step = lax.broadcasted_iota(i32, (hf, 128), 0)
-    held = jnp.concatenate([step + tab[2, c * per + b] * hf for b in range(per)], axis=0)
-    wide = jnp.concatenate([held] * (R // 128), axis=1)
+def visible(cfg, kpos, qpos_ref, c, r):
+    C, R = cfg.C, cfg.R
+    wide = jnp.concatenate([kpos[pl.ds(aligned(c, C), C), :]] * (R // 128), axis=1)
     return wide <= qpos_ref[:, pl.ds(aligned(r, R), R)]
 
 
-def each_tile(cfg, tab, nc, stages):
+def each_tile(cfg, tab, nc, count, stages):
     def step(_, at):
         group = []
-        for _ in range(cfg.G):
+        for _ in range(count):
             r, c = at
             past = r >= cfg.nr
             group.append((jnp.where(past, 0, r), jnp.where(past, nc - 1, c)))
             end = c + 1 >= tab[3, jnp.where(past, 0, r)]
             at = (jnp.where(end, r + 1, r), jnp.where(end, 0, c + 1))
-        held = [()] * cfg.G
+        held = [()] * count
         for stage in stages:
             held = [stage(*spot, *value) for spot, value in zip(group, held)]
         return at
 
-    lax.fori_loop(0, lax.div(tab[3, 127] + (cfg.G - 1), cfg.G), step, (jnp.int32(0), jnp.int32(0)))
+    lax.fori_loop(0, lax.div(tab[3, 127] + (count - 1), count), step, (jnp.int32(0), jnp.int32(0)))
 
 
 def work(cfg, n, products):
@@ -169,13 +170,13 @@
     qs, dos = take(2) if first else q
     (stat_ref,) = take(1) if last else [None]
     ml, acc = take(2)
-    ks, vs, vt = take(3)
+    ks, vs, vt, kpos = take(4)
     w, C, R = cfg.width, cfg.C, cfg.R
     keys = n * cfg.slab
     if first:
         load_rows(cfg, tab, q, qs)
         load_rows(cfg, tab, q, dos, cfg.heads)
-    load_keys(cfg, tab, kv, ks, vs)
+    load_keys(cfg, tab, kv, ks, vs, kpos)
     for c in range(keys // 256):
         vt[:, c * 256:(c + 1) * 256] = vs[c * 256:(c + 1) * 256, :].T
     if first:
@@ -189,7 +190,7 @@
 
     def scores(r, c):
         s = dot(ks[pl.ds(aligned(c, C), C), :], qs[pl.ds(aligned(r, R), R), :], NT)
-        return (jnp.where(visible(cfg, tab, qpos, c, r), s, HIDE),)
+        return (jnp.where(visible(cfg, kpos, qpos, c, r), s, HIDE),)
 
     def weights(r, c, s):
         top = jnp.max(s, axis=0, keepdims=True) * scale
@@ -206,7 +207,7 @@
         acc[:, here] = acc[:, here] * kept + mixed * added
         return ()
 
-    each_tile(cfg, tab, keys // C, (scores, weights, absorb))
+    each_tile(cfg, tab, keys // C, 8, (scores, weights, absorb))
     if not last:
         return
 
@@ -252,6 +253,7 @@
     return pl.pallas_call(
         functools.partial(parts_body, cfg), out_shape=(jax.ShapeDtypeStruct((cfg.tokens, (cfg.heads + 1) * cfg.width), bf16),) * 4,
         in_specs=[SMEM, VMEM, VMEM], out_specs=(VMEM,) * 4, scratch_shapes=[pltpu.VMEM(row, f32)] * 2, name="parts",
+        compiler_params=pltpu.CompilerParams(vmem_limit_bytes=12 * 2**20),
         cost_estimate=pl.CostEstimate(flops=1 << 20, bytes_accessed=12 << 20, transcendentals=0),
     )(tab, stat, acc)
 
@@ -261,7 +263,7 @@
     row, key = (cfg.rows, w), (n * cfg.slab, w)
     state = [jax.ShapeDtypeStruct((2, cfg.rows), f32), jax.ShapeDtypeStruct((w, cfg.rows), f32)]
     out = ([jax.ShapeDtypeStruct(row, bf16)] * 2 if first else []) + ([state[0]] if last else []) + state
-    scratch = [pltpu.VMEM(key, bf16), pltpu.VMEM(key, bf16), pltpu.VMEM(key[::-1], bf16)]
+    scratch = [pltpu.VMEM(key, bf16), pltpu.VMEM(key, bf16), pltpu.VMEM(key[::-1], bf16), pltpu.VMEM((key[0], 128), i32)]
     given = [tab, qpos, *q, *kv, *(before or ())]
     found = pl.pallas_call(
         functools.partial(forward_body, cfg, n, first, last), out_shape=tuple(out),
@@ -281,11 +283,11 @@
     (ld,) = take(1) if first else stat
     gqt = [] if last else take(1)
     gkv = take(n)
-    ks, vs, kt, gks, gvs = take(5)
+    ks, vs, kt, gks, gvs, kpos = take(6)
     gqt, gqs = (take(2) if last else (gqt[0], None))
     w, C, R, hf = cfg.width, cfg.C, cfg.R, cfg.half
     keys = n * cfg.slab
-    load_keys(cfg, tab, kv, ks, vs)
+    load_keys(cfg, tab, kv, ks, vs, kpos)
     for c in range(keys // 256):
         kt[:, c * 256:(c + 1) * 256] = ks[c * 256:(c + 1) * 256, :].T
     gks[...] = jnp.zeros_like(gks)
@@ -304,7 +306,7 @@
         at, here = pl.ds(aligned(c, C), C), pl.ds(aligned(r, R), R)
         s = dot(ks[at, :], qs[here, :], NT)
         gw = dot(vs[at, :], dos[here, :], NT)
-        return jnp.where(visible(cfg, tab, qpos, c, r), s, HIDE), gw
+        return jnp.where(visible(cfg, kpos, qpos, c, r), s, HIDE), gw
 
     def weights(r, c, s, gw):
         here = pl.ds(aligned(r, R), R)
@@ -322,7 +324,7 @@
         gqt[:, here] += gq
         return ()
 
-    each_tile(cfg, tab, keys // C, (scores, weights, products, absorb))
+    each_tile(cfg, tab, keys // C, 4, (scores, weights, products, absorb))
     if last:
         def turn(r, _):
             here = pl.ds(aligned(r, 256), 256)
@@ -352,7 +354,8 @@
     else:
         out = ([jax.ShapeDtypeStruct((2, cfg.rows), f32)] if first else []) + [jax.ShapeDtypeStruct(row[::-1], f32)]
     out += [jax.ShapeDtypeStruct((cfg.slab, 2 * w), bf16)] * n
-    scratch = [pltpu.VMEM(key, bf16), pltpu.VMEM(key, bf16), pltpu.VMEM(key[::-1], bf16), pltpu.VMEM(key, f32), pltpu.VMEM(key, f32)]
+    scratch = [pltpu.VMEM(key, bf16), pltpu.VMEM(key, bf16), pltpu.VMEM(key[::-1], bf16), pltpu.VMEM(key, f32), pltpu.VMEM(key, f32),
+               pltpu.VMEM((key[0], 128), i32)]
     if last:
         scratch += [pltpu.VMEM(row[::-1], f32), pltpu.VMEM(row, f32)]
     given = [tab, qpos, *q, *kv, *stat] + ([] if first else [before]) + list(parts or ())
@@ -387,6 +390,7 @@
 def merge(cfg, parts):
     out = [jax.ShapeDtypeStruct((cfg.tokens // 2, cfg.heads * cfg.width), t) for t in (bf16, bf16, f32, f32)]
     return pl.pallas_call(functools.partial(merge_body, cfg), out_shape=tuple(out), in_specs=[VMEM] * 4, out_specs=(VMEM,) * 4, name="merge",
+                          compiler_params=pltpu.CompilerParams(vmem_limit_bytes=8 * 2**20),
                           cost_estimate=pl.CostEstimate(flops=1 << 20, bytes_accessed=8 << 20, transcendentals=0))(*parts)
 
 
@@ -405,7 +409,7 @@
     n = cfg.tokens // 2
     out = [jax.ShapeDtypeStruct((n, 2 * cfg.width), bf16), jax.ShapeDtypeStruct((n, 2 * cfg.heads * cfg.width), bf16)] * 2
     return pl.pallas_call(functools.partial(split_body, cfg), out_shape=tuple(out), in_specs=[VMEM] * 4, out_specs=(VMEM,) * 4,
-                          name="split")(query, key, value, d_attended)
+                          compiler_params=pltpu.CompilerParams(vmem_limit_bytes=4 * 2**20), name="split")(query, key, value, d_attended)
 
 
 def add(parts):
@@ -443,10 +447,28 @@
     return add([at[0], up[:n], down[:n], far, plus, minus]), gq
 
 
+def settle_body(core_axis, *refs):
+    att, gq, gkv, att_got, gq_got, gkv_got, out, out_q, out_k, out_v = refs
+    core = lax.axis_index(core_axis) & 1
+    w = out_k.shape[2]
+    for at, sources in ((core, (att, gq, gkv)), (1 - core, (att_got, gq_got, gkv_got))):
+        out[at] = sources[0][...]
+        out_q[at] = sources[1][...]
+        out_k[at] = sources[2][:, :w] * w ** -0.5
+        out_v[at] = sources[2][:, w:]
+
+
+def settle(cfg, mine, got):
+    n, w = cfg.tokens // 2, cfg.width
+    out = [jax.ShapeDtypeStruct((2, n, cfg.heads * w), bf16), jax.ShapeDtypeStruct((2, n, cfg.heads * w), f32)]
+    out += [jax.ShapeDtypeStruct((2, n, w), f32)] * 2
+    return pl.pallas_call(functools.partial(settle_body, "inner"), out_shape=tuple(out), in_specs=[VMEM] * 6, out_specs=(VMEM,) * 4,
+                          compiler_params=pltpu.CompilerParams(vmem_limit_bytes=4 * 2**20), name="settle")(*mine, *got)
+
+
 def on_device(query, key, value, d_attended, stretch_ids):
     width = key.shape[2]
     cfg = Cfg(query.shape[2] // width, key.shape[1] // 2, width)
-    core = lax.axis_index("inner") & 1
     sets = ((0,), (1,), (2,), (3,), (1, 3))
     pair, rows, pair_given, rows_given = split(cfg, query, key, value, d_attended)
     pair = jnp.concatenate([pair, shift(pair_given, core=1)], axis=0)
@@ -479,14 +501,8 @@
     gkv, gq = scatter(gkv, gq, n)
     att, att_given, gq, gq_given = merge(cfg, gq)
 
-    def settled(mine, given):
-        other = shift(given, core=1)
-        return jnp.where(core == 0, jnp.stack([mine, other]), jnp.stack([other, mine]))
-
-    att = settled(att, att_given)
-    gq = settled(gq, gq_given)
-    gkv = settled(gkv[:n // 2], gkv[n // 2:])
-    return att, gq, gkv[..., :width] * width ** -0.5, gkv[..., width:]
+    given = [shift(v, core=1) for v in (att_given, gq_given, gkv[n // 2:])]
+    return settle(cfg, [att, gq, gkv[:n // 2]], given)
 
 
 def solution(mesh):

time: 143 us -> 134 us (0.937)
  Pallas kernels: 62 us -> 54.4 us
  starting transfers between devices: 50.8 us -> 55.9 us
  other arithmetic: 5.39 us -> 0.66 us
  waiting for transfers between devices: 19.3 us -> 17.4 us
    ppermute x32, starting transfers between devices: 50.8 us -> 55.9 us  [shift(): return lax.ppermute(a, AXES, pairs)]
    select_n x3 -> x0, other arithmetic: 2.42 us -> none  [settled(): jnp.where(core == 0, jnp.stack([mine, other]), jnp.stack([other, mine]))]
    pallas_call x1, Pallas kernels: 2.66 us -> 0.65 us  [merge(): pl.pallas_call(functools.partial(merge_body, cfg), out_shape=tuple(out),...]
    ppermute x32, waiting for transfers between devices: 19.3 us -> 17.4 us  [shift(): return lax.ppermute(a, AXES, pairs)]
    pallas_call x1, Pallas kernels: 1.81 us -> 0.04 us  [split(): pl.pallas_call(functools.partial(split_body, cfg), out_shape=tuple(out),...]
    pallas_call x3, Pallas kernels: 22.9 us -> 21.3 us  [forward(): pl.pallas_call(functools.partial(forward_body, cfg, n, first, last), out_...]
    pallas_call x1, Pallas kernels: 3.48 us -> 2.04 us  [parts(): pl.pallas_call(functools.partial(parts_body, cfg), out_shape=(jax.ShapeDt...]
    unnamed x50 -> x18, local copies, waits for them, and re-layouts: 3.5 us -> 4.08 us
  transfers between devices with their start and end apart: 32 -> 32, of which waited for: 10 -> 10; matrix products, arithmetic and copies ran while one was open for 2% -> 0% of each run, Pallas kernels for 27% -> 25%
where the time goes in v3:
time: 134 us
  starting transfers between devices  55.9 us (42%)
  Pallas kernels  54.4 us (41%)
  waiting for transfers between devices  17.4 us (13%)
  local copies, waits for them, and re-layouts  4.25 us (3%)
    ppermute x32, starting transfers between devices, shift(): return lax.ppermute(a, AXES, pairs)  55.9 us
    pallas_call x4, Pallas kernels, backward(): pl.pallas_call(functools.partial(backward_body, cfg, n, first, last), out...  28.2 us
    pallas_call x3, Pallas kernels, forward(): pl.pallas_call(functools.partial(forward_body, cfg, n, first, last), out_...  21.3 us
    ppermute x32, waiting for transfers between devices, shift(): return lax.ppermute(a, AXES, pairs)  17.4 us
    unnamed x18, local copies, waits for them, and re-layouts  4.08 us
  transfers between devices with their start and end apart: 32, of which 10 were waited for; matrix products, arithmetic and copies ran while one was open for 0% of the time, Pallas kernels for 25%

profile of v3, /device:TPU:1, one launch (start us, length us, event | category | flops | bytes accessed | tf_op | source)
XLA Modules:
  0.0 133.6 jit_solution(5005290572599733471)
XLA Ops:
  4.0 3.3 %collective-permute-start.1 = (bf16[64,1280]{1,0:T(8,128)(2,1)S(1)}, bf16[64,1280]{1,0:T(8,128)(2,1)S(1)}, u32[]{:S(2)}, u32[]{:S(2)}) collective-permute-start(bf16[64,1280]{1,0:T(8,128)(2,1)S(1)} %get-tuple-element.81), channel_id=1, source_target_pairs={{0,1},{1,0},{2,3},{3,2},{4,5},{5,4},{6,7},{7,6},{8,9},{9,8},{10,11... | collective-permute-start | bytes 491528 | tf_op jit(solution)/shard_map/ppermute | solution.py:42
  8.7 2.7 %collective-permute-start.4 = (bf16[128,1280]{1,0:T(8,128)(2,1)S(1)}, bf16[128,1280]{1,0:T(8,128)(2,1)S(1)}, u32[]{:S(2)}, u32[]{:S(2)}) collective-permute-start(bf16[128,1280]{1,0:T(8,128)(2,1)S(1)} %pad_maximum_fusion.2.refs_2_), channel_id=1, source_target_pairs={{0,192},{1,193},{2,194},{3,195},{4,196},{5,197},{6,198},{7,199},{8... | collective-permute-start | bytes 983048 | tf_op jit(solution)/shard_map/ppermute | solution.py:42
  12.6 3.0 %collective-permute-start.2 = (bf16[128,256]{1,0:T(8,128)(2,1)S(1)}, bf16[128,256]{1,0:T(8,128)(2,1)S(1)}, u32[]{:S(2)}, u32[]{:S(2)}) collective-permute-start(bf16[128,256]{1,0:T(8,128)(2,1)S(1)} %pad_maximum_fusion.7), channel_id=1, source_target_pairs={{0,12},{1,13},{2,14},{3,15},{4,0},{5,1},{6,2},{7,3},{8,4},{9,5},{1... | collective-permute-start | bytes 196616 | tf_op jit(solution)/shard_map/ppermute | solution.py:42
  19.6 3.3 %collective-permute-start.6 = (bf16[256,256]{1,0:T(8,128)(2,1)S(1)}, bf16[256,256]{1,0:T(8,128)(2,1)S(1)}, u32[]{:S(2)}, u32[]{:S(2)}) collective-permute-start(bf16[256,256]{1,0:T(8,128)(2,1)S(1)} %get-tuple-element.164), channel_id=1, source_target_pairs={{0,14},{1,15},{2,0},{3,1},{4,2},{5,3},{6,4},{7,5},{8,6},{9,7},{10,... | collective-permute-start | bytes 393224 | tf_op jit(solution)/shard_map/ppermute | solution.py:42
  27.0 2.4 %collective-permute-done.7 = bf16[128,256]{1,0:T(8,128)(2,1)S(1)} collective-permute-done((bf16[128,256]{1,0:T(8,128)(2,1)S(1)}, bf16[128,256]{1,0:T(8,128)(2,1)S(1)}, u32[]{:S(2)}, u32[]{:S(2)}) %collective-permute-start.7) | collective-permute-done | bytes 65568 | tf_op jit(solution)/shard_map/ppermute | solution.py:42
  32.3 2.7 %collective-permute-start.12 = (bf16[1024,256]{1,0:T(8,128)(2,1)S(1)}, bf16[1024,256]{1,0:T(8,128)(2,1)S(1)}, u32[]{:S(2)}, u32[]{:S(2)}) collective-permute-start(bf16[1024,256]{1,0:T(8,128)(2,1)S(1)} %slice_dynamic-update-slice_fusion.refs_6_.refs_4_), channel_id=1, source_target_pairs={{0,48},{1,49},{2,50},{3,51},{4,52},{5,53},{6,54},{7,55},{8,56},{9,... | collective-permute-start | bytes 1572872 | tf_op jit(solution)/shard_map/ppermute | solution.py:42
  35.0 6.0 %attend.3 = (bf16[2560,128]{1,0:T(8,128)(2,1)S(1)}, bf16[2560,128]{1,0:T(8,128)(2,1)S(1)}, f32[2,2560]{1,0:T(2,128)S(1)}, f32[128,2560]{1,0:T(8,128)S(1)}) custom-call(s32[4,128]{1,0:T(4,128)S(1)} %get-tuple-element.90.refs_0_.tab, s32[1,2560]{1,0:T(1,128)S(1)} %get-tuple-element.91.refs_1_, bf16[128,1280]{1,0:T(8,128)(2,1)S(1)} %pad_maximum_fusion.2.refs_2_, ...), custom_call_target="tpu_custom_call" | custom-call | flops 1677721600 | bytes 4194304 | tf_op jit(solution)/shard_map/attend/pallas_call | solution.py:268
  41.0 2.8 %collective-permute-done.12.refs_4_ = bf16[1024,256]{1,0:T(8,128)(2,1)S(1)} collective-permute-done((bf16[1024,256]{1,0:T(8,128)(2,1)S(1)}, bf16[1024,256]{1,0:T(8,128)(2,1)S(1)}, u32[]{:S(2)}, u32[]{:S(2)}) %collective-permute-start.12) | collective-permute-done | bytes 524320 | tf_op jit(solution)/shard_map/ppermute | solution.py:42
  43.8 3.5 %collective-permute-start.13 = (bf16[512,256]{1,0:T(8,128)(2,1)S(1)}, bf16[512,256]{1,0:T(8,128)(2,1)S(1)}, u32[]{:S(2)}, u32[]{:S(2)}) collective-permute-start(bf16[512,256]{1,0:T(8,128)(2,1)S(1)} %slice.114), channel_id=1, source_target_pairs={{0,48},{1,49},{2,50},{3,51},{4,52},{5,53},{6,54},{7,55},{8,56},{9,... | collective-permute-start | bytes 786440 | tf_op jit(solution)/shard_map/ppermute | solution.py:42
  47.6 8.5 %attend.4 = (f32[2,2560]{1,0:T(2,128)S(1)}, f32[128,2560]{1,0:T(8,128)S(1)}) custom-call(s32[4,128]{1,0:T(4,128)S(1)} %get-tuple-element.101.refs_0_, s32[1,2560]{1,0:T(1,128)S(1)} %get-tuple-element.91.refs_1_, bf16[2560,128]{1,0:T(8,128)(2,1)S(1)} %get-tuple-element.98.refs_2_, bf16[2560,128]{1,0:T(8,128)(2,1)S(1)} %get-tuple-element.99.refs_3_, ...), custom_call_target="tpu_custom_call" | custom-call | flops 3355443200 | bytes 4194304 | tf_op jit(solution)/shard_map/attend/pallas_call | solution.py:268
  56.2 6.8 %attend.5 = (f32[2,2560]{1,0:T(2,128)S(1)}, f32[2,2560]{1,0:T(2,128)}, f32[128,2560]{1,0:T(8,128)S(1)}) custom-call(s32[4,128]{1,0:T(4,128)S(1)} %get-tuple-element.100.refs_0_, s32[1,2560]{1,0:T(1,128)S(1)} %get-tuple-element.91.refs_1_, bf16[2560,128]{1,0:T(8,128)(2,1)S(1)} %get-tuple-element.98.refs_2_, bf16[2560,128]{1,0:T(8,128)(2,1)S(1)} %get-tuple-element.99.refs_3_, ...), custom_call_target="tpu_custom_call" | custom-call | flops 1677721600 | bytes 4194304 | tf_op jit(solution)/shard_map/attend/pallas_call | solution.py:268
  63.3 2.8 %collective-permute-start.15 = (f32[2,2560]{1,0:T(2,128)S(1)}, f32[2,2560]{1,0:T(2,128)S(1)}, u32[]{:S(2)}, u32[]{:S(2)}) collective-permute-start(f32[2,2560]{1,0:T(2,128)S(1)} %get-tuple-element.112.stat_ref.refs_5_), channel_id=1, source_target_pairs={{0,128},{1,129},{2,130},{3,131},{4,132},{5,133},{6,134},{7,135},{8... | collective-permute-start | bytes 61448 | tf_op jit(solution)/shard_map/ppermute | solution.py:42
  68.8 6.9 %grads.4 = (f32[2,2560]{1,0:T(2,128)S(1)}, f32[128,2560]{1,0:T(8,128)S(1)}, bf16[1024,256]{1,0:T(8,128)(2,1)S(1)}) custom-call(s32[4,128]{1,0:T(4,128)S(1)} %get-tuple-element.100.refs_0_, s32[1,2560]{1,0:T(1,128)S(1)} %get-tuple-element.91.refs_1_, bf16[2560,128]{1,0:T(8,128)(2,1)S(1)} %get-tuple-element.98.refs_2_, ...), custom_call_target="tpu_custom_call" | custom-call | flops 4194304000 | bytes 4194304 | tf_op jit(solution)/shard_map/grads/pallas_call | solution.py:362
  75.7 2.8 %collective-permute-start.18 = (bf16[512,256]{1,0:T(8,128)(2,1)S(1)}, bf16[512,256]{1,0:T(8,128)(2,1)S(1)}, u32[]{:S(2)}, u32[]{:S(2)}) collective-permute-start(bf16[512,256]{1,0:T(8,128)(2,1)S(1)} %get-tuple-element.159), channel_id=1, source_target_pairs={{0,48},{1,49},{2,50},{3,51},{4,52},{5,53},{6,54},{7,55},{8,56},{9,... | collective-permute-start | bytes 786440 | tf_op jit(solution)/shard_map/ppermute | solution.py:42
  78.5 6.9 %grads.5 = (f32[128,2560]{1,0:T(8,128)S(1)}, bf16[1024,256]{1,0:T(8,128)(2,1)S(1)}) custom-call(s32[4,128]{1,0:T(4,128)S(1)} %get-tuple-element.118.refs_0_, s32[1,2560]{1,0:T(1,128)S(1)} %get-tuple-element.91.refs_1_, bf16[2560,128]{1,0:T(8,128)(2,1)S(1)} %get-tuple-element.98.refs_2_, bf16[2560,128]{1,0:T(8,128)(2,1)S(1)} %get-tuple-element.99.refs_3_, ...), custom_call_target="tpu_custom_call" | custom-call | flops 4194304000 | bytes 4194304 | tf_op jit(solution)/shard_map/grads/pallas_call | solution.py:362
  85.5 6.8 %grads.6 = (f32[128,2560]{1,0:T(8,128)S(1)}, bf16[1024,256]{1,0:T(8,128)(2,1)S(1)}) custom-call(s32[4,128]{1,0:T(4,128)S(1)} %get-tuple-element.117.refs_0_, s32[1,2560]{1,0:T(1,128)S(1)} %get-tuple-element.91.refs_1_, bf16[2560,128]{1,0:T(8,128)(2,1)S(1)} %get-tuple-element.98.refs_2_, bf16[2560,128]{1,0:T(8,128)(2,1)S(1)} %get-tuple-element.99.refs_3_, ...), custom_call_target="tpu_custom_call" | custom-call | flops 4194304000 | bytes 4194304 | tf_op jit(solution)/shard_map/grads/pallas_call | solution.py:362
  92.6 3.0 %collective-permute-start.20 = (bf16[1024,256]{1,0:T(8,128)(2,1)S(1)}, bf16[1024,256]{1,0:T(8,128)(2,1)S(1)}, u32[]{:S(2)}, u32[]{:S(2)}) collective-permute-start(bf16[1024,256]{1,0:T(8,128)(2,1)S(1)} %pad_maximum_fusion.1), channel_id=1, source_target_pairs={{0,48},{1,49},{2,50},{3,51},{4,52},{5,53},{6,54},{7,55},{8,56},{9,... | collective-permute-start | bytes 1572872 | tf_op jit(solution)/shard_map/ppermute | solution.py:42
  95.6 7.6 %grads.7 = (bf16[128,1408]{1,0:T(8,128)(2,1)S(1)}, bf16[128,1408]{1,0:T(8,128)(2,1)S(1)}, bf16[128,1408]{1,0:T(8,128)(2,1)S(1)}, bf16[128,1408]{1,0:T(8,128)(2,1)S(1)}, bf16[1024,256]{1,0:T(8,128)(2,1)S(1)}) custom-call(s32[4,128]{1,0:T(4,128)S(1)} %get-tuple-element.90.refs_0_.tab, s32[1,2560]{1,0:T(1,128)S(1)} %get-tuple-element.91.refs_1_, ...), custom_call_target="tpu_custom_call" | custom-call | flops 4194304000 | bytes 4194304 | tf_op jit(solution)/shard_map/grads/pallas_call | solution.py:362
  103.6 2.9 %collective-permute-start.24 = (bf16[128,1408]{1,0:T(8,128)(2,1)S(1)}, bf16[128,1408]{1,0:T(8,128)(2,1)S(1)}, u32[]{:S(2)}, u32[]{:S(2)}) collective-permute-start(bf16[128,1408]{1,0:T(8,128)(2,1)S(1)} %get-tuple-element.140), channel_id=1, source_target_pairs={{0,128},{1,129},{2,130},{3,131},{4,132},{5,133},{6,134},{7,135},{8... | collective-permute-start | bytes 1081352 | tf_op jit(solution)/shard_map/ppermute | solution.py:42
  107.3 2.7 %collective-permute-start.22 = (bf16[256,256]{1,0:T(8,128)(2,1)S(1)}, bf16[256,256]{1,0:T(8,128)(2,1)S(1)}, u32[]{:S(2)}, u32[]{:S(2)}) collective-permute-start(bf16[256,256]{1,0:T(8,128)(2,1)S(1)} %pad_maximum_fusion.6), channel_id=1, source_target_pairs={{0,14},{1,15},{2,0},{3,1},{4,2},{5,3},{6,4},{7,5},{8,6},{9,7},{10,... | collective-permute-start | bytes 393224 | tf_op jit(solution)/shard_map/ppermute | solution.py:42
  112.8 2.5 %collective-permute-done.24.refs_2_ = bf16[128,1408]{1,0:T(8,128)(2,1)S(1)} collective-permute-done((bf16[128,1408]{1,0:T(8,128)(2,1)S(1)}, bf16[128,1408]{1,0:T(8,128)(2,1)S(1)}, u32[]{:S(2)}, u32[]{:S(2)}) %collective-permute-start.24) | collective-permute-done | bytes 360480 | tf_op jit(solution)/shard_map/ppermute | solution.py:42
  116.0 3.6 %collective-permute-start.28 = (bf16[128,256]{1,0:T(8,128)(2,1)S(1)}, bf16[128,256]{1,0:T(8,128)(2,1)S(1)}, u32[]{:S(2)}, u32[]{:S(2)}) collective-permute-start(bf16[128,256]{1,0:T(8,128)(2,1)S(1)} %get-tuple-element.153), channel_id=1, source_target_pairs={{0,12},{1,13},{2,14},{3,15},{4,0},{5,1},{6,2},{7,3},{8,4},{9,5},{1... | collective-permute-start | bytes 196616 | tf_op jit(solution)/shard_map/ppermute | solution.py:42
  120.2 8.9 %collective-permute-start.29 = (bf16[64,640]{1,0:T(8,128)(2,1)S(1)}, bf16[64,640]{1,0:T(8,128)(2,1)S(1)}, u32[]{:S(2)}, u32[]{:S(2)}) collective-permute-start(bf16[64,640]{1,0:T(8,128)(2,1)S(1)} %get-tuple-element.150), channel_id=1, source_target_pairs={{0,1},{1,0},{2,3},{3,2},{4,5},{5,4},{6,7},{7,6},{8,9},{9,8},{10,11... | collective-permute-start | bytes 245768 | tf_op jit(solution)/shard_map/ppermute | solution.py:42
  129.3 2.5 %collective-permute-start.31 = (f32[64,256]{1,0:T(8,128)S(1)}, f32[64,256]{1,0:T(8,128)S(1)}, u32[]{:S(2)}, u32[]{:S(2)}) collective-permute-start(f32[64,256]{1,0:T(8,128)S(1)} %get-tuple-element.161), channel_id=1, source_target_pairs={{0,1},{1,0},{2,3},{3,2},{4,5},{5,4},{6,7},{7,6},{8,9},{9,8},{10,11... | collective-permute-start | bytes 196616 | tf_op jit(solution)/shard_map/ppermute | solution.py:42
  (92 shorter events, 27.8 us)
Async XLA Ops:
  8.6 11.0 %collective-permute-start.5 = (bf16[128,1280]{1,0:T(8,128)(2,1)S(1)}, bf16[128,1280]{1,0:T(8,128)(2,1)S(1)}, u32[]{:S(2)}, u32[]{:S(2)}) collective-permute-start(bf16[128,1280]{1,0:T(8,128)(2,1)S(1)} %pad_maximum_fusion.2.refs_2_), channel_id=1, source_target_pairs={{0,64},{1,65},{2,66},{3,67},{4,68},{5,69},{6,70},{7,71},{8,72},{9,... | collective-permute-start | bytes 983048 | tf_op jit(solution)/shard_map/ppermute | solution.py:42
  8.7 10.9 %collective-permute-start.4 = (bf16[128,1280]{1,0:T(8,128)(2,1)S(1)}, bf16[128,1280]{1,0:T(8,128)(2,1)S(1)}, u32[]{:S(2)}, u32[]{:S(2)}) collective-permute-start(bf16[128,1280]{1,0:T(8,128)(2,1)S(1)} %pad_maximum_fusion.2.refs_2_), channel_id=1, source_target_pairs={{0,192},{1,193},{2,194},{3,195},{4,196},{5,197},{6,198},{7,199},{8... | collective-permute-start | bytes 983048 | tf_op jit(solution)/shard_map/ppermute | solution.py:42
  11.4 6.2 %collective-permute-start.3 = (bf16[128,256]{1,0:T(8,128)(2,1)S(1)}, bf16[128,256]{1,0:T(8,128)(2,1)S(1)}, u32[]{:S(2)}, u32[]{:S(2)}) collective-permute-start(bf16[128,256]{1,0:T(8,128)(2,1)S(1)} %pad_maximum_fusion.7), channel_id=1, source_target_pairs={{0,4},{1,5},{2,6},{3,7},{4,8},{5,9},{6,10},{7,11},{8,12},{9,13},{1... | collective-permute-start | bytes 196616 | tf_op jit(solution)/shard_map/ppermute | solution.py:42
  12.6 7.0 %collective-permute-start.2 = (bf16[128,256]{1,0:T(8,128)(2,1)S(1)}, bf16[128,256]{1,0:T(8,128)(2,1)S(1)}, u32[]{:S(2)}, u32[]{:S(2)}) collective-permute-start(bf16[128,256]{1,0:T(8,128)(2,1)S(1)} %pad_maximum_fusion.7), channel_id=1, source_target_pairs={{0,12},{1,13},{2,14},{3,15},{4,0},{5,1},{6,2},{7,3},{8,4},{9,5},{1... | collective-permute-start | bytes 196616 | tf_op jit(solution)/shard_map/ppermute | solution.py:42
  19.6 7.4 %collective-permute-start.6 = (bf16[256,256]{1,0:T(8,128)(2,1)S(1)}, bf16[256,256]{1,0:T(8,128)(2,1)S(1)}, u32[]{:S(2)}, u32[]{:S(2)}) collective-permute-start(bf16[256,256]{1,0:T(8,128)(2,1)S(1)} %get-tuple-element.164), channel_id=1, source_target_pairs={{0,14},{1,15},{2,0},{3,1},{4,2},{5,3},{6,4},{7,5},{8,6},{9,7},{10,... | collective-permute-start | bytes 393224 | tf_op jit(solution)/shard_map/ppermute | solution.py:42
  22.9 9.4 %collective-permute-start.9 = (bf16[128,1280]{1,0:T(8,128)(2,1)S(1)}, bf16[128,1280]{1,0:T(8,128)(2,1)S(1)}, u32[]{:S(2)}, u32[]{:S(2)}) collective-permute-start(bf16[128,1280]{1,0:T(8,128)(2,1)S(1)} %pad_maximum_fusion.2.refs_2_), channel_id=1, source_target_pairs={{0,128},{1,129},{2,130},{3,131},{4,132},{5,133},{6,134},{7,135},{8... | collective-permute-start | bytes 983048 | tf_op jit(solution)/shard_map/ppermute | solution.py:42
  32.3 11.5 %collective-permute-start.12 = (bf16[1024,256]{1,0:T(8,128)(2,1)S(1)}, bf16[1024,256]{1,0:T(8,128)(2,1)S(1)}, u32[]{:S(2)}, u32[]{:S(2)}) collective-permute-start(bf16[1024,256]{1,0:T(8,128)(2,1)S(1)} %slice_dynamic-update-slice_fusion.refs_6_.refs_4_), channel_id=1, source_target_pairs={{0,48},{1,49},{2,50},{3,51},{4,52},{5,53},{6,54},{7,55},{8,56},{9,... | collective-permute-start | bytes 1572872 | tf_op jit(solution)/shard_map/ppermute | solution.py:42
  35.0 12.3 %collective-permute-start.10 = (bf16[1024,256]{1,0:T(8,128)(2,1)S(1)}, bf16[1024,256]{1,0:T(8,128)(2,1)S(1)}, u32[]{:S(2)}, u32[]{:S(2)}) collective-permute-start(bf16[1024,256]{1,0:T(8,128)(2,1)S(1)} %slice_dynamic-update-slice_fusion.refs_6_.refs_4_), channel_id=1, source_target_pairs={{0,16},{1,17},{2,18},{3,19},{4,20},{5,21},{6,22},{7,23},{8,24},{9,... | collective-permute-start | bytes 1572872 | tf_op jit(solution)/shard_map/ppermute | solution.py:42
  43.8 12.3 %collective-permute-start.13 = (bf16[512,256]{1,0:T(8,128)(2,1)S(1)}, bf16[512,256]{1,0:T(8,128)(2,1)S(1)}, u32[]{:S(2)}, u32[]{:S(2)}) collective-permute-start(bf16[512,256]{1,0:T(8,128)(2,1)S(1)} %slice.114), channel_id=1, source_target_pairs={{0,48},{1,49},{2,50},{3,51},{4,52},{5,53},{6,54},{7,55},{8,56},{9,... | collective-permute-start | bytes 786440 | tf_op jit(solution)/shard_map/ppermute | solution.py:42
  47.3 8.7 %collective-permute-start.11 = (bf16[512,256]{1,0:T(8,128)(2,1)S(1)}, bf16[512,256]{1,0:T(8,128)(2,1)S(1)}, u32[]{:S(2)}, u32[]{:S(2)}) collective-permute-start(bf16[512,256]{1,0:T(8,128)(2,1)S(1)} %slice.113), channel_id=1, source_target_pairs={{0,16},{1,17},{2,18},{3,19},{4,20},{5,21},{6,22},{7,23},{8,24},{9,... | collective-permute-start | bytes 786440 | tf_op jit(solution)/shard_map/ppermute | solution.py:42
  63.0 5.8 %collective-permute-start.16 = (f32[2,2560]{1,0:T(2,128)S(1)}, f32[2,2560]{1,0:T(2,128)S(1)}, u32[]{:S(2)}, u32[]{:S(2)}) collective-permute-start(f32[2,2560]{1,0:T(2,128)S(1)} %get-tuple-element.112.stat_ref.refs_5_), channel_id=1, source_target_pairs={{0,64},{1,65},{2,66},{3,67},{4,68},{5,69},{6,70},{7,71},{8,72},{9,... | collective-permute-start | bytes 61448 | tf_op jit(solution)/shard_map/ppermute | solution.py:42
  63.3 5.5 %collective-permute-start.15 = (f32[2,2560]{1,0:T(2,128)S(1)}, f32[2,2560]{1,0:T(2,128)S(1)}, u32[]{:S(2)}, u32[]{:S(2)}) collective-permute-start(f32[2,2560]{1,0:T(2,128)S(1)} %get-tuple-element.112.stat_ref.refs_5_), channel_id=1, source_target_pairs={{0,128},{1,129},{2,130},{3,131},{4,132},{5,133},{6,134},{7,135},{8... | collective-permute-start | bytes 61448 | tf_op jit(solution)/shard_map/ppermute | solution.py:42
  75.7 9.7 %collective-permute-start.18 = (bf16[512,256]{1,0:T(8,128)(2,1)S(1)}, bf16[512,256]{1,0:T(8,128)(2,1)S(1)}, u32[]{:S(2)}, u32[]{:S(2)}) collective-permute-start(bf16[512,256]{1,0:T(8,128)(2,1)S(1)} %get-tuple-element.159), channel_id=1, source_target_pairs={{0,48},{1,49},{2,50},{3,51},{4,52},{5,53},{6,54},{7,55},{8,56},{9,... | collective-permute-start | bytes 786440 | tf_op jit(solution)/shard_map/ppermute | solution.py:42
  78.5 6.9 %collective-permute-start.17 = (bf16[512,256]{1,0:T(8,128)(2,1)S(1)}, bf16[512,256]{1,0:T(8,128)(2,1)S(1)}, u32[]{:S(2)}, u32[]{:S(2)}) collective-permute-start(bf16[512,256]{1,0:T(8,128)(2,1)S(1)} %get-tuple-element.160), channel_id=1, source_target_pairs={{0,16},{1,17},{2,18},{3,19},{4,20},{5,21},{6,22},{7,23},{8,24},{9,... | collective-permute-start | bytes 786440 | tf_op jit(solution)/shard_map/ppermute | solution.py:42
  92.5 10.8 %collective-permute-start.19 = (bf16[1024,256]{1,0:T(8,128)(2,1)S(1)}, bf16[1024,256]{1,0:T(8,128)(2,1)S(1)}, u32[]{:S(2)}, u32[]{:S(2)}) collective-permute-start(bf16[1024,256]{1,0:T(8,128)(2,1)S(1)} %pad_maximum_fusion), channel_id=1, source_target_pairs={{0,16},{1,17},{2,18},{3,19},{4,20},{5,21},{6,22},{7,23},{8,24},{9,... | collective-permute-start | bytes 1572872 | tf_op jit(solution)/shard_map/ppermute | solution.py:42
  92.6 10.6 %collective-permute-start.20 = (bf16[1024,256]{1,0:T(8,128)(2,1)S(1)}, bf16[1024,256]{1,0:T(8,128)(2,1)S(1)}, u32[]{:S(2)}, u32[]{:S(2)}) collective-permute-start(bf16[1024,256]{1,0:T(8,128)(2,1)S(1)} %pad_maximum_fusion.1), channel_id=1, source_target_pairs={{0,48},{1,49},{2,50},{3,51},{4,52},{5,53},{6,54},{7,55},{8,56},{9,... | collective-permute-start | bytes 1572872 | tf_op jit(solution)/shard_map/ppermute | solution.py:42
  103.5 9.3 %collective-permute-start.23 = (bf16[128,1408]{1,0:T(8,128)(2,1)S(1)}, bf16[128,1408]{1,0:T(8,128)(2,1)S(1)}, u32[]{:S(2)}, u32[]{:S(2)}) collective-permute-start(bf16[128,1408]{1,0:T(8,128)(2,1)S(1)} %get-tuple-element.139), channel_id=1, source_target_pairs={{0,64},{1,65},{2,66},{3,67},{4,68},{5,69},{6,70},{7,71},{8,72},{9,... | collective-permute-start | bytes 1081352 | tf_op jit(solution)/shard_map/ppermute | solution.py:42
  103.6 11.7 %collective-permute-start.24 = (bf16[128,1408]{1,0:T(8,128)(2,1)S(1)}, bf16[128,1408]{1,0:T(8,128)(2,1)S(1)}, u32[]{:S(2)}, u32[]{:S(2)}) collective-permute-start(bf16[128,1408]{1,0:T(8,128)(2,1)S(1)} %get-tuple-element.140), channel_id=1, source_target_pairs={{0,128},{1,129},{2,130},{3,131},{4,132},{5,133},{6,134},{7,135},{8... | collective-permute-start | bytes 1081352 | tf_op jit(solution)/shard_map/ppermute | solution.py:42
  106.6 9.3 %collective-permute-start.25 = (bf16[128,1408]{1,0:T(8,128)(2,1)S(1)}, bf16[128,1408]{1,0:T(8,128)(2,1)S(1)}, u32[]{:S(2)}, u32[]{:S(2)}) collective-permute-start(bf16[128,1408]{1,0:T(8,128)(2,1)S(1)} %get-tuple-element.141), channel_id=1, source_target_pairs={{0,192},{1,193},{2,194},{3,195},{4,196},{5,197},{6,198},{7,199},{8... | collective-permute-start | bytes 1081352 | tf_op jit(solution)/shard_map/ppermute | solution.py:42
  107.3 5.5 %collective-permute-start.22 = (bf16[256,256]{1,0:T(8,128)(2,1)S(1)}, bf16[256,256]{1,0:T(8,128)(2,1)S(1)}, u32[]{:S(2)}, u32[]{:S(2)}) collective-permute-start(bf16[256,256]{1,0:T(8,128)(2,1)S(1)} %pad_maximum_fusion.6), channel_id=1, source_target_pairs={{0,14},{1,15},{2,0},{3,1},{4,2},{5,3},{6,4},{7,5},{8,6},{9,7},{10,... | collective-permute-start | bytes 393224 | tf_op jit(solution)/shard_map/ppermute | solution.py:42
  112.3 16.9 %collective-permute-start.26 = (bf16[128,256]{1,0:T(8,128)(2,1)S(1)}, bf16[128,256]{1,0:T(8,128)(2,1)S(1)}, u32[]{:S(2)}, u32[]{:S(2)}) collective-permute-start(bf16[128,256]{1,0:T(8,128)(2,1)S(1)} %get-tuple-element.154), channel_id=1, source_target_pairs={{0,8},{1,9},{2,10},{3,11},{4,12},{5,13},{6,14},{7,15},{8,0},{9,1},... | collective-permute-start | bytes 196616 | tf_op jit(solution)/shard_map/ppermute | solution.py:42
  115.9 13.3 %collective-permute-start.27 = (bf16[128,256]{1,0:T(8,128)(2,1)S(1)}, bf16[128,256]{1,0:T(8,128)(2,1)S(1)}, u32[]{:S(2)}, u32[]{:S(2)}) collective-permute-start(bf16[128,256]{1,0:T(8,128)(2,1)S(1)} %get-tuple-element.152), channel_id=1, source_target_pairs={{0,4},{1,5},{2,6},{3,7},{4,8},{5,9},{6,10},{7,11},{8,12},{9,13},{1... | collective-permute-start | bytes 196616 | tf_op jit(solution)/shard_map/ppermute | solution.py:42
  116.0 13.2 %collective-permute-start.28 = (bf16[128,256]{1,0:T(8,128)(2,1)S(1)}, bf16[128,256]{1,0:T(8,128)(2,1)S(1)}, u32[]{:S(2)}, u32[]{:S(2)}) collective-permute-start(bf16[128,256]{1,0:T(8,128)(2,1)S(1)} %get-tuple-element.153), channel_id=1, source_target_pairs={{0,12},{1,13},{2,14},{3,15},{4,0},{5,1},{6,2},{7,3},{8,4},{9,5},{1... | collective-permute-start | bytes 196616 | tf_op jit(solution)/shard_map/ppermute | solution.py:42
  120.2 11.6 %collective-permute-start.29 = (bf16[64,640]{1,0:T(8,128)(2,1)S(1)}, bf16[64,640]{1,0:T(8,128)(2,1)S(1)}, u32[]{:S(2)}, u32[]{:S(2)}) collective-permute-start(bf16[64,640]{1,0:T(8,128)(2,1)S(1)} %get-tuple-element.150), channel_id=1, source_target_pairs={{0,1},{1,0},{2,3},{3,2},{4,5},{5,4},{6,7},{7,6},{8,9},{9,8},{10,11... | collective-permute-start | bytes 245768 | tf_op jit(solution)/shard_map/ppermute | solution.py:42
  (13 other events, 34.2 us)

commit v4 on v3

--- a/solution.py
+++ b/solution.py
@@ -207,7 +207,7 @@
         acc[:, here] = acc[:, here] * kept + mixed * added
         return ()
 
-    each_tile(cfg, tab, keys // C, 8, (scores, weights, absorb))
+    each_tile(cfg, tab, keys // C, 7, (scores, weights, absorb))
     if not last:
         return
 
@@ -324,7 +324,7 @@
         gqt[:, here] += gq
         return ()
 
-    each_tile(cfg, tab, keys // C, 4, (scores, weights, products, absorb))
+    each_tile(cfg, tab, keys // C, 7, (scores, weights, products, absorb))
     if last:
         def turn(r, _):
             here = pl.ds(aligned(r, 256), 256)

time: 134 us -> 132 us (0.985)
  Pallas kernels: 54.4 us -> 51.2 us
    pallas_call x4, Pallas kernels: 28.2 us -> 26.4 us  [backward(): pl.pallas_call(functools.partial(backward_body, cfg, n, first, last), out...]
    pallas_call x3, Pallas kernels: 21.3 us -> 19.9 us  [forward(): pl.pallas_call(functools.partial(forward_body, cfg, n, first, last), out_...]
  transfers between devices with their start and end apart: 32 -> 32, of which waited for: 10 -> 10; matrix products, arithmetic and copies ran while one was open for 0% -> 0% of each run, Pallas kernels for 25% -> 24%
where the time goes in v4:
time: 132 us
  starting transfers between devices  56.3 us (43%)
  Pallas kernels  51.2 us (39%)
  waiting for transfers between devices  18.2 us (14%)
  local copies, waits for them, and re-layouts  4.25 us (3%)
    ppermute x32, starting transfers between devices, shift(): return lax.ppermute(a, AXES, pairs)  56.3 us
    pallas_call x4, Pallas kernels, backward(): pl.pallas_call(functools.partial(backward_body, cfg, n, first, last), out...  26.4 us
    pallas_call x3, Pallas kernels, forward(): pl.pallas_call(functools.partial(forward_body, cfg, n, first, last), out_...  19.9 us
    ppermute x32, waiting for transfers between devices, shift(): return lax.ppermute(a, AXES, pairs)  18.2 us
    unnamed x18, local copies, waits for them, and re-layouts  4.08 us
  transfers between devices with their start and end apart: 32, of which 10 were waited for; matrix products, arithmetic and copies ran while one was open for 0% of the time, Pallas kernels for 24%

profile of v4, /device:TPU:1, one launch (start us, length us, event | category | flops | bytes accessed | tf_op | source)
XLA Modules:
  0.0 131.6 jit_solution(8796619456946193206)
XLA Ops:
  4.0 3.3 %collective-permute-start.1 = (bf16[64,1280]{1,0:T(8,128)(2,1)S(1)}, bf16[64,1280]{1,0:T(8,128)(2,1)S(1)}, u32[]{:S(2)}, u32[]{:S(2)}) collective-permute-start(bf16[64,1280]{1,0:T(8,128)(2,1)S(1)} %get-tuple-element.81), channel_id=1, source_target_pairs={{0,1},{1,0},{2,3},{3,2},{4,5},{5,4},{6,7},{7,6},{8,9},{9,8},{10,11... | collective-permute-start | bytes 491528 | tf_op jit(solution)/shard_map/ppermute | solution.py:42
  8.7 2.7 %collective-permute-start.4 = (bf16[128,1280]{1,0:T(8,128)(2,1)S(1)}, bf16[128,1280]{1,0:T(8,128)(2,1)S(1)}, u32[]{:S(2)}, u32[]{:S(2)}) collective-permute-start(bf16[128,1280]{1,0:T(8,128)(2,1)S(1)} %pad_maximum_fusion.2.refs_2_), channel_id=1, source_target_pairs={{0,192},{1,193},{2,194},{3,195},{4,196},{5,197},{6,198},{7,199},{8... | collective-permute-start | bytes 983048 | tf_op jit(solution)/shard_map/ppermute | solution.py:42
  12.6 3.0 %collective-permute-start.2 = (bf16[128,256]{1,0:T(8,128)(2,1)S(1)}, bf16[128,256]{1,0:T(8,128)(2,1)S(1)}, u32[]{:S(2)}, u32[]{:S(2)}) collective-permute-start(bf16[128,256]{1,0:T(8,128)(2,1)S(1)} %pad_maximum_fusion.7), channel_id=1, source_target_pairs={{0,12},{1,13},{2,14},{3,15},{4,0},{5,1},{6,2},{7,3},{8,4},{9,5},{1... | collective-permute-start | bytes 196616 | tf_op jit(solution)/shard_map/ppermute | solution.py:42
  19.6 3.3 %collective-permute-start.6 = (bf16[256,256]{1,0:T(8,128)(2,1)S(1)}, bf16[256,256]{1,0:T(8,128)(2,1)S(1)}, u32[]{:S(2)}, u32[]{:S(2)}) collective-permute-start(bf16[256,256]{1,0:T(8,128)(2,1)S(1)} %get-tuple-element.164), channel_id=1, source_target_pairs={{0,14},{1,15},{2,0},{3,1},{4,2},{5,3},{6,4},{7,5},{8,6},{9,7},{10,... | collective-permute-start | bytes 393224 | tf_op jit(solution)/shard_map/ppermute | solution.py:42
  27.0 2.4 %collective-permute-done.7 = bf16[128,256]{1,0:T(8,128)(2,1)S(1)} collective-permute-done((bf16[128,256]{1,0:T(8,128)(2,1)S(1)}, bf16[128,256]{1,0:T(8,128)(2,1)S(1)}, u32[]{:S(2)}, u32[]{:S(2)}) %collective-permute-start.7) | collective-permute-done | bytes 65568 | tf_op jit(solution)/shard_map/ppermute | solution.py:42
  32.3 2.7 %collective-permute-start.12 = (bf16[1024,256]{1,0:T(8,128)(2,1)S(1)}, bf16[1024,256]{1,0:T(8,128)(2,1)S(1)}, u32[]{:S(2)}, u32[]{:S(2)}) collective-permute-start(bf16[1024,256]{1,0:T(8,128)(2,1)S(1)} %slice_dynamic-update-slice_fusion.refs_6_.refs_4_), channel_id=1, source_target_pairs={{0,48},{1,49},{2,50},{3,51},{4,52},{5,53},{6,54},{7,55},{8,56},{9,... | collective-permute-start | bytes 1572872 | tf_op jit(solution)/shard_map/ppermute | solution.py:42
  35.0 5.3 %attend.3 = (bf16[2560,128]{1,0:T(8,128)(2,1)S(1)}, bf16[2560,128]{1,0:T(8,128)(2,1)S(1)}, f32[2,2560]{1,0:T(2,128)S(1)}, f32[128,2560]{1,0:T(8,128)S(1)}) custom-call(s32[4,128]{1,0:T(4,128)S(1)} %get-tuple-element.90.refs_0_.tab, s32[1,2560]{1,0:T(1,128)S(1)} %get-tuple-element.91.refs_1_, bf16[128,1280]{1,0:T(8,128)(2,1)S(1)} %pad_maximum_fusion.2.refs_2_, ...), custom_call_target="tpu_custom_call" | custom-call | flops 1677721600 | bytes 4194304 | tf_op jit(solution)/shard_map/attend/pallas_call | solution.py:268
  40.3 3.5 %collective-permute-done.12.refs_4_ = bf16[1024,256]{1,0:T(8,128)(2,1)S(1)} collective-permute-done((bf16[1024,256]{1,0:T(8,128)(2,1)S(1)}, bf16[1024,256]{1,0:T(8,128)(2,1)S(1)}, u32[]{:S(2)}, u32[]{:S(2)}) %collective-permute-start.12) | collective-permute-done | bytes 524320 | tf_op jit(solution)/shard_map/ppermute | solution.py:42
  43.8 3.5 %collective-permute-start.13 = (bf16[512,256]{1,0:T(8,128)(2,1)S(1)}, bf16[512,256]{1,0:T(8,128)(2,1)S(1)}, u32[]{:S(2)}, u32[]{:S(2)}) collective-permute-start(bf16[512,256]{1,0:T(8,128)(2,1)S(1)} %slice.114), channel_id=1, source_target_pairs={{0,48},{1,49},{2,50},{3,51},{4,52},{5,53},{6,54},{7,55},{8,56},{9,... | collective-permute-start | bytes 786440 | tf_op jit(solution)/shard_map/ppermute | solution.py:42
  47.6 8.4 %attend.4 = (f32[2,2560]{1,0:T(2,128)S(1)}, f32[128,2560]{1,0:T(8,128)S(1)}) custom-call(s32[4,128]{1,0:T(4,128)S(1)} %get-tuple-element.101.refs_0_, s32[1,2560]{1,0:T(1,128)S(1)} %get-tuple-element.91.refs_1_, bf16[2560,128]{1,0:T(8,128)(2,1)S(1)} %get-tuple-element.98.refs_2_, bf16[2560,128]{1,0:T(8,128)(2,1)S(1)} %get-tuple-element.99.refs_3_, ...), custom_call_target="tpu_custom_call" | custom-call | flops 3355443200 | bytes 4194304 | tf_op jit(solution)/shard_map/attend/pallas_call | solution.py:268
  56.1 6.2 %attend.5 = (f32[2,2560]{1,0:T(2,128)S(1)}, f32[2,2560]{1,0:T(2,128)}, f32[128,2560]{1,0:T(8,128)S(1)}) custom-call(s32[4,128]{1,0:T(4,128)S(1)} %get-tuple-element.100.refs_0_, s32[1,2560]{1,0:T(1,128)S(1)} %get-tuple-element.91.refs_1_, bf16[2560,128]{1,0:T(8,128)(2,1)S(1)} %get-tuple-element.98.refs_2_, bf16[2560,128]{1,0:T(8,128)(2,1)S(1)} %get-tuple-element.99.refs_3_, ...), custom_call_target="tpu_custom_call" | custom-call | flops 1677721600 | bytes 4194304 | tf_op jit(solution)/shard_map/attend/pallas_call | solution.py:268
  62.6 2.7 %collective-permute-start.15 = (f32[2,2560]{1,0:T(2,128)S(1)}, f32[2,2560]{1,0:T(2,128)S(1)}, u32[]{:S(2)}, u32[]{:S(2)}) collective-permute-start(f32[2,2560]{1,0:T(2,128)S(1)} %get-tuple-element.112.stat_ref.refs_5_), channel_id=1, source_target_pairs={{0,128},{1,129},{2,130},{3,131},{4,132},{5,133},{6,134},{7,135},{8... | collective-permute-start | bytes 61448 | tf_op jit(solution)/shard_map/ppermute | solution.py:42
  68.1 6.4 %grads.4 = (f32[2,2560]{1,0:T(2,128)S(1)}, f32[128,2560]{1,0:T(8,128)S(1)}, bf16[1024,256]{1,0:T(8,128)(2,1)S(1)}) custom-call(s32[4,128]{1,0:T(4,128)S(1)} %get-tuple-element.100.refs_0_, s32[1,2560]{1,0:T(1,128)S(1)} %get-tuple-element.91.refs_1_, bf16[2560,128]{1,0:T(8,128)(2,1)S(1)} %get-tuple-element.98.refs_2_, ...), custom_call_target="tpu_custom_call" | custom-call | flops 4194304000 | bytes 4194304 | tf_op jit(solution)/shard_map/grads/pallas_call | solution.py:362
  74.6 2.7 %collective-permute-start.18 = (bf16[512,256]{1,0:T(8,128)(2,1)S(1)}, bf16[512,256]{1,0:T(8,128)(2,1)S(1)}, u32[]{:S(2)}, u32[]{:S(2)}) collective-permute-start(bf16[512,256]{1,0:T(8,128)(2,1)S(1)} %get-tuple-element.159), channel_id=1, source_target_pairs={{0,48},{1,49},{2,50},{3,51},{4,52},{5,53},{6,54},{7,55},{8,56},{9,... | collective-permute-start | bytes 786440 | tf_op jit(solution)/shard_map/ppermute | solution.py:42
  77.3 6.4 %grads.5 = (f32[128,2560]{1,0:T(8,128)S(1)}, bf16[1024,256]{1,0:T(8,128)(2,1)S(1)}) custom-call(s32[4,128]{1,0:T(4,128)S(1)} %get-tuple-element.118.refs_0_, s32[1,2560]{1,0:T(1,128)S(1)} %get-tuple-element.91.refs_1_, bf16[2560,128]{1,0:T(8,128)(2,1)S(1)} %get-tuple-element.98.refs_2_, bf16[2560,128]{1,0:T(8,128)(2,1)S(1)} %get-tuple-element.99.refs_3_, ...), custom_call_target="tpu_custom_call" | custom-call | flops 4194304000 | bytes 4194304 | tf_op jit(solution)/shard_map/grads/pallas_call | solution.py:362
  83.9 6.4 %grads.6 = (f32[128,2560]{1,0:T(8,128)S(1)}, bf16[1024,256]{1,0:T(8,128)(2,1)S(1)}) custom-call(s32[4,128]{1,0:T(4,128)S(1)} %get-tuple-element.117.refs_0_, s32[1,2560]{1,0:T(1,128)S(1)} %get-tuple-element.91.refs_1_, bf16[2560,128]{1,0:T(8,128)(2,1)S(1)} %get-tuple-element.98.refs_2_, bf16[2560,128]{1,0:T(8,128)(2,1)S(1)} %get-tuple-element.99.refs_3_, ...), custom_call_target="tpu_custom_call" | custom-call | flops 4194304000 | bytes 4194304 | tf_op jit(solution)/shard_map/grads/pallas_call | solution.py:362
  90.8 2.8 %collective-permute-start.20 = (bf16[1024,256]{1,0:T(8,128)(2,1)S(1)}, bf16[1024,256]{1,0:T(8,128)(2,1)S(1)}, u32[]{:S(2)}, u32[]{:S(2)}) collective-permute-start(bf16[1024,256]{1,0:T(8,128)(2,1)S(1)} %pad_maximum_fusion.1), channel_id=1, source_target_pairs={{0,48},{1,49},{2,50},{3,51},{4,52},{5,53},{6,54},{7,55},{8,56},{9,... | collective-permute-start | bytes 1572872 | tf_op jit(solution)/shard_map/ppermute | solution.py:42
  93.5 7.2 %grads.7 = (bf16[128,1408]{1,0:T(8,128)(2,1)S(1)}, bf16[128,1408]{1,0:T(8,128)(2,1)S(1)}, bf16[128,1408]{1,0:T(8,128)(2,1)S(1)}, bf16[128,1408]{1,0:T(8,128)(2,1)S(1)}, bf16[1024,256]{1,0:T(8,128)(2,1)S(1)}) custom-call(s32[4,128]{1,0:T(4,128)S(1)} %get-tuple-element.90.refs_0_.tab, s32[1,2560]{1,0:T(1,128)S(1)} %get-tuple-element.91.refs_1_, ...), custom_call_target="tpu_custom_call" | custom-call | flops 4194304000 | bytes 4194304 | tf_op jit(solution)/shard_map/grads/pallas_call | solution.py:362
  104.8 2.7 %collective-permute-start.22 = (bf16[256,256]{1,0:T(8,128)(2,1)S(1)}, bf16[256,256]{1,0:T(8,128)(2,1)S(1)}, u32[]{:S(2)}, u32[]{:S(2)}) collective-permute-start(bf16[256,256]{1,0:T(8,128)(2,1)S(1)} %pad_maximum_fusion.6), channel_id=1, source_target_pairs={{0,14},{1,15},{2,0},{3,1},{4,2},{5,3},{6,4},{7,5},{8,6},{9,7},{10,... | collective-permute-start | bytes 393224 | tf_op jit(solution)/shard_map/ppermute | solution.py:42
  107.5 2.3 %collective-permute-done.21 = bf16[256,256]{1,0:T(8,128)(2,1)S(1)} collective-permute-done((bf16[256,256]{1,0:T(8,128)(2,1)S(1)}, bf16[256,256]{1,0:T(8,128)(2,1)S(1)}, u32[]{:S(2)}, u32[]{:S(2)}) %collective-permute-start.21) | collective-permute-done | bytes 131104 | tf_op jit(solution)/shard_map/ppermute | solution.py:42
  110.2 2.5 %collective-permute-done.24.refs_2_ = bf16[128,1408]{1,0:T(8,128)(2,1)S(1)} collective-permute-done((bf16[128,1408]{1,0:T(8,128)(2,1)S(1)}, bf16[128,1408]{1,0:T(8,128)(2,1)S(1)}, u32[]{:S(2)}, u32[]{:S(2)}) %collective-permute-start.24) | collective-permute-done | bytes 360480 | tf_op jit(solution)/shard_map/ppermute | solution.py:42
  113.5 3.6 %collective-permute-start.28 = (bf16[128,256]{1,0:T(8,128)(2,1)S(1)}, bf16[128,256]{1,0:T(8,128)(2,1)S(1)}, u32[]{:S(2)}, u32[]{:S(2)}) collective-permute-start(bf16[128,256]{1,0:T(8,128)(2,1)S(1)} %get-tuple-element.153), channel_id=1, source_target_pairs={{0,12},{1,13},{2,14},{3,15},{4,0},{5,1},{6,2},{7,3},{8,4},{9,5},{1... | collective-permute-start | bytes 196616 | tf_op jit(solution)/shard_map/ppermute | solution.py:42
  117.7 9.4 %collective-permute-start.29 = (bf16[64,640]{1,0:T(8,128)(2,1)S(1)}, bf16[64,640]{1,0:T(8,128)(2,1)S(1)}, u32[]{:S(2)}, u32[]{:S(2)}) collective-permute-start(bf16[64,640]{1,0:T(8,128)(2,1)S(1)} %get-tuple-element.150), channel_id=1, source_target_pairs={{0,1},{1,0},{2,3},{3,2},{4,5},{5,4},{6,7},{7,6},{8,9},{9,8},{10,11... | collective-permute-start | bytes 245768 | tf_op jit(solution)/shard_map/ppermute | solution.py:42
  127.2 2.6 %collective-permute-start.31 = (f32[64,256]{1,0:T(8,128)S(1)}, f32[64,256]{1,0:T(8,128)S(1)}, u32[]{:S(2)}, u32[]{:S(2)}) collective-permute-start(f32[64,256]{1,0:T(8,128)S(1)} %get-tuple-element.161), channel_id=1, source_target_pairs={{0,1},{1,0},{2,3},{3,2},{4,5},{5,4},{6,7},{7,6},{8,9},{9,8},{10,11... | collective-permute-start | bytes 196616 | tf_op jit(solution)/shard_map/ppermute | solution.py:42
  (92 shorter events, 28.7 us)
Async XLA Ops:
  8.6 11.0 %collective-permute-start.5 = (bf16[128,1280]{1,0:T(8,128)(2,1)S(1)}, bf16[128,1280]{1,0:T(8,128)(2,1)S(1)}, u32[]{:S(2)}, u32[]{:S(2)}) collective-permute-start(bf16[128,1280]{1,0:T(8,128)(2,1)S(1)} %pad_maximum_fusion.2.refs_2_), channel_id=1, source_target_pairs={{0,64},{1,65},{2,66},{3,67},{4,68},{5,69},{6,70},{7,71},{8,72},{9,... | collective-permute-start | bytes 983048 | tf_op jit(solution)/shard_map/ppermute | solution.py:42
  8.7 10.9 %collective-permute-start.4 = (bf16[128,1280]{1,0:T(8,128)(2,1)S(1)}, bf16[128,1280]{1,0:T(8,128)(2,1)S(1)}, u32[]{:S(2)}, u32[]{:S(2)}) collective-permute-start(bf16[128,1280]{1,0:T(8,128)(2,1)S(1)} %pad_maximum_fusion.2.refs_2_), channel_id=1, source_target_pairs={{0,192},{1,193},{2,194},{3,195},{4,196},{5,197},{6,198},{7,199},{8... | collective-permute-start | bytes 983048 | tf_op jit(solution)/shard_map/ppermute | solution.py:42
  11.4 6.2 %collective-permute-start.3 = (bf16[128,256]{1,0:T(8,128)(2,1)S(1)}, bf16[128,256]{1,0:T(8,128)(2,1)S(1)}, u32[]{:S(2)}, u32[]{:S(2)}) collective-permute-start(bf16[128,256]{1,0:T(8,128)(2,1)S(1)} %pad_maximum_fusion.7), channel_id=1, source_target_pairs={{0,4},{1,5},{2,6},{3,7},{4,8},{5,9},{6,10},{7,11},{8,12},{9,13},{1... | collective-permute-start | bytes 196616 | tf_op jit(solution)/shard_map/ppermute | solution.py:42
  12.6 7.0 %collective-permute-start.2 = (bf16[128,256]{1,0:T(8,128)(2,1)S(1)}, bf16[128,256]{1,0:T(8,128)(2,1)S(1)}, u32[]{:S(2)}, u32[]{:S(2)}) collective-permute-start(bf16[128,256]{1,0:T(8,128)(2,1)S(1)} %pad_maximum_fusion.7), channel_id=1, source_target_pairs={{0,12},{1,13},{2,14},{3,15},{4,0},{5,1},{6,2},{7,3},{8,4},{9,5},{1... | collective-permute-start | bytes 196616 | tf_op jit(solution)/shard_map/ppermute | solution.py:42
  19.6 7.4 %collective-permute-start.6 = (bf16[256,256]{1,0:T(8,128)(2,1)S(1)}, bf16[256,256]{1,0:T(8,128)(2,1)S(1)}, u32[]{:S(2)}, u32[]{:S(2)}) collective-permute-start(bf16[256,256]{1,0:T(8,128)(2,1)S(1)} %get-tuple-element.164), channel_id=1, source_target_pairs={{0,14},{1,15},{2,0},{3,1},{4,2},{5,3},{6,4},{7,5},{8,6},{9,7},{10,... | collective-permute-start | bytes 393224 | tf_op jit(solution)/shard_map/ppermute | solution.py:42
  22.9 9.4 %collective-permute-start.9 = (bf16[128,1280]{1,0:T(8,128)(2,1)S(1)}, bf16[128,1280]{1,0:T(8,128)(2,1)S(1)}, u32[]{:S(2)}, u32[]{:S(2)}) collective-permute-start(bf16[128,1280]{1,0:T(8,128)(2,1)S(1)} %pad_maximum_fusion.2.refs_2_), channel_id=1, source_target_pairs={{0,128},{1,129},{2,130},{3,131},{4,132},{5,133},{6,134},{7,135},{8... | collective-permute-start | bytes 983048 | tf_op jit(solution)/shard_map/ppermute | solution.py:42
  32.3 11.5 %collective-permute-start.12 = (bf16[1024,256]{1,0:T(8,128)(2,1)S(1)}, bf16[1024,256]{1,0:T(8,128)(2,1)S(1)}, u32[]{:S(2)}, u32[]{:S(2)}) collective-permute-start(bf16[1024,256]{1,0:T(8,128)(2,1)S(1)} %slice_dynamic-update-slice_fusion.refs_6_.refs_4_), channel_id=1, source_target_pairs={{0,48},{1,49},{2,50},{3,51},{4,52},{5,53},{6,54},{7,55},{8,56},{9,... | collective-permute-start | bytes 1572872 | tf_op jit(solution)/shard_map/ppermute | solution.py:42
  35.0 12.3 %collective-permute-start.10 = (bf16[1024,256]{1,0:T(8,128)(2,1)S(1)}, bf16[1024,256]{1,0:T(8,128)(2,1)S(1)}, u32[]{:S(2)}, u32[]{:S(2)}) collective-permute-start(bf16[1024,256]{1,0:T(8,128)(2,1)S(1)} %slice_dynamic-update-slice_fusion.refs_6_.refs_4_), channel_id=1, source_target_pairs={{0,16},{1,17},{2,18},{3,19},{4,20},{5,21},{6,22},{7,23},{8,24},{9,... | collective-permute-start | bytes 1572872 | tf_op jit(solution)/shard_map/ppermute | solution.py:42
  43.8 12.3 %collective-permute-start.13 = (bf16[512,256]{1,0:T(8,128)(2,1)S(1)}, bf16[512,256]{1,0:T(8,128)(2,1)S(1)}, u32[]{:S(2)}, u32[]{:S(2)}) collective-permute-start(bf16[512,256]{1,0:T(8,128)(2,1)S(1)} %slice.114), channel_id=1, source_target_pairs={{0,48},{1,49},{2,50},{3,51},{4,52},{5,53},{6,54},{7,55},{8,56},{9,... | collective-permute-start | bytes 786440 | tf_op jit(solution)/shard_map/ppermute | solution.py:42
  47.3 8.7 %collective-permute-start.11 = (bf16[512,256]{1,0:T(8,128)(2,1)S(1)}, bf16[512,256]{1,0:T(8,128)(2,1)S(1)}, u32[]{:S(2)}, u32[]{:S(2)}) collective-permute-start(bf16[512,256]{1,0:T(8,128)(2,1)S(1)} %slice.113), channel_id=1, source_target_pairs={{0,16},{1,17},{2,18},{3,19},{4,20},{5,21},{6,22},{7,23},{8,24},{9,... | collective-permute-start | bytes 786440 | tf_op jit(solution)/shard_map/ppermute | solution.py:42
  62.3 5.8 %collective-permute-start.16 = (f32[2,2560]{1,0:T(2,128)S(1)}, f32[2,2560]{1,0:T(2,128)S(1)}, u32[]{:S(2)}, u32[]{:S(2)}) collective-permute-start(f32[2,2560]{1,0:T(2,128)S(1)} %get-tuple-element.112.stat_ref.refs_5_), channel_id=1, source_target_pairs={{0,64},{1,65},{2,66},{3,67},{4,68},{5,69},{6,70},{7,71},{8,72},{9,... | collective-permute-start | bytes 61448 | tf_op jit(solution)/shard_map/ppermute | solution.py:42
  62.6 5.4 %collective-permute-start.15 = (f32[2,2560]{1,0:T(2,128)S(1)}, f32[2,2560]{1,0:T(2,128)S(1)}, u32[]{:S(2)}, u32[]{:S(2)}) collective-permute-start(f32[2,2560]{1,0:T(2,128)S(1)} %get-tuple-element.112.stat_ref.refs_5_), channel_id=1, source_target_pairs={{0,128},{1,129},{2,130},{3,131},{4,132},{5,133},{6,134},{7,135},{8... | collective-permute-start | bytes 61448 | tf_op jit(solution)/shard_map/ppermute | solution.py:42
  74.6 9.2 %collective-permute-start.18 = (bf16[512,256]{1,0:T(8,128)(2,1)S(1)}, bf16[512,256]{1,0:T(8,128)(2,1)S(1)}, u32[]{:S(2)}, u32[]{:S(2)}) collective-permute-start(bf16[512,256]{1,0:T(8,128)(2,1)S(1)} %get-tuple-element.159), channel_id=1, source_target_pairs={{0,48},{1,49},{2,50},{3,51},{4,52},{5,53},{6,54},{7,55},{8,56},{9,... | collective-permute-start | bytes 786440 | tf_op jit(solution)/shard_map/ppermute | solution.py:42
  77.3 6.5 %collective-permute-start.17 = (bf16[512,256]{1,0:T(8,128)(2,1)S(1)}, bf16[512,256]{1,0:T(8,128)(2,1)S(1)}, u32[]{:S(2)}, u32[]{:S(2)}) collective-permute-start(bf16[512,256]{1,0:T(8,128)(2,1)S(1)} %get-tuple-element.160), channel_id=1, source_target_pairs={{0,16},{1,17},{2,18},{3,19},{4,20},{5,21},{6,22},{7,23},{8,24},{9,... | collective-permute-start | bytes 786440 | tf_op jit(solution)/shard_map/ppermute | solution.py:42
  90.4 10.3 %collective-permute-start.19 = (bf16[1024,256]{1,0:T(8,128)(2,1)S(1)}, bf16[1024,256]{1,0:T(8,128)(2,1)S(1)}, u32[]{:S(2)}, u32[]{:S(2)}) collective-permute-start(bf16[1024,256]{1,0:T(8,128)(2,1)S(1)} %pad_maximum_fusion), channel_id=1, source_target_pairs={{0,16},{1,17},{2,18},{3,19},{4,20},{5,21},{6,22},{7,23},{8,24},{9,... | collective-permute-start | bytes 1572872 | tf_op jit(solution)/shard_map/ppermute | solution.py:42
  90.8 10.0 %collective-permute-start.20 = (bf16[1024,256]{1,0:T(8,128)(2,1)S(1)}, bf16[1024,256]{1,0:T(8,128)(2,1)S(1)}, u32[]{:S(2)}, u32[]{:S(2)}) collective-permute-start(bf16[1024,256]{1,0:T(8,128)(2,1)S(1)} %pad_maximum_fusion.1), channel_id=1, source_target_pairs={{0,48},{1,49},{2,50},{3,51},{4,52},{5,53},{6,54},{7,55},{8,56},{9,... | collective-permute-start | bytes 1572872 | tf_op jit(solution)/shard_map/ppermute | solution.py:42
  101.0 9.2 %collective-permute-start.23 = (bf16[128,1408]{1,0:T(8,128)(2,1)S(1)}, bf16[128,1408]{1,0:T(8,128)(2,1)S(1)}, u32[]{:S(2)}, u32[]{:S(2)}) collective-permute-start(bf16[128,1408]{1,0:T(8,128)(2,1)S(1)} %get-tuple-element.139), channel_id=1, source_target_pairs={{0,64},{1,65},{2,66},{3,67},{4,68},{5,69},{6,70},{7,71},{8,72},{9,... | collective-permute-start | bytes 1081352 | tf_op jit(solution)/shard_map/ppermute | solution.py:42
  101.9 10.8 %collective-permute-start.24 = (bf16[128,1408]{1,0:T(8,128)(2,1)S(1)}, bf16[128,1408]{1,0:T(8,128)(2,1)S(1)}, u32[]{:S(2)}, u32[]{:S(2)}) collective-permute-start(bf16[128,1408]{1,0:T(8,128)(2,1)S(1)} %get-tuple-element.140), channel_id=1, source_target_pairs={{0,128},{1,129},{2,130},{3,131},{4,132},{5,133},{6,134},{7,135},{8... | collective-permute-start | bytes 1081352 | tf_op jit(solution)/shard_map/ppermute | solution.py:42
  104.0 9.3 %collective-permute-start.25 = (bf16[128,1408]{1,0:T(8,128)(2,1)S(1)}, bf16[128,1408]{1,0:T(8,128)(2,1)S(1)}, u32[]{:S(2)}, u32[]{:S(2)}) collective-permute-start(bf16[128,1408]{1,0:T(8,128)(2,1)S(1)} %get-tuple-element.141), channel_id=1, source_target_pairs={{0,192},{1,193},{2,194},{3,195},{4,196},{5,197},{6,198},{7,199},{8... | collective-permute-start | bytes 1081352 | tf_op jit(solution)/shard_map/ppermute | solution.py:42
  104.8 5.4 %collective-permute-start.22 = (bf16[256,256]{1,0:T(8,128)(2,1)S(1)}, bf16[256,256]{1,0:T(8,128)(2,1)S(1)}, u32[]{:S(2)}, u32[]{:S(2)}) collective-permute-start(bf16[256,256]{1,0:T(8,128)(2,1)S(1)} %pad_maximum_fusion.6), channel_id=1, source_target_pairs={{0,14},{1,15},{2,0},{3,1},{4,2},{5,3},{6,4},{7,5},{8,6},{9,7},{10,... | collective-permute-start | bytes 393224 | tf_op jit(solution)/shard_map/ppermute | solution.py:42
  109.8 17.4 %collective-permute-start.26 = (bf16[128,256]{1,0:T(8,128)(2,1)S(1)}, bf16[128,256]{1,0:T(8,128)(2,1)S(1)}, u32[]{:S(2)}, u32[]{:S(2)}) collective-permute-start(bf16[128,256]{1,0:T(8,128)(2,1)S(1)} %get-tuple-element.154), channel_id=1, source_target_pairs={{0,8},{1,9},{2,10},{3,11},{4,12},{5,13},{6,14},{7,15},{8,0},{9,1},... | collective-permute-start | bytes 196616 | tf_op jit(solution)/shard_map/ppermute | solution.py:42
  113.4 13.8 %collective-permute-start.27 = (bf16[128,256]{1,0:T(8,128)(2,1)S(1)}, bf16[128,256]{1,0:T(8,128)(2,1)S(1)}, u32[]{:S(2)}, u32[]{:S(2)}) collective-permute-start(bf16[128,256]{1,0:T(8,128)(2,1)S(1)} %get-tuple-element.152), channel_id=1, source_target_pairs={{0,4},{1,5},{2,6},{3,7},{4,8},{5,9},{6,10},{7,11},{8,12},{9,13},{1... | collective-permute-start | bytes 196616 | tf_op jit(solution)/shard_map/ppermute | solution.py:42
  113.5 13.7 %collective-permute-start.28 = (bf16[128,256]{1,0:T(8,128)(2,1)S(1)}, bf16[128,256]{1,0:T(8,128)(2,1)S(1)}, u32[]{:S(2)}, u32[]{:S(2)}) collective-permute-start(bf16[128,256]{1,0:T(8,128)(2,1)S(1)} %get-tuple-element.153), channel_id=1, source_target_pairs={{0,12},{1,13},{2,14},{3,15},{4,0},{5,1},{6,2},{7,3},{8,4},{9,5},{1... | collective-permute-start | bytes 196616 | tf_op jit(solution)/shard_map/ppermute | solution.py:42
  117.7 12.1 %collective-permute-start.29 = (bf16[64,640]{1,0:T(8,128)(2,1)S(1)}, bf16[64,640]{1,0:T(8,128)(2,1)S(1)}, u32[]{:S(2)}, u32[]{:S(2)}) collective-permute-start(bf16[64,640]{1,0:T(8,128)(2,1)S(1)} %get-tuple-element.150), channel_id=1, source_target_pairs={{0,1},{1,0},{2,3},{3,2},{4,5},{5,4},{6,7},{7,6},{8,9},{9,8},{10,11... | collective-permute-start | bytes 245768 | tf_op jit(solution)/shard_map/ppermute | solution.py:42
  (13 other events, 34.4 us)
